TPU v7x, 32 devices: a whole 2x2x4 slice. The times are simulated.
32 devices in a mesh: br: 2 (over x), seq: 8 (over z, y), ch: 2 (over core).
Axes of the slice: x: 2, y: 2, z: 4, core: 2. Of those that a mesh axis runs over, the one named last changes fastest.
Arguments:
- inputs: float32 [8192, 2048], P('seq'), may hold values from -6 to 6
- lengths: int32 [6], replicated, may hold values from 1 to 7168, as said below
- norm_gain1: bfloat16 [2048], P('seq'), may hold values from 0.5 to 1.5
- in_weight: bfloat16 [2, 2048, 2560], P('br', 'seq', 'ch'), may hold values from -0.125 to 0.125
- conv_weight: bfloat16 [4, 2, 2, 640], P(None, 'ch', 'br', 'seq'), may hold values from -3 to 3
- conv_bias: bfloat16 [2, 2, 640], P('ch', 'br', 'seq'), may hold values from -3 to 3
- gate_weight: bfloat16 [2, 2, 2, 4, 160, 160], P(None, 'ch', 'br', None, 'seq'), may hold values from -0.5 to 0.5
- gate_bias: bfloat16 [2, 2, 2, 640], P(None, 'ch', 'br', 'seq'), may hold values from -4 to 4
- decay_param: bfloat16 [2, 2, 640], P('ch', 'br', 'seq'), may hold values from 3 to 11
- out_weight: bfloat16 [2, 2, 640, 2048], P('ch', 'br', None, 'seq'), may hold values from -0.25 to 0.25
- norm_gain2: bfloat16 [2048], P('seq'), may hold values from 0.5 to 1.5
- mlp_in: bfloat16 [2, 2048, 6144], P(None, 'seq', ('br', 'ch')), may hold values from -0.125 to 0.125
- mlp_down: bfloat16 [6144, 2048], P(('br', 'ch'), 'seq'), may hold values from -0.15625 to 0.15625
- cotangent: float32 [8192, 2048], P('seq'), may hold values from -6 to 6
Outputs:
- output: float32 [8192, 2048], P('seq', ('br', 'ch'))
- inputs_grad: float32 [8192, 2048], P('seq')
- norm_gain1_grad: float32 [2048], P('seq')
- in_weight_grad: float32 [2, 2048, 2560], P('br', 'seq', 'ch')
- conv_weight_grad: float32 [4, 2, 2, 640], P(None, 'ch', 'br', 'seq')
- conv_bias_grad: float32 [2, 2, 640], P('ch', 'br', 'seq')
- gate_weight_grad: float32 [2, 2, 2, 4, 160, 160], P(None, 'ch', 'br', None, 'seq')
- gate_bias_grad: float32 [2, 2, 2, 640], P(None, 'ch', 'br', 'seq')
- decay_param_grad: float32 [2, 2, 640], P('ch', 'br', 'seq')
- out_weight_grad: float32 [2, 2, 640, 2048], P('ch', 'br', None, 'seq')
- norm_gain2_grad: float32 [2048], P('seq')
- mlp_in_grad: float32 [2, 2048, 6144], P(None, 'seq', ('br', 'ch'))
- mlp_down_grad: float32 [6144, 2048], P(('br', 'ch'), 'seq')
- decay_mean: float32 [2, 2, 640], P('ch', 'br', 'seq')
Inputs may be any that keep to these rules, and one draw needn't show every extreme that they name: 6 positive lengths summing to 8192; one of them, neither the first nor the last, equals 7168.
All inputs are finite; a program needn't handle non-finite values.
Results may differ from a plain program's by a relative error of at most 0.011.
Values may be sent and summed in bfloat16 or wider, within the bound.
No kernel may reach another device: no remote copies, remote signals or barrier semaphores. Data moves between devices by JAX's collectives and lax.ppermute only.
A program may use at most 320 MiB of HBM per device.

v0:
```python
import jax
import jax.numpy as jnp
from jax import lax
from jax.sharding import PartitionSpec as P

NORM_EPS = 1e-06
DECAY_SCALE = 8.0


def from_behind(x, axis, by):
    devices = lax.axis_size(axis)
    pairs = [(i, i + by) for i in range(devices) if 0 <= i + by < devices]
    return lax.ppermute(x, axis, pairs)


def entering_2(x, axis, combine, identity, reverse):
    devices, position = (lax.axis_size(axis), lax.axis_index(axis))
    everything = jax.tree.map(lambda part: lax.all_gather(part, axis), x)
    start = jax.tree.map(
        lambda part, zero: jnp.broadcast_to(jnp.asarray(zero, part.dtype), part.shape), x, identity
    )

    def turn(k, before):
        at = devices - 1 - k if reverse else k
        reached = at > position if reverse else at < position
        new = combine(before, jax.tree.map(lambda part: part[at], everything))
        return jax.tree.map(lambda a, b: jnp.where(reached, a, b), new, before)

    return lax.fori_loop(0, devices, turn, start)


def linear_combine(earlier, later):
    return (earlier[0] * later[0], later[0] * earlier[1] + later[1])


def gated_input(gate_pre, unit_val, decay_rate, at_reset):
    rec_gate = jax.nn.sigmoid(gate_pre[0])
    in_gate = jax.nn.sigmoid(gate_pre[1])
    log_decay = -DECAY_SCALE * rec_gate * jax.nn.softplus(-decay_rate)
    keep_val = jnp.where(at_reset, jnp.float32(0.0), jnp.exp(log_decay))
    norm_scale = jnp.where(at_reset, jnp.float32(1.0), jnp.sqrt(-jnp.expm1(2.0 * log_decay)))
    return (keep_val, norm_scale * in_gate * unit_val)


def mlp_act(pair_in):
    return jax.nn.gelu(pair_in[0]) * pair_in[1]


def per_device(
    inputs,
    lengths,
    norm_gain1,
    in_weight,
    conv_weight,
    conv_bias,
    gate_weight,
    gate_bias,
    decay_param,
    out_weight,
    norm_gain2,
    mlp_in,
    mlp_down,
    cotangent,
):
    row_count = inputs.shape[0]
    model_width = inputs.shape[1]
    seq_count = lax.axis_size("seq")
    seq_index = lax.axis_index("seq")
    gathered = (
        lax.all_gather(norm_gain1, "seq", axis=0, tiled=True),
        lax.all_gather(in_weight, "seq", axis=1, tiled=True),
        lax.all_gather(conv_weight, "seq", axis=3, tiled=True),
        lax.all_gather(conv_bias, "seq", axis=2, tiled=True),
        lax.all_gather(gate_weight, "seq", axis=4, tiled=True),
        lax.all_gather(gate_bias, "seq", axis=3, tiled=True),
        lax.all_gather(decay_param, "seq", axis=2, tiled=True),
        lax.all_gather(out_weight, "seq", axis=3, tiled=True),
        lax.all_gather(norm_gain2, "seq", axis=0, tiled=True),
        lax.all_gather(mlp_in, "seq", axis=1, tiled=True),
        lax.all_gather(mlp_down, "seq", axis=1, tiled=True),
    )
    gain_one = gathered[0].astype(jnp.float32)
    w_in = gathered[1][0]
    conv_w = gathered[2][:, 0, 0].astype(jnp.float32)
    conv_b = gathered[3][0, 0].astype(jnp.float32)
    gate_w = gathered[4][:, 0, 0]
    gate_b = gathered[5][:, 0, 0].astype(jnp.float32)
    decay_rate = gathered[6][0, 0].astype(jnp.float32)
    w_out = gathered[7][0, 0]
    gain_two = gathered[8].astype(jnp.float32)
    w_mlp = gathered[9]
    w_down = gathered[10]
    channels = decay_rate.shape[0]
    head_count = gate_w.shape[1]
    block_size = gate_w.shape[2]
    conv_span = conv_w.shape[0] - 1
    group_size = lax.axis_size(("br", "ch"))
    col_count = model_width // group_size
    col_start = lax.axis_index(("br", "ch")) * col_count
    doc_starts = jnp.cumsum(lengths) - lengths
    positions = (
        jnp.arange(row_count + conv_span, dtype=jnp.int32) + seq_index * row_count - conv_span
    )
    doc_ext = jnp.sum((positions[:, None] >= doc_starts[None, 1:]).astype(jnp.int32), axis=1)
    doc_own = doc_ext[conv_span:]
    at_reset = jnp.any(positions[conv_span:, None] == doc_starts[None, :], axis=1)[:, None]
    rstd_one = lax.rsqrt(jnp.mean(inputs * inputs, axis=1, keepdims=True) + NORM_EPS)
    normed_one = inputs * rstd_one
    h_one = (normed_one * gain_one).astype(jnp.bfloat16)
    z_own = jnp.dot(h_one, w_in, preferred_element_type=jnp.float32).astype(jnp.bfloat16)
    pair_out = lax.all_to_all(z_own[None], "br", split_axis=2, concat_axis=0, tiled=True)
    z_gate = pair_out[0].astype(jnp.float32)
    z_rec = pair_out[1]
    rim_rows = from_behind(z_rec[row_count - conv_span :], "seq", 1)
    ext_rows = jnp.concatenate([rim_rows, z_rec], axis=0).astype(jnp.float32)
    conv_sum = jnp.broadcast_to(conv_b, (row_count, channels))
    lag_masks = []
    for lag_index in range(conv_span + 1):
        lo_row = conv_span - lag_index
        lag_valid = (doc_ext[lo_row : lo_row + row_count] == doc_own).astype(jnp.float32)[:, None]
        lag_masks.append(lag_valid)
        conv_sum = conv_sum + conv_w[lag_index] * ext_rows[lo_row : lo_row + row_count] * lag_valid
    unit_low = conv_sum.astype(jnp.bfloat16)
    unit_val = unit_low.astype(jnp.float32)
    unit_blocks = unit_low.reshape(row_count, head_count, block_size)
    gate_pre = (
        jnp.einsum(
            "thi,ghij->gthj", unit_blocks, gate_w, preferred_element_type=jnp.float32
        ).reshape(2, row_count, channels)
        + gate_b[:, None, :]
    )
    carry_keep, drive_term = gated_input(gate_pre, unit_val, decay_rate, at_reset)
    decay_sum = jnp.sum(
        jnp.exp(-DECAY_SCALE * jax.nn.sigmoid(gate_pre[0]) * jax.nn.softplus(-decay_rate)), axis=0
    )
    keep_prod, local_state = lax.associative_scan(linear_combine, (carry_keep, drive_term), axis=0)
    ones_vec = jnp.ones((channels,), jnp.float32)
    zeros_vec = jnp.zeros((channels,), jnp.float32)
    entering = entering_2(
        (keep_prod[-1], local_state[-1]), "seq", linear_combine, (ones_vec, zeros_vec), False
    )[1]
    state_val = local_state + keep_prod * entering
    gate_act = jax.nn.gelu(z_gate)
    mixed_low = (gate_act * state_val).astype(jnp.bfloat16)
    attn_part = jnp.dot(mixed_low, w_out, preferred_element_type=jnp.float32)
    resid_one = inputs + lax.psum(attn_part, ("br", "ch"))
    rstd_two = lax.rsqrt(jnp.mean(resid_one * resid_one, axis=1, keepdims=True) + NORM_EPS)
    normed_two = resid_one * rstd_two
    h_two = (normed_two * gain_two).astype(jnp.bfloat16)
    resid_share = lax.dynamic_slice_in_dim(resid_one, col_start, col_count, 1)
    gate_up = jnp.einsum("td,gdf->gtf", h_two, w_mlp, preferred_element_type=jnp.float32)
    hidden_val, act_back = jax.vjp(mlp_act, gate_up)
    hidden_low = hidden_val.astype(jnp.bfloat16)
    mlp_part = jnp.dot(hidden_low, w_down, preferred_element_type=jnp.float32)
    output = resid_share + lax.psum_scatter(
        mlp_part.astype(jnp.bfloat16), ("br", "ch"), scatter_dimension=1, tiled=True
    ).astype(jnp.float32)
    d_mlp = cotangent.astype(jnp.bfloat16)
    d_hidden = jnp.einsum("td,fd->tf", d_mlp, w_down, preferred_element_type=jnp.float32)
    g_down = jnp.einsum("tf,td->fd", hidden_low, d_mlp, preferred_element_type=jnp.float32)
    d_gate_up = act_back(d_hidden)[0].astype(jnp.bfloat16)
    g_mlp = jnp.einsum("td,gtf->gdf", h_two, d_gate_up, preferred_element_type=jnp.float32)
    d_h_part = jnp.einsum("gtf,gdf->td", d_gate_up, w_mlp, preferred_element_type=jnp.float32)
    d_h_two = lax.psum(d_h_part, ("br", "ch"))
    g_gain_two = jnp.sum(d_h_two * normed_two, axis=0)
    d_normed_two = d_h_two * gain_two
    d_resid_one = cotangent + rstd_two * (
        d_normed_two - normed_two * jnp.mean(d_normed_two * normed_two, axis=1, keepdims=True)
    )
    d_attn = d_resid_one.astype(jnp.bfloat16)
    g_out = jnp.einsum("tk,td->kd", mixed_low, d_attn, preferred_element_type=jnp.float32)
    d_mixed = jnp.einsum("td,kd->tk", d_attn, w_out, preferred_element_type=jnp.float32)
    d_state = d_mixed * gate_act
    d_gate_act = d_mixed * state_val
    d_z_gate = jax.vjp(jax.nn.gelu, z_gate)[1](d_gate_act)[0]
    next_keep = jnp.concatenate([carry_keep[1:], jnp.ones((1, channels), jnp.float32)], axis=0)
    tail_prod, local_adj = lax.associative_scan(
        linear_combine, (next_keep, d_state), axis=0, reverse=True
    )
    arriving = entering_2(
        (carry_keep[0] * tail_prod[0], carry_keep[0] * local_adj[0]),
        "seq",
        linear_combine,
        (ones_vec, zeros_vec),
        True,
    )[1]
    adjoint = local_adj + tail_prod * arriving
    previous = jnp.concatenate([entering[None], state_val[:-1]], axis=0)

    def input_part(pre_arg, unit_arg, rate_arg):
        return gated_input(pre_arg, unit_arg, rate_arg, at_reset)

    input_back = jax.vjp(input_part, gate_pre, unit_val, decay_rate)[1]
    d_gate_pre, d_unit, g_decay = input_back((adjoint * previous, adjoint))
    d_pre_low = d_gate_pre.astype(jnp.bfloat16)
    d_pre_blocks = d_pre_low.reshape(2, row_count, head_count, block_size)
    g_gate_w = jnp.einsum(
        "thi,gthj->ghij", unit_blocks, d_pre_blocks, preferred_element_type=jnp.float32
    )
    g_gate_b = jnp.sum(d_pre_low.astype(jnp.float32), axis=1)
    d_conv = d_unit + jnp.einsum(
        "gthj,ghij->thi", d_pre_blocks, gate_w, preferred_element_type=jnp.float32
    ).reshape(row_count, channels)
    g_conv_b = jnp.sum(d_conv, axis=0)
    conv_terms = []
    d_ext = jnp.zeros((row_count + conv_span, channels), jnp.float32)
    for lag_index in range(conv_span + 1):
        lo_row = conv_span - lag_index
        masked_grad = d_conv * lag_masks[lag_index]
        conv_terms.append(jnp.sum(masked_grad * ext_rows[lo_row : lo_row + row_count], axis=0))
        d_ext = d_ext + jnp.pad(masked_grad * conv_w[lag_index], ((lo_row, lag_index), (0, 0)))
    g_conv_w = jnp.stack(conv_terms)
    from_next = from_behind(d_ext[:conv_span], "seq", -1)
    d_rec = d_ext[conv_span:] + jnp.pad(from_next, ((row_count - conv_span, 0), (0, 0)))
    d_both = jnp.stack([d_z_gate, d_rec]).astype(jnp.bfloat16)
    d_own = lax.all_to_all(d_both, "br", split_axis=0, concat_axis=2, tiled=True)[0]
    g_in = jnp.einsum("td,tq->dq", h_one, d_own, preferred_element_type=jnp.float32)
    d_h_one = lax.psum(
        jnp.einsum("tq,dq->td", d_own, w_in, preferred_element_type=jnp.float32), ("br", "ch")
    )
    g_gain_one = jnp.sum(d_h_one * normed_one, axis=0)
    d_normed_one = d_h_one * gain_one
    inputs_grad = d_resid_one + rstd_one * (
        d_normed_one - normed_one * jnp.mean(d_normed_one * normed_one, axis=1, keepdims=True)
    )
    all_sums = (
        lax.psum_scatter(g_gain_one, "seq", scatter_dimension=0, tiled=True),
        lax.psum_scatter(g_in[None], "seq", scatter_dimension=1, tiled=True),
        lax.psum_scatter(g_conv_w[:, None, None], "seq", scatter_dimension=3, tiled=True),
        lax.psum_scatter(g_conv_b[None, None], "seq", scatter_dimension=2, tiled=True),
        lax.psum_scatter(g_gate_w[:, None, None], "seq", scatter_dimension=4, tiled=True),
        lax.psum_scatter(g_gate_b[:, None, None], "seq", scatter_dimension=3, tiled=True),
        lax.psum_scatter(g_decay[None, None], "seq", scatter_dimension=2, tiled=True),
        lax.psum_scatter(decay_sum[None, None], "seq", scatter_dimension=2, tiled=True),
        lax.psum_scatter(g_out[None, None], "seq", scatter_dimension=3, tiled=True),
        lax.psum_scatter(g_gain_two, "seq", scatter_dimension=0, tiled=True),
        lax.psum_scatter(g_mlp, "seq", scatter_dimension=1, tiled=True),
        lax.psum_scatter(g_down, "seq", scatter_dimension=1, tiled=True),
    )
    decay_mean = all_sums[7] / (row_count * seq_count)
    return (
        output,
        inputs_grad,
        all_sums[0],
        all_sums[1],
        all_sums[2],
        all_sums[3],
        all_sums[4],
        all_sums[5],
        all_sums[6],
        all_sums[8],
        all_sums[9],
        all_sums[10],
        all_sums[11],
        decay_mean,
    )


def solution(mesh):
    placed = (
        P("seq", None),
        P(),
        P("seq"),
        P("br", "seq", "ch"),
        P(None, "ch", "br", "seq"),
        P("ch", "br", "seq"),
        P(None, "ch", "br", None, "seq", None),
        P(None, "ch", "br", "seq"),
        P("ch", "br", "seq"),
        P("ch", "br", None, "seq"),
        P("seq"),
        P(None, "seq", ("br", "ch")),
        P(("br", "ch"), "seq"),
        P("seq", None),
    )
    return jax.shard_map(
        per_device,
        mesh=mesh,
        in_specs=placed,
        out_specs=(
            P("seq", ("br", "ch")),
            P("seq", None),
            P("seq"),
            P("br", "seq", "ch"),
            P(None, "ch", "br", "seq"),
            P("ch", "br", "seq"),
            P(None, "ch", "br", None, "seq", None),
            P(None, "ch", "br", "seq"),
            P("ch", "br", "seq"),
            P("ch", "br", None, "seq"),
            P("seq"),
            P(None, "seq", ("br", "ch")),
            P(("br", "ch"), "seq"),
            P("ch", "br", "seq"),
        ),
        check_vma=False,
    )
```

profile of v0, /device:TPU:0, one launch (start us, length us, event | category | flops | bytes accessed | tf_op | source)
XLA Modules:
  0.0 3215.4 jit_solution(14389025672072379194)
XLA Ops:
  10.9 22.4 all-gather
  39.2 17.4 all-reduce.97
  56.8 32.1 all_gather.50
  146.1 34.8 %all_gather.51 = bf16[2,1,1,4,160,160]{5,3,2,1,0,4:T(4,128)(2,1)} all-gather(bf16[2,1,1,4,20,160]{5,3,2,1,0,4:T(4,128)(2,1)S(1)} %copy.113), channel_id=1, replica_groups=mesh['br'=2,'seq'=8,'ch'=2] {'seq'}, dimensions={4}, use_global_device_ids=true | all-gather | bytes 460800 | tf_op jit(solution)/shard_map/all_gather | solution.py:74
  183.3 31.1 all_gather.52
  542.3 31.2 all-gather.1
  574.3 30.2 all-gather.2
  622.4 19.4 all-gather.3
  641.8 132.5 %all-reduce.103.cloned.1.call-done = f32[1024,2048]{1,0:T(8,128)} async-done(((f32[1024,2048]{1,0:T(8,128)}), f32[1024,2048]{1,0:T(8,128)}) %all-reduce.103.cloned.1.call-update) | async-done | bytes 8388624 | tf_op jit(solution)/shard_map/psum | solution.py:146
  784.4 168.6 %all-gather.15.cloned.1.call-done = bf16[2,2048,1536]{2,1,0:T(8,128)(2,1)} async-done(((bf16[2,256,1536]{2,1,0:T(8,128)(2,1)}), bf16[2,2048,1536]{2,1,0:T(8,128)(2,1)}) %all-gather.15.cloned.1.call-update) | async-done | bytes 12582928 | tf_op jit(solution)/shard_map/all_gather | solution.py:79
  953.0 20.6 convolution_bitcast_fusion.2
  973.6 79.5 %all-gather.17.cloned.1.call-done = bf16[1536,2048]{1,0:T(8,128)(2,1)} async-done(((bf16[1536,256]{1,0:T(8,128)(2,1)}), bf16[1536,2048]{1,0:T(8,128)(2,1)}) %all-gather.17.cloned.1.call-update) | async-done | bytes 6291472 | tf_op jit(solution)/shard_map/all_gather | solution.py:80
  1053.0 21.0 multiply_bitcast_fusion
  1074.1 21.2 convolution_bitcast_fusion.3
  1153.7 92.8 %all-reduce.105.cloned.1.call-done = f32[1024,2048]{1,0:T(8,128)} async-done(((f32[1024,2048]{1,0:T(8,128)}), f32[1024,2048]{1,0:T(8,128)}) %all-reduce.105.cloned.1.call-update) | async-done | bytes 8388624 | tf_op jit(solution)/shard_map/psum | solution.py:164
  1555.1 20.8 rev.8
  1576.0 21.0 rev.9
  1596.9 30.3 all-gather.4
  1627.2 30.2 all-gather.5
  1739.5 20.4 all_to_all.30
  1774.0 23.8 convolution_bitcast_fusion
  1840.2 45.6 %reduce-scatter.39.cloned.1.call-done = f32[80,1]{1,0:T(8,128)} async-done(((f32[640,1]{1,0:T(8,128)}), f32[80,1]{1,0:T(8,128)}) %reduce-scatter.39.cloned.1.call-update) | async-done | bytes 336
  1887.1 62.1 %reduce-scatter.35.cloned.1.call-done = f32[80,2]{1,0:T(8,128)} async-done(((f32[640,2]{1,0:T(8,128)}), f32[80,2]{1,0:T(8,128)}) %reduce-scatter.35.cloned.1.call-update) | async-done | bytes 656
  1950.9 62.0 %reduce-scatter.31.cloned.1.call-done = f32[80,4]{1,0:T(8,128)} async-done(((f32[640,4]{1,0:T(8,128)}), f32[80,4]{1,0:T(8,128)}) %reduce-scatter.31.cloned.1.call-update) | async-done | bytes 1296
  2014.7 84.6 %all-reduce.109.cloned.1.call-done = f32[2,1,1,4,160,160]{5,3,2,1,0,4:T(4,128)} async-done(((f32[2,1,1,4,160,160]{5,3,2,1,0,4:T(4,128)}), f32[2,1,1,4,160,160]{5,3,2,1,0,4:T(4,128)}) %all-reduce.109.cloned.1.call-update) | async-done | bytes 819216
  2100.9 44.8 %reduce-scatter.21.cloned.1.call-done = bf16[1024,512]{1,0:T(8,128)(2,1)} async-done(((bf16[1024,2048]{1,0:T(8,128)(2,1)}), bf16[1024,512]{1,0:T(8,128)(2,1)}) %reduce-scatter.21.cloned.1.call-update) | async-done | bytes 1048592 | tf_op jit(solution)/shard_map/reduce_scatter | solution.py:155
  2149.3 151.7 %all-reduce.107.cloned.1.call-done = f32[1024,2048]{1,0:T(8,128)} async-done(((f32[1024,2048]{1,0:T(8,128)}), f32[1024,2048]{1,0:T(8,128)}) %all-reduce.107.cloned.1.call-update) | async-done | bytes 8388624 | tf_op jit(solution)/shard_map/psum | solution.py:218
  2307.9 39.1 %all-reduce.96 = (f32[2048]{0:T(1024)S(1)}, f32[2048]{0:T(1024)S(1)}) all-reduce(f32[2048]{0:T(1024)S(1)} %get-tuple-element.364, f32[2048]{0:T(1024)S(1)} %copy-done.64), channel_id=3, replica_groups=mesh['br'=2,'seq'=8,'ch'=2] {'seq'}, use_global_device_ids=true, to_apply=%region_16.17.clone | all-reduce | flops 4096 | bytes 32768
  2361.2 347.8 %reduce-scatter.27.cloned.1.call-done = f32[2,256,1536]{1,2,0:T(8,128)} async-done(((f32[2,2048,1536]{1,2,0:T(8,128)}), f32[2,256,1536]{1,2,0:T(8,128)}) %reduce-scatter.27.cloned.1.call-update) | async-done | bytes 3145744 | tf_op jit(solution)/shard_map/reduce_scatter | solution.py:237
  2712.6 102.7 %reduce-scatter.25.cloned.1.call-done = f32[1,1,640,256]{3,2,1,0:T(8,128)} async-done(((f32[1,1,640,2048]{3,2,1,0:T(8,128)}), f32[1,1,640,256]{3,2,1,0:T(8,128)}) %reduce-scatter.25.cloned.1.call-update) | async-done | bytes 655376 | tf_op jit(solution)/shard_map/reduce_scatter | solution.py:235
  2815.3 211.6 %reduce-scatter.29.cloned.1.call-done = f32[1536,256]{1,0:T(8,128)} async-done(((f32[1536,2048]{1,0:T(8,128)}), f32[1536,256]{1,0:T(8,128)}) %reduce-scatter.29.cloned.1.call-update) | async-done | bytes 1572880 | tf_op jit(solution)/shard_map/reduce_scatter | solution.py:238
  3026.9 181.2 %reduce-scatter.23.cloned.1.call-done = f32[1,256,1280]{2,1,0:T(8,128)} async-done(((f32[1,2048,1280]{2,1,0:T(8,128)}), f32[1,256,1280]{2,1,0:T(8,128)}) %reduce-scatter.23.cloned.1.call-update) | async-done | bytes 1310736 | tf_op jit(solution)/shard_map/reduce_scatter | solution.py:228
  (724 shorter events, 963.0 us)
Async XLA Ops:
  7.2 98.1 %all-gather.11.cloned.1.call-start = ((), (), s32[]{:S(2)}) async-start(), calls=%async_computation.12 | async-start | bytes 5898240 | tf_op jit(solution)/shard_map/all_gather | solution.py:71
  7.9 603.2 %all-gather.13.cloned.1.call-start = ((), (), s32[]{:S(2)}) async-start(), calls=%async_computation.13 | async-start | bytes 2949120 | tf_op jit(solution)/shard_map/all_gather | solution.py:77
  56.6 201.6 %copy-start.49 = (f32[640]{0:T(1024)}, f32[640]{0:T(1024)S(1)}, u32[]{:S(2)}) copy-start(f32[640]{0:T(1024)S(1)} %convert_element_type.147) | copy-start | bytes 7684
  142.0 83.3 %all-to-all-start = ((bf16[2,2,327680]{2,1,0:T(2,128)(2,1)}), bf16[2,2,327680]{2,1,0:T(2,128)(2,1)S(1)}, u32[]{:S(2)}, u32[]{:S(2)}) async-start(bf16[2,2,327680]{2,1,0:T(2,128)(2,1)} %reshape.232), calls=%async_computation | async-start | bytes 5242880 | tf_op jit(solution)/shard_map/all_to_all | solution.py:111
  146.0 628.3 %all-reduce.103.cloned.1.call-start = ((), (), s32[]{:S(2)}) async-start(), calls=%async_computation.14 | async-start | bytes 16777216 | tf_op jit(solution)/shard_map/psum | solution.py:146
  235.9 2.7 collective-permute-start
  621.2 331.8 %all-gather.15.cloned.1.call-start = ((), (), s32[]{:S(2)}) async-start(), calls=%async_computation.15 | async-start | bytes 14155776 | tf_op jit(solution)/shard_map/all_gather | solution.py:79
  621.8 431.3 %all-gather.17.cloned.1.call-start = ((), (), s32[]{:S(2)}) async-start(), calls=%async_computation.16 | async-start | bytes 7077888 | tf_op jit(solution)/shard_map/all_gather | solution.py:80
  622.4 624.1 %all-reduce.105.cloned.1.call-start = ((), (), s32[]{:S(2)}) async-start(), calls=%async_computation.18 | async-start | bytes 16777216 | tf_op jit(solution)/shard_map/psum | solution.py:164
  641.8 612.3 %copy-start.58 = (f32[8,1,256]{2,1,0:T(1,128)}, f32[8,1,256]{2,1,0:T(1,128)S(1)}, u32[]{:S(2)}) copy-start(f32[8,1,256]{2,1,0:T(1,128)S(1)} %convert_element_type.146) | copy-start | bytes 24580
  1095.3 742.2 %reduce-scatter.33.cloned.1.call-start = ((), (), s32[]{:S(2)}) async-start(), calls=%async_computation.25 | async-start | bytes 368640
  1575.9 82.3 %copy-start.42 = (f32[640]{0:T(1024)S(1)}, f32[640]{0:T(1024)}, u32[]{:S(2)}) copy-start(f32[640]{0:T(1024)} %copy-done.41) | copy-start | bytes 7684
  1575.9 82.3 %copy-start.44 = (f32[640]{0:T(1024)S(1)}, f32[640]{0:T(1024)}, u32[]{:S(2)}) copy-start(f32[640]{0:T(1024)} %copy-done.43) | copy-start | bytes 7684
  1575.9 82.3 %copy-start.46 = (f32[640]{0:T(1024)S(1)}, f32[640]{0:T(1024)}, u32[]{:S(2)}) copy-start(f32[640]{0:T(1024)} %copy-done.45) | copy-start | bytes 7684
  1575.9 82.3 %copy-start.48 = (f32[640]{0:T(1024)S(1)}, f32[640]{0:T(1024)}, u32[]{:S(2)}) copy-start(f32[640]{0:T(1024)} %copy-done.47) | copy-start | bytes 7684
  1575.9 82.3 %copy-start.50 = (f32[640]{0:T(1024)S(1)}, f32[640]{0:T(1024)}, u32[]{:S(2)}) copy-start(f32[640]{0:T(1024)} %copy-done.49) | copy-start | bytes 7684
  1576.0 82.3 %copy-start.52 = (f32[640]{0:T(1024)S(1)}, f32[640]{0:T(1024)}, u32[]{:S(2)}) copy-start(f32[640]{0:T(1024)} %copy-done.51) | copy-start | bytes 7684
  1576.0 82.3 %copy-start.66 = (pred[1024]{0:T(1024)(128)(4,1)S(1)}, pred[1024]{0:T(1024)(128)(4,1)}, u32[]{:S(2)}) copy-start(pred[1024]{0:T(1024)(128)(4,1)} %copy-done.65) | copy-start | bytes 3076
  1576.0 82.3 %copy-start.89 = (f32[1,640]{1,0:T(1,128)S(1)}, f32[1,640]{1,0:T(1,128)}, u32[]{:S(2)}) copy-start(f32[1,640]{1,0:T(1,128)} %broadcast_in_dim.108) | copy-start | bytes 7684
  1697.1 141.7 %reduce-scatter.37.cloned.1.call-start = ((), (), s32[]{:S(2)}) async-start(), calls=%async_computation.27 | async-start | bytes 368640
  1699.0 186.7 %reduce-scatter.39.cloned.1.call-start = ((), (), s32[]{:S(2)}) async-start(), calls=%async_computation.28 | async-start | bytes 368640
  1704.6 244.6 %reduce-scatter.35.cloned.1.call-start = ((), (), s32[]{:S(2)}) async-start(), calls=%async_computation.26 | async-start | bytes 368640
  1706.8 306.1 %reduce-scatter.31.cloned.1.call-start = ((), (), s32[]{:S(2)}) async-start(), calls=%async_computation.24 | async-start | bytes 368640
  1713.5 385.8 %all-reduce.109.cloned.1.call-start = ((), (), s32[]{:S(2)}) async-start(), calls=%async_computation.29 | async-start | bytes 2621440
  1719.6 426.2 %reduce-scatter.21.cloned.1.call-start = ((), (), s32[]{:S(2)}) async-start(), calls=%async_computation.17 | async-start | bytes 5242880 | tf_op jit(solution)/shard_map/reduce_scatter | solution.py:155
  1730.6 570.4 %all-reduce.107.cloned.1.call-start = ((), (), s32[]{:S(2)}) async-start(), calls=%async_computation.19 | async-start | bytes 16777216 | tf_op jit(solution)/shard_map/psum | solution.py:218
  1733.3 5.6 collective-permute-start.1
  1773.4 935.7 %reduce-scatter.27.cloned.1.call-start = ((), (), s32[]{:S(2)}) async-start(), calls=%async_computation.22 | async-start | bytes 28311552 | tf_op jit(solution)/shard_map/reduce_scatter | solution.py:237
  1797.9 1017.4 %reduce-scatter.25.cloned.1.call-start = ((), (), s32[]{:S(2)}) async-start(), calls=%async_computation.21 | async-start | bytes 5898240 | tf_op jit(solution)/shard_map/reduce_scatter | solution.py:235
  1809.1 1217.8 %reduce-scatter.29.cloned.1.call-start = ((), (), s32[]{:S(2)}) async-start(), calls=%async_computation.23 | async-start | bytes 14155776 | tf_op jit(solution)/shard_map/reduce_scatter | solution.py:238
  1823.6 1384.5 %reduce-scatter.23.cloned.1.call-start = ((), (), s32[]{:S(2)}) async-start(), calls=%async_computation.20 | async-start | bytes 11796480 | tf_op jit(solution)/shard_map/reduce_scatter | solution.py:228
  2149.3 158.6 %copy-start.64 = (f32[2048]{0:T(1024)S(1)}, f32[2048]{0:T(1024)}, u32[]{:S(2)}) copy-start(f32[2048]{0:T(1024)} %get-tuple-element.362) | copy-start | bytes 24580
  (89 other events, 1603.4 us)
Sparse Core Ops, SparseCore 0:
  10.2 95.0 all-gather.10
  107.4 60.5 all-gather.12
  621.3 152.9 all-reduce.102
  776.4 176.5 all-gather.14
  954.9 98.1 all-gather.16
  1095.4 151.0 all-reduce.104
  1697.2 61.2 reduce-scatter.32
  1761.8 60.2 reduce-scatter.36
  1825.4 60.3 reduce-scatter.38
  1888.9 60.2 reduce-scatter.34
  1952.5 60.3 reduce-scatter.30
  2016.9 82.4 all-reduce.108
  2102.0 43.6 reduce-scatter.20
  2148.1 152.8 all-reduce.106
  2304.7 404.2 reduce-scatter.26
  2713.1 102.1 reduce-scatter.24
  2819.3 207.4 reduce-scatter.28
  3030.9 177.1 reduce-scatter.22
where the time goes:
time: 3240 us; the launch traced here: 3220 us
  waiting for transfers between devices  1790 us (55%)
  local copies, waits for them, and re-layouts  638 us (20%)
  blocking collectives  339 us (10%)
  other arithmetic  241 us (7%)
  matrix products  182 us (6%)
    reduce_scatter x1, waiting for transfers between devices, per_device(): lax.psum_scatter(g_mlp, 'seq', scatter_dimension=1, tiled=True)  348 us
    unnamed x24, waiting for transfers between devices  257 us
    reduce_scatter x1, waiting for transfers between devices, per_device(): lax.psum_scatter(g_down, 'seq', scatter_dimension=1, tiled=True)  212 us
    slice x73, local copies, waits for them, and re-layouts, per_device(): lax.associative_scan(linear_combine, (next_keep, d_state), axis=0, revers...  203 us
    reduce_scatter x1, waiting for transfers between devices, per_device(): lax.psum_scatter(g_in[None], 'seq', scatter_dimension=1, tiled=True)  181 us
    all_gather x1, waiting for transfers between devices, per_device(): lax.all_gather(mlp_in, 'seq', axis=1, tiled=True)  169 us
    psum x1, waiting for transfers between devices, per_device(): lax.psum(jnp.einsum('tq,dq->td', d_own, w_in, preferred_element_type=jnp....  152 us
    psum x1, waiting for transfers between devices, per_device(): resid_one = inputs + lax.psum(attn_part, ('br', 'ch'))  133 us
  transfers between devices with their start and end apart: 21, of which 16 were waited for; matrix products, arithmetic and copies ran while one was open for 19% of the time, Pallas kernels for 0%

commit v1 on v0

v1 whole, which is shorter than its diff:
```python
import functools

import jax
import jax.numpy as jnp
from jax import lax
from jax.experimental import pallas as pl
from jax.experimental.pallas import tpu as pltpu
from jax.sharding import PartitionSpec as P

NORM_EPS = 1e-06
DECAY_SCALE = 8.0
GELU_C = 0.7978845608028654
GELU_K = 0.044715
LANES = 128
ROWS = 128
SWAP = [(0, 1), (1, 0)]
F32 = jnp.float32
BF16 = jnp.bfloat16


def ring_order(count):
    return list(range(0, count, 2)) + list(range(count - 1, 0, -2))


def ring_place(index, count):
    half = index // 2
    return jnp.where(index % 2 == 0, half, count - 1 - half)


class Ring:
    def __init__(self, count, depth=2):
        order = ring_order(count)
        self.count = count
        self.pairs = {
            1: [(order[i], order[(i + 1) % count]) for i in range(count)],
            -1: [(order[(i + 1) % count], order[i]) for i in range(count)],
        }
        self.done = {1: [], -1: []}
        self.depth = depth

    def hop(self, x, way):
        done = self.done[way]
        if len(done) >= self.depth:
            x, _ = lax.optimization_barrier((x, done[-self.depth]))
        got = lax.ppermute(x, "seq", self.pairs[way])
        done.append(got)
        return got

    def gather(self, x):
        n = self.count
        parts = [None] * n
        parts[0] = x
        ahead = behind = x
        for step in range(1, n // 2):
            ahead = self.hop(ahead, 1)
            behind = self.hop(behind, -1)
            parts[n - step] = ahead
            parts[step] = behind
        cut = x.shape[0] // 2
        far = [self.hop(ahead[:cut], 1), self.hop(behind[cut:], -1)]
        parts[n // 2] = jnp.concatenate(far, axis=0)
        return parts

    def scatter(self, part):
        n = self.count
        half = n // 2
        far = part(half)
        cut = far.shape[0] // 2
        ahead = self.hop(far[:cut].astype(BF16), 1)
        behind = self.hop(far[cut:].astype(BF16), -1)
        for step in range(1, half):
            up, down = part(half - step), part(half + step)
            if step == 1:
                up = jnp.concatenate([up[:cut] + ahead.astype(F32), up[cut:]], axis=0)
                down = jnp.concatenate([down[:cut], down[cut:] + behind.astype(F32)], axis=0)
            else:
                up = up + ahead.astype(F32)
                down = down + behind.astype(F32)
            ahead = self.hop(up.astype(BF16), 1)
            behind = self.hop(down.astype(BF16), -1)
        return part(0) + (ahead.astype(F32) + behind.astype(F32))


def group_sum(part):
    half = part.shape[0] // 2
    core = lax.axis_index("ch")
    mine = lax.dynamic_slice_in_dim(part, core * half, half, 0)
    theirs = lax.dynamic_slice_in_dim(part, (1 - core) * half, half, 0)
    chip = (mine.astype(F32) + lax.ppermute(theirs, "ch", SWAP).astype(F32)).astype(BF16)
    both = (chip.astype(F32) + lax.ppermute(chip, "br", SWAP).astype(F32)).astype(BF16)
    other = lax.ppermute(both, "ch", SWAP)
    first = core == 0
    return jnp.concatenate([jnp.where(first, both, other), jnp.where(first, other, both)], axis=0)


def tiny_group_sum(x):
    x = x + lax.ppermute(x, "ch", SWAP)
    return x + lax.ppermute(x, "br", SWAP)


def entering(pair, reverse):
    count, index = lax.axis_size("seq"), lax.axis_index("seq")
    spread = jnp.broadcast_to(pair[None], (count,) + pair.shape)
    every = lax.all_to_all(spread, "seq", 0, 0, tiled=True)
    value = jnp.zeros(pair.shape[1:], F32)
    for k in range(count):
        at = count - 1 - k if reverse else k
        new = every[at, 1] + every[at, 0] * value
        value = jnp.where((at > index) if reverse else (at < index), new, value)
    return value


def gelu_both(x):
    square = x * x
    bent = jnp.tanh(GELU_C * (x + GELU_K * (x * square)))
    half = 0.5 * (1.0 + bent)
    slope = half + 0.5 * x * (1.0 - bent * bent) * (GELU_C * (1.0 + 3.0 * GELU_K * square))
    return x * half, slope


def minus_expm1(x, exp_x):
    series = 1.0 + x * (1.0 / 6.0)
    for k in (5.0, 4.0, 3.0, 2.0):
        series = 1.0 + x * (1.0 / k) * series
    return jnp.where(x > -0.2, -x * series, 1.0 - exp_x)


def scan_rows(keep, add, reverse):
    rows = keep.shape[0]
    at = lax.broadcasted_iota(jnp.int32, keep.shape, 0)
    step = 1
    while step < rows:
        shift = rows - step if reverse else step
        inside = (at < rows - step) if reverse else (at >= step)
        far_add = jnp.where(inside, pltpu.roll(add, shift, 0), 0.0)
        add = add + keep * far_add
        keep = keep * jnp.where(inside, pltpu.roll(keep, shift, 0), 1.0)
        step *= 2
    return keep, add


def forward_kernel(
    z_ref, rim_ref, mask_ref, conv_ref, wide_ref, bias_ref, rate_ref,
    unit_ref, gate_ref, loc_ref, prod_ref, last_ref, total_ref, ext,
):
    block = pl.program_id(0)
    rows, channels = z_ref.shape
    span = conv_ref.shape[0] - 2

    @pl.when(block == 0)
    def _():
        ext[0:8] = rim_ref[...]
        last_ref[0:1] = jnp.ones((1, channels), F32)
        last_ref[1:8] = jnp.zeros((7, channels), F32)
        total_ref[...] = jnp.zeros_like(total_ref)

    @pl.when(block > 0)
    def _():
        ext[0:8] = ext[rows : rows + 8]

    ext[8 : rows + 8] = z_ref[...].astype(F32)
    conv = jnp.broadcast_to(conv_ref[span + 1 : span + 2], (rows, channels))
    for lag in range(span + 1):
        conv = conv + conv_ref[lag : lag + 1] * ext[8 - lag : 8 - lag + rows] * mask_ref[:, lag : lag + 1]
    unit_ref[...] = conv.astype(BF16)
    pre = jnp.dot(unit_ref[...], wide_ref[...], preferred_element_type=F32) + bias_ref[...]
    gate_ref[...] = jax.nn.sigmoid(pre)
    reset = mask_ref[:, span + 1 : span + 2] > 0.5
    for lane in range(0, channels, LANES):
        own = slice(lane, lane + LANES)
        in_gate = gate_ref[:, channels + lane : channels + lane + LANES]
        log_decay = gate_ref[:, own] * rate_ref[0:1, own]
        decay = jnp.exp(log_decay)
        scale = jnp.sqrt(minus_expm1(2.0 * log_decay, decay * decay))
        total_ref[0:1, own] += jnp.sum(decay, axis=0, keepdims=True)
        keep = jnp.where(reset, 0.0, decay)
        drive = jnp.where(reset, 1.0, scale) * in_gate * unit_ref[:, own].astype(F32)
        prod, loc = scan_rows(keep, drive, False)
        loc = loc + prod * last_ref[1:2, own]
        prod = prod * last_ref[0:1, own]
        loc_ref[:, own] = loc
        prod_ref[:, own] = prod
        last_ref[0:1, own] = prod[rows - 1 :]
        last_ref[1:2, own] = loc[rows - 1 :]


def adjoint_kernel(
    dmix_ref, zg_ref, loc_ref, prod_ref, gate_ref, mask_ref, enter_ref, rate_ref,
    adj_ref, tail_ref, dzg_ref, head_ref, after,
):
    step = pl.program_id(0)
    rows, channels = zg_ref.shape
    reset_col = mask_ref.shape[1] - 1

    @pl.when(step == 0)
    def _():
        head_ref[0:1] = jnp.ones((1, channels), F32)
        head_ref[1:8] = jnp.zeros((7, channels), F32)
        after[0:2] = jnp.ones((2, channels), F32)
        after[2:8] = jnp.zeros((6, channels), F32)

    reset = mask_ref[:, 4:5] > 0.5
    for lane in range(0, channels, LANES):
        own = slice(lane, lane + LANES)
        state = loc_ref[:, own] + prod_ref[:, own] * enter_ref[0:1, own]
        act, slope = gelu_both(zg_ref[:, own].astype(F32))
        dmix = dmix_ref[:, own].astype(F32)
        dzg_ref[:, own] = (dmix * state * slope).astype(BF16)
        keep = jnp.where(reset, 0.0, jnp.exp(gate_ref[:, own] * rate_ref[0:1, own]))
        at = lax.broadcasted_iota(jnp.int32, keep.shape, 0)
        nxt = jnp.where(at == rows - 1, after[0:1, own], pltpu.roll(keep, rows - 1, 0))
        tail, adj = scan_rows(nxt, dmix * act, True)
        adj = adj + tail * after[2:3, own]
        tail = tail * after[1:2, own]
        adj_ref[:, own] = adj
        tail_ref[:, own] = tail
        after[0:1, own] = keep[0:1]
        after[1:2, own] = tail[0:1]
        after[2:3, own] = adj[0:1]
        head_ref[0:1, own] = keep[0:1] * tail[0:1]
        head_ref[1:2, own] = keep[0:1] * adj[0:1]


def backward_kernel(
    adj_ref, tail_ref, arrive_ref, loc_ref, prod_ref, loc0_ref, prod0_ref, enter_ref, gate_ref,
    unit_ref, mask_ref, z_ref, z0_ref, rim_ref, conv_ref, wide_ref, rate_ref,
    dz_ref, gw_ref, sums_ref, edge_ref, dpre, ddir, zext, moved,
):
    step = pl.program_id(0)
    block = pl.num_programs(0) - 1 - step
    rows, channels = z_ref.shape
    span = conv_ref.shape[0] - 2

    @pl.when(step == 0)
    def _():
        gw_ref[...] = jnp.zeros_like(gw_ref)
        sums_ref[...] = jnp.zeros_like(sums_ref)
        moved[...] = jnp.zeros_like(moved)

    @pl.when(step > 0)
    def _():
        for lag in range(1, span + 1):
            moved[lag - 1, rows : rows + 8] = moved[lag - 1, 0:8]

    zext[8 : rows + 8] = z_ref[...].astype(F32)

    @pl.when(block == 0)
    def _():
        zext[0:8] = rim_ref[...]

    @pl.when(block > 0)
    def _():
        zext[0:8] = z0_ref[8:16].astype(F32)

    reset = mask_ref[:, 4:5] > 0.5
    for lane in range(0, channels, LANES):
        own = slice(lane, lane + LANES)
        two = slice(channels + lane, channels + lane + LANES)
        enter = enter_ref[0:1, own]
        adj = adj_ref[:, own] + tail_ref[:, own] * arrive_ref[0:1, own]
        state = loc_ref[:, own] + prod_ref[:, own] * enter
        before = jnp.where(block == 0, enter, loc0_ref[7:8, own] + prod0_ref[7:8, own] * enter)
        at = lax.broadcasted_iota(jnp.int32, state.shape, 0)
        previous = jnp.where(at == 0, before, pltpu.roll(state, 1, 0))
        rec_gate, in_gate = gate_ref[:, own], gate_ref[:, two]
        unit = unit_ref[:, own].astype(F32)
        rate = rate_ref[0:1, own]
        log_decay = rec_gate * rate
        decay = jnp.exp(log_decay)
        scale = jnp.sqrt(minus_expm1(2.0 * log_decay, decay * decay))
        dlog = decay * (adj * previous - adj * in_gate * unit * (decay / scale))
        dlog = jnp.where(reset, 0.0, dlog)
        sums_ref[0:1, own] += jnp.sum(dlog * rec_gate, axis=0, keepdims=True)
        scale = jnp.where(reset, 1.0, scale)
        dpre[:, own] = (dlog * rate * (rec_gate * (1.0 - rec_gate))).astype(BF16)
        through = adj * scale
        dpre[:, two] = (through * unit * (in_gate * (1.0 - in_gate))).astype(BF16)
        ddir[:, own] = through * in_gate

    gw_ref[...] += lax.dot_general(
        unit_ref[...], dpre[...], (((0,), (0,)), ((), ())), preferred_element_type=F32
    )
    dconv_all = ddir[...] + lax.dot_general(
        dpre[...], wide_ref[...], (((1,), (1,)), ((), ())), preferred_element_type=F32
    )
    ddir[...] = dconv_all
    for lane in range(0, channels, LANES):
        own = slice(lane, lane + LANES)
        two = slice(channels + lane, channels + lane + LANES)
        dconv = ddir[:, own]
        sums_ref[1:2, own] += jnp.sum(dpre[:, own].astype(F32), axis=0, keepdims=True)
        sums_ref[2:3, own] += jnp.sum(dpre[:, two].astype(F32), axis=0, keepdims=True)
        sums_ref[3:4, own] += jnp.sum(dconv, axis=0, keepdims=True)
        sums_ref[4:5, own] += jnp.sum(dconv * zext[8 : 8 + rows, own], axis=0, keepdims=True)
        dz = dconv * conv_ref[0:1, own]
        edge = jnp.zeros((8, LANES), F32)
        at8 = lax.broadcasted_iota(jnp.int32, edge.shape, 0)
        for lag in range(1, span + 1):
            kept = dconv * mask_ref[:, lag : lag + 1]
            sums_ref[4 + lag : 5 + lag, own] += jnp.sum(
                kept * zext[8 - lag : 8 - lag + rows, own], axis=0, keepdims=True
            )
            moved[lag - 1, 0:rows, own] = kept * conv_ref[lag : lag + 1, own]
            dz = dz + moved[lag - 1, lag : lag + rows, own]
            edge = edge + jnp.where(
                at8 >= 8 - lag, pltpu.roll(moved[lag - 1, 0:8, own], 8 - lag, 0), 0.0
            )
        dz_ref[:, own] = dz.astype(BF16)
        edge_ref[0:8, own] = edge

        @pl.when(step == 0)
        def _():
            edge_ref[8:16, own] = dz[rows - 8 :]


def kernel_params():
    return pltpu.CompilerParams(
        dimension_semantics=("arbitrary",), vmem_limit_bytes=48 * 1024 * 1024
    )


def forward_local(z, rim, mask, conv, wide, bias, rate):
    tokens, channels = z.shape[0], rate.shape[1]
    rows = min(ROWS, tokens)
    spec = lambda shape, index: pl.BlockSpec(shape, index)
    whole = lambda x: pl.BlockSpec(x.shape, lambda i: (0,) * x.ndim)
    time = lambda width, at=0: pl.BlockSpec((rows, width), lambda i: (i, at))
    fixed = pl.BlockSpec((8, channels), lambda i: (0, 0))
    return pl.pallas_call(
        forward_kernel,
        grid=(tokens // rows,),
        in_specs=[time(channels, 1), whole(rim), time(mask.shape[1]), whole(conv), whole(wide), whole(bias), whole(rate)],
        out_specs=[time(channels), time(2 * channels), time(channels), time(channels), fixed, fixed],
        out_shape=[
            jax.ShapeDtypeStruct((tokens, channels), BF16),
            jax.ShapeDtypeStruct((tokens, 2 * channels), F32),
            jax.ShapeDtypeStruct((tokens, channels), F32),
            jax.ShapeDtypeStruct((tokens, channels), F32),
            jax.ShapeDtypeStruct((8, channels), F32),
            jax.ShapeDtypeStruct((8, channels), F32),
        ],
        scratch_shapes=[pltpu.VMEM((rows + 8, channels), F32)],
        compiler_params=kernel_params(),
    )(z, rim, mask, conv, wide, bias, rate)


def adjoint_local(dmix, z, loc, prod, gate, mask, enter, rate):
    tokens, channels = loc.shape
    rows = min(ROWS, tokens)
    last = tokens // rows - 1
    whole = lambda x: pl.BlockSpec(x.shape, lambda i: (0,) * x.ndim)
    time = lambda width: pl.BlockSpec((rows, width), lambda i: (last - i, 0))
    return pl.pallas_call(
        adjoint_kernel,
        grid=(tokens // rows,),
        in_specs=[time(channels)] * 5 + [time(mask.shape[1]), whole(enter), whole(rate)],
        out_specs=[time(channels)] * 3 + [pl.BlockSpec((8, channels), lambda i: (0, 0))],
        out_shape=[
            jax.ShapeDtypeStruct((tokens, channels), F32),
            jax.ShapeDtypeStruct((tokens, channels), F32),
            jax.ShapeDtypeStruct((tokens, channels), BF16),
            jax.ShapeDtypeStruct((8, channels), F32),
        ],
        scratch_shapes=[pltpu.VMEM((8, channels), F32)],
        compiler_params=kernel_params(),
    )(dmix, z, loc, prod, gate, mask, enter, rate)


def backward_local(adj, tail, arrive, loc, prod, enter, gate, unit, mask, z, rim, conv, wide, rate):
    tokens, channels = loc.shape
    rows = min(ROWS, tokens)
    last = tokens // rows - 1
    whole = lambda x: pl.BlockSpec(x.shape, lambda i: (0,) * x.ndim)
    time = lambda width, at=0: pl.BlockSpec((rows, width), lambda i: (last - i, at))
    ahead = lambda size, at=0: pl.BlockSpec(
        (size, channels), lambda i: (jnp.maximum((last - i) * (rows // size) - 1, 0), at)
    )
    fixed = lambda size, width: pl.BlockSpec((size, width), lambda i: (0, 0))
    span = conv.shape[0] - 2
    return pl.pallas_call(
        backward_kernel,
        grid=(tokens // rows,),
        in_specs=[
            time(channels), time(channels), whole(arrive), time(channels), time(channels), ahead(8), ahead(8),
            whole(enter), time(2 * channels), time(channels), time(mask.shape[1]), time(channels, 1), ahead(16, 1),
            whole(rim), whole(conv), whole(wide), whole(rate),
        ],
        out_specs=[time(channels), fixed(channels, 2 * channels), fixed(16, channels), fixed(16, channels)],
        out_shape=[
            jax.ShapeDtypeStruct((tokens, channels), BF16),
            jax.ShapeDtypeStruct((channels, 2 * channels), F32),
            jax.ShapeDtypeStruct((16, channels), F32),
            jax.ShapeDtypeStruct((16, channels), F32),
        ],
        scratch_shapes=[
            pltpu.VMEM((rows, 2 * channels), BF16),
            pltpu.VMEM((rows, channels), F32),
            pltpu.VMEM((rows + 8, channels), F32),
            pltpu.VMEM((span, rows + 8, channels), F32),
        ],
        compiler_params=kernel_params(),
    )(adj, tail, arrive, loc, prod, loc, prod, enter, gate, unit, mask, z, z, rim, conv, wide, rate)


def pad_rows(x, rows, before=False):
    extra = rows - x.shape[0]
    return jnp.pad(x, ((extra, 0) if before else (0, extra), (0, 0)))


def per_device(
    inputs,
    lengths,
    norm_gain1,
    in_weight,
    conv_weight,
    conv_bias,
    gate_weight,
    gate_bias,
    decay_param,
    out_weight,
    norm_gain2,
    mlp_in,
    mlp_down,
    cotangent,
):
    tokens, width = inputs.shape
    count, index = lax.axis_size("seq"), lax.axis_index("seq")
    br, ch = lax.axis_index("br"), lax.axis_index("ch")
    place = ring_place(index, count)
    order = jnp.asarray(ring_order(count), jnp.int32)
    cols = width // count
    taps = conv_weight.shape[0]
    span = taps - 1
    part_ch = conv_weight.shape[3]
    channels = part_ch * count
    heads, part_in, block = gate_weight.shape[3], gate_weight.shape[4], gate_weight.shape[5]
    true_of = [order[(place + k) % count] for k in range(count)]
    ring_of = [(ring_place(jnp.int32(s), count) - place) % count for s in range(count)]

    def to_ring(x):
        return jnp.concatenate(
            [lax.dynamic_slice_in_dim(x, true_of[k] * cols, cols, 1) for k in range(count)], axis=1
        )

    def from_ring(x):
        return jnp.concatenate(
            [lax.dynamic_slice_in_dim(x, ring_of[s] * cols, cols, 1) for s in range(count)], axis=1
        )

    ring = Ring(count)

    small = jnp.concatenate(
        [
            norm_gain1,
            norm_gain2,
            conv_weight.reshape(-1),
            conv_bias.reshape(-1),
            gate_bias.reshape(-1),
            decay_param.reshape(-1),
        ]
    )
    fold = 2 * block
    small_rows = -(-small.shape[0] // fold)
    small = jnp.pad(small, (0, small_rows * fold - small.shape[0])).reshape(small_rows, fold)
    gate_rows = heads * part_in
    packed = jnp.concatenate(
        [gate_weight[:, 0, 0].transpose(1, 2, 0, 3).reshape(gate_rows, fold), small], axis=0
    )
    packed = pad_rows(packed, -(-packed.shape[0] // 32) * 32)
    packed_all = ring.gather(packed)

    own_cols = lax.dynamic_slice_in_dim(in_weight[0], br * channels, channels, 1)
    far_cols = lax.ppermute(
        lax.dynamic_slice_in_dim(in_weight[0], (1 - br) * channels, channels, 1), "br", SWAP
    )
    w_in_own = jnp.concatenate(
        [jnp.where(br == 0, own_cols, far_cols), jnp.where(br == 0, far_cols, own_cols)], axis=1
    )
    w_in = ring.gather(w_in_own)
    w_out = ring.gather(out_weight[0, 0])
    w_mlp = ring.gather(mlp_in)
    w_down = ring.gather(mlp_down)

    doc_starts = jnp.cumsum(lengths) - lengths
    positions = jnp.arange(tokens + span, dtype=jnp.int32) + index * tokens - span
    doc_ext = jnp.sum((positions[:, None] >= doc_starts[None, 1:]).astype(jnp.int32), axis=1)
    lags = [
        (doc_ext[span - lag : span - lag + tokens] == doc_ext[span:]).astype(F32) for lag in range(taps)
    ]
    reset = jnp.any(positions[span:, None] == doc_starts[None, :], axis=1).astype(F32)
    mask = jnp.stack(lags + [reset], axis=1)

    small_all = jnp.stack([part[gate_rows : gate_rows + small_rows].reshape(-1) for part in packed_all])
    gain_one = small_all[:, :cols].astype(F32).reshape(1, width)
    gain_two = small_all[:, cols : 2 * cols].astype(F32).reshape(1, width)
    ring_index = jnp.stack(ring_of)
    place_hot = (ring_index[:, None] == jnp.arange(count)[None, :]).astype(BF16)
    chan = jnp.dot(place_hot, small_all[:, 2 * cols :], preferred_element_type=F32)
    chan = chan[:, : (taps + 4) * part_ch].reshape(count, taps + 4, part_ch)
    chan = chan.transpose(1, 0, 2).reshape(taps + 4, channels)
    conv = chan[: taps + 1]
    gate_bias_all = chan[taps + 1 : taps + 3].reshape(1, 2 * channels)
    decay_rate = chan[taps + 3 : taps + 4]
    rate = -DECAY_SCALE * jax.nn.softplus(-decay_rate)

    stacked = jnp.concatenate([part[:gate_rows] for part in packed_all], axis=0)
    row = jnp.arange(channels)
    row_head, row_in = row // block, row % block
    source = ring_index[row_in // part_in] * gate_rows + row_head * part_in + row_in % part_in
    row_hot = (source[:, None] == jnp.arange(channels)[None, :]).astype(BF16)
    wide_col = jnp.arange(2 * channels)
    wide_gate, wide_head, wide_out = (
        wide_col // channels,
        (wide_col % channels) // block,
        wide_col % block,
    )
    spread_hot = (jnp.arange(fold)[:, None] == (wide_gate * block + wide_out)[None, :]).astype(BF16)
    on_block = (row_head[:, None] == wide_head[None, :]).astype(BF16)
    compact = jnp.dot(row_hot, stacked, preferred_element_type=F32).astype(BF16)
    wide = jnp.dot(compact, spread_hot, preferred_element_type=F32).astype(BF16) * on_block

    x_in = to_ring(inputs)
    rstd_one = lax.rsqrt(jnp.mean(x_in * x_in, axis=1, keepdims=True) + NORM_EPS)
    h_one = (x_in * rstd_one * gain_one).astype(BF16)
    z = jnp.dot(h_one, jnp.concatenate(w_in, axis=0), preferred_element_type=F32).astype(BF16)

    forward_pairs = [(i, i + 1) for i in range(count - 1)]
    rim = lax.ppermute(z[tokens - 8 :, channels:], "seq", forward_pairs).astype(F32)
    unit, gates, loc, prod, last, total = forward_local(z, rim, mask, conv, wide, gate_bias_all, rate)
    enter = entering(last[:2], False)[None]
    act = jax.nn.gelu(z[:, :channels].astype(F32))
    mixed = (act * (loc + prod * enter)).astype(BF16)

    w_out_all = jnp.concatenate(w_out, axis=1)
    attn = group_sum(jnp.dot(mixed, w_out_all, preferred_element_type=F32).astype(BF16))
    resid = x_in + attn.astype(F32)
    rstd_two = lax.rsqrt(jnp.mean(resid * resid, axis=1, keepdims=True) + NORM_EPS)
    h_two = (resid * rstd_two * gain_two).astype(BF16)

    w_mlp_all = jnp.concatenate(w_mlp, axis=1)
    gate_up = jnp.einsum("td,gdf->gtf", h_two, w_mlp_all, preferred_element_type=F32)
    act_gate, act_slope = gelu_both(gate_up[0])
    hidden = (act_gate * gate_up[1]).astype(BF16)
    cot = to_ring(cotangent)
    d_mlp = cot.astype(BF16)

    def chunk(x, k):
        return x[:, k * cols : (k + 1) * cols]

    g_down = ring.scatter(
        lambda k: lax.dot_general(
            hidden, chunk(d_mlp, k), (((0,), (0,)), ((), ())), preferred_element_type=F32
        )
    )
    w_down_all = jnp.concatenate(w_down, axis=1)
    d_hidden = jnp.einsum("td,fd->tf", d_mlp, w_down_all, preferred_element_type=F32)
    d_gate_up = jnp.stack([d_hidden * gate_up[1] * act_slope, d_hidden * act_gate]).astype(BF16)
    g_mlp = ring.scatter(
        lambda k: jnp.einsum("td,gtf->gdf", chunk(h_two, k), d_gate_up, preferred_element_type=F32)
    )
    d_h_two = group_sum(
        jnp.einsum("gtf,gdf->td", d_gate_up, w_mlp_all, preferred_element_type=F32).astype(BF16)
    ).astype(F32)

    mlp_part = jnp.dot(hidden, w_down_all, preferred_element_type=F32).astype(BF16)
    per = width // 4 // cols

    def columns(x, b, c):
        first = (b * 2 + c) * per
        at = [(ring_place(first + j, count) - place) % count for j in range(per)]
        return jnp.concatenate([lax.dynamic_slice_in_dim(x, a * cols, cols, 1) for a in at], axis=1)

    mine = jnp.concatenate([columns(mlp_part, b, ch) for b in range(2)], axis=1)
    theirs = jnp.concatenate([columns(mlp_part, b, 1 - ch) for b in range(2)], axis=1)
    chip = mine.astype(F32) + lax.ppermute(theirs, "ch", SWAP).astype(F32)
    own = lax.dynamic_slice_in_dim(chip, br * (width // 4), width // 4, 1)
    far = lax.dynamic_slice_in_dim(chip, (1 - br) * (width // 4), width // 4, 1).astype(BF16)
    output = columns(resid, br, ch) + own + lax.ppermute(far, "br", SWAP).astype(F32)

    normed_two = resid * rstd_two
    g_gain_two = jnp.sum(d_h_two * normed_two, axis=0)
    d_normed = d_h_two * gain_two
    d_resid = cot + rstd_two * (d_normed - normed_two * jnp.mean(d_normed * normed_two, axis=1, keepdims=True))
    d_attn = d_resid.astype(BF16)
    g_out = ring.scatter(
        lambda k: lax.dot_general(
            mixed, chunk(d_attn, k), (((0,), (0,)), ((), ())), preferred_element_type=F32
        )
    )
    d_mixed = jnp.einsum("td,kd->tk", d_attn, w_out_all, preferred_element_type=F32)

    adj, tail, d_z_gate, head = adjoint_local(d_mixed, z, loc, prod, gates, mask, enter, rate)
    arrive = entering(head[:2], True)[None]
    d_z_rec, g_wide, sums, edge = backward_local(
        adj, tail, arrive, loc, prod, enter, gates, unit, mask, z, rim, conv, wide, rate
    )
    backward_pairs = [(i + 1, i) for i in range(count - 1)]
    from_next = lax.ppermute(edge[:8], "seq", backward_pairs)
    fixed = (edge[8:] + from_next).astype(BF16)
    d_z_rec = jnp.concatenate([d_z_rec[: tokens - 8], fixed], axis=0)
    d_z = jnp.concatenate([d_z_gate, d_z_rec], axis=1)

    w_in_all = jnp.concatenate(w_in, axis=0)
    g_in = ring.scatter(
        lambda k: lax.dot_general(
            chunk(h_one, k), d_z, (((0,), (0,)), ((), ())), preferred_element_type=F32
        )
    )
    keep_half = lax.dynamic_slice_in_dim(g_in, br * channels, channels, 1)
    send_half = lax.dynamic_slice_in_dim(g_in, (1 - br) * channels, channels, 1).astype(BF16)
    got_half = lax.ppermute(send_half, "br", SWAP).astype(F32)
    g_in = jnp.concatenate(
        [jnp.where(br == 0, keep_half, got_half), jnp.where(br == 0, got_half, keep_half)], axis=1
    )
    d_h_part = lax.dot_general(d_z, w_in_all, (((1,), (1,)), ((), ())), preferred_element_type=F32)
    d_h_one = group_sum(d_h_part.astype(BF16)).astype(F32)
    normed_one = x_in * rstd_one
    g_gain_one = jnp.sum(d_h_one * normed_one, axis=0)
    d_normed = d_h_one * gain_one
    inputs_grad = from_ring(
        d_resid + rstd_one * (d_normed - normed_one * jnp.mean(d_normed * normed_one, axis=1, keepdims=True))
    )

    g_compact = lax.dot_general(
        (g_wide * on_block.astype(F32)).astype(BF16),
        spread_hot,
        (((1,), (1,)), ((), ())),
        preferred_element_type=F32,
    ).astype(BF16)
    g_gates = lax.dot_general(row_hot, g_compact, (((0,), (0,)), ((), ())), preferred_element_type=F32)
    g_decay = sums[0:1] * -DECAY_SCALE * -jax.nn.sigmoid(-decay_rate)
    g_chan = jnp.concatenate([sums[4 : 4 + taps], sums[3:4], sums[1:3], g_decay, total[0:1]], axis=0)
    g_chan = g_chan.reshape(taps + 5, count, part_ch).transpose(1, 0, 2).reshape(count, -1)
    g_chan = lax.dot_general(
        place_hot.astype(F32), g_chan, (((0,), (0,)), ((), ())), precision=lax.Precision.HIGHEST
    )
    g_small = jnp.concatenate(
        [g_gain_one.reshape(count, cols), g_gain_two.reshape(count, cols), g_chan], axis=1
    )
    g_rows = -(-g_small.shape[1] // fold)
    g_small = jnp.pad(g_small, ((0, 0), (0, g_rows * fold - g_small.shape[1]))).reshape(count, g_rows, fold)
    g_packed = jnp.concatenate([g_gates.reshape(count, gate_rows, fold), g_small], axis=1)
    total_rows = -(-g_packed.shape[1] // 32) * 32
    g_packed = jnp.pad(g_packed, ((0, 0), (0, total_rows - g_packed.shape[1]), (0, 0)))
    g_own = ring.scatter(lambda k: g_packed[k])
    g_gate_w = g_own[:gate_rows].reshape(heads, part_in, 2, block).transpose(2, 0, 1, 3)[:, None, None]
    g_flat = g_own[gate_rows : gate_rows + g_rows].reshape(-1)
    g_gain_one, g_gain_two = g_flat[:cols], g_flat[cols : 2 * cols]
    g_chan = g_flat[2 * cols : 2 * cols + (taps + 5) * part_ch].reshape(taps + 5, part_ch)
    return (
        output,
        inputs_grad,
        g_gain_one,
        g_in[None],
        g_chan[:taps][:, None, None],
        g_chan[taps][None, None],
        g_gate_w,
        g_chan[taps + 1 : taps + 3][:, None, None],
        g_chan[taps + 3][None, None],
        g_out[None, None],
        g_gain_two,
        g_mlp,
        g_down,
        g_chan[taps + 4][None, None] / (tokens * count),
    )


def solution(mesh):
    placed = (
        P("seq", None),
        P(),
        P("seq"),
        P("br", "seq", "ch"),
        P(None, "ch", "br", "seq"),
        P("ch", "br", "seq"),
        P(None, "ch", "br", None, "seq", None),
        P(None, "ch", "br", "seq"),
        P("ch", "br", "seq"),
        P("ch", "br", None, "seq"),
        P("seq"),
        P(None, "seq", ("br", "ch")),
        P(("br", "ch"), "seq"),
        P("seq", None),
    )
    return jax.shard_map(
        per_device,
        mesh=mesh,
        in_specs=placed,
        out_specs=(
            P("seq", ("br", "ch")),
            P("seq", None),
            P("seq"),
            P("br", "seq", "ch"),
            P(None, "ch", "br", "seq"),
            P("ch", "br", "seq"),
            P(None, "ch", "br", None, "seq", None),
            P(None, "ch", "br", "seq"),
            P("ch", "br", "seq"),
            P("ch", "br", None, "seq"),
            P("seq"),
            P(None, "seq", ("br", "ch")),
            P(("br", "ch"), "seq"),
            P("ch", "br", "seq"),
        ),
        check_vma=False,
    )
```

time: 3240 us -> 861 us (0.27)
  waiting for transfers between devices: 1790 us -> 286 us
  local copies, waits for them, and re-layouts: 638 us -> 126 us
  blocking collectives: 339 us -> 0 us
  other arithmetic: 241 us -> 99.6 us
  starting transfers between devices: 7.76 us -> 113 us
  Pallas kernels: 0 us -> 47.9 us
    reduce_scatter x5 -> x0, waiting for transfers between devices: 888 us -> none  [the longest x1 348 us: per_device(): lax.psum_scatter(g_mlp, 'seq', scatter_dimension=1, tiled=True)]
    psum x3 -> x0, waiting for transfers between devices: 377 us -> none  [the longest x1 152 us: per_device(): lax.psum(jnp.einsum('tq,dq->td', d_own, w_in, preferred_element_type=jnp....]
    slice x145 -> x49, local copies, waits for them, and re-layouts: 340 us -> 7.75 us  [the longest x10 2.5 us: gather(): far = [self.hop(ahead[:cut], 1), self.hop(behind[cut:], -1)]]
    ppermute x2 -> x95, waiting for transfers between devices: 3.27 us -> 278 us  [the longest x80 246 us: hop(): got = lax.ppermute(x, 'seq', self.pairs[way])]
    all_gather x4 -> x0, waiting for transfers between devices: 264 us -> none  [the longest x1 169 us: per_device(): lax.all_gather(mlp_in, 'seq', axis=1, tiled=True)]
    all_gather x9 -> x0, blocking collectives: 262 us -> none  [the longest x4 122 us: entering_2(): everything = jax.tree.map(lambda part: lax.all_gather(part, axis), x)]
    unnamed x24 -> x0, waiting for transfers between devices: 257 us -> none
    pad x72 -> x1, local copies, waits for them, and re-layouts: 154 us -> 0.01 us  [per_device(): jnp.pad(small, (0, small_rows * fold - small.shape[0]))]
  transfers between devices with their start and end apart: 21 -> 97, of which waited for: 16 -> 51; matrix products, arithmetic and copies ran while one was open for 19% -> 35% of each run, Pallas kernels for 0% -> 6%
where the time goes in v1:
time: 861 us; the launch traced here: 851 us
  waiting for transfers between devices  286 us (33%)
  matrix products  170 us (20%)
  local copies, waits for them, and re-layouts  126 us (15%)
  starting transfers between devices  113 us (13%)
  other arithmetic  99.6 us (12%)
  Pallas kernels  47.9 us (6%)
    ppermute x80, waiting for transfers between devices, hop(): got = lax.ppermute(x, 'seq', self.pairs[way])  246 us
    ppermute x80, starting transfers between devices, hop(): got = lax.ppermute(x, 'seq', self.pairs[way])  94.8 us
    unnamed x242, local copies, waits for them, and re-layouts  88.4 us
    dot_general x8, matrix products, per_device(): jnp.einsum('td,gtf->gdf', chunk(h_two, k), d_gate_up, preferred_element_t...  27 us
    pallas_call x1, Pallas kernels, backward_local(): pl.pallas_call(backward_kernel, grid=(tokens // rows,), in_specs=[time(ch...  22.8 us
    dot_general x8, matrix products, per_device(): lax.dot_general(chunk(h_one, k), d_z, (((0,), (0,)), ((), ())), preferred...  18.2 us
    dot_general x1, matrix products, per_device(): jnp.einsum('td,gdf->gtf', h_two, w_mlp_all, preferred_element_type=F32)  18.2 us
    dot_general x1, matrix products, per_device(): jnp.einsum('td,fd->tf', d_mlp, w_down_all, preferred_element_type=F32)  17.9 us
  transfers between devices with their start and end apart: 97, of which 51 were waited for; matrix products, arithmetic and copies ran while one was open for 35% of the time, Pallas kernels for 6%

profile of v1, /device:TPU:0, one launch (start us, length us, event | category | flops | bytes accessed | tf_op | source)
XLA Modules:
  0.0 850.8 jit_solution(10470790613021957695)
XLA Ops:
  64.9 6.2 multiply_convert_fusion.1
  83.2 9.5 %collective-permute-done.13 = bf16[256,1280]{1,0:T(8,128)(2,1)S(1)} collective-permute-done((bf16[256,1280]{1,0:T(8,128)(2,1)S(1)}, bf16[256,1280]{1,0:T(8,128)(2,1)S(1)}, u32[]{:S(2)}, u32[]{:S(2)}) %collective-permute-start.13) | collective-permute-done | bytes 655392 | tf_op jit(solution)/shard_map/ppermute | solution.py:45
  123.6 9.3 %convolution_convert_fusion.1.z_ref.zg_ref.z0_ref = bf16[1024,1280]{1,0:T(8,128)(2,1)} fusion(bf16[1024,2048]{1,0:T(8,128)(2,1)S(1)} %copy-done.21, bf16[2048,1280]{1,0:T(8,128)(2,1)} %constant_dynamic-update-slice_fusion), kind=kOutput, calls=%fused_computation.59 | convolution fusion | flops 5370019840 | bytes 12058624 | tf_op jit(solution)/shard_map/dot_general | solution.py:525
  140.9 14.3 %shard_map.254 = (bf16[1024,640]{1,0:T(8,128)(2,1)S(1)}, f32[1024,1280]{1,0:T(8,128)}, f32[1024,640]{1,0:T(8,128)S(1)}, f32[1024,640]{1,0:T(8,128)}, f32[8,640]{1,0:T(8,128)S(1)}, /*index=5*/f32[8,640]{1,0:T(8,128)S(1)}) custom-call(bf16[1024,1280]{1,0:T(8,128)(2,1)} %convolution_convert_fusion.1.z_ref.zg_ref.z0_ref, ...), custom_call_target="tpu_custom_call" | custom-call | tf_op jit(solution)/shard_map/pallas_call | solution.py:329
  205.5 7.1 collective-permute-done.32
  225.4 21.7 %collective-permute-done.33 = bf16[2,256,1536]{1,2,0:T(8,128)(2,1)} collective-permute-done((bf16[2,256,1536]{1,2,0:T(8,128)(2,1)}, bf16[2,256,1536]{1,2,0:T(8,128)(2,1)}, u32[]{:S(2)}, u32[]{:S(2)}) %collective-permute-start.33) | collective-permute-done | bytes 1572896 | tf_op jit(solution)/shard_map/ppermute | solution.py:45
  264.7 6.2 convert_element_type.409
  273.8 6.9 collective-permute-done.34
  294.0 8.4 collective-permute-done.35
  302.4 14.1 %collective-permute-done.40 = bf16[1536,256]{1,0:T(8,128)(2,1)S(1)} collective-permute-done((bf16[1536,256]{1,0:T(8,128)(2,1)S(1)}, bf16[1536,256]{1,0:T(8,128)(2,1)S(1)}, u32[]{:S(2)}, u32[]{:S(2)}) %collective-permute-start.40) | collective-permute-done | bytes 786464 | tf_op jit(solution)/shard_map/ppermute | solution.py:45
  326.3 7.9 collective-permute-done.41
  354.6 18.2 %convolution_bitcast_fusion = f32[2,1024,1536]{1,2,0:T(8,128)} fusion(bf16[2,2048,1536]{1,2,0:T(8,128)(2,1)} %copy-done.51, bf16[1024,2048]{1,0:T(8,128)(2,1)S(1)} %multiply_convert_fusion), kind=kOutput, calls=%fused_computation.24 | convolution fusion | flops 12884901888 | bytes 29360128 | tf_op jit(solution)/shard_map/td,gdf->gtf/dot_general | solution.py:541
  377.7 17.9 %fusion.25 = (bf16[1,1024,1536]{1,2,0:T(8,128)(2,1)}, bf16[1,1024,1536]{1,2,0:T(8,128)(2,1)}, bf16[1024,1536]{0,1:T(8,128)(2,1)S(1)}) fusion(f32[2,1024,1536]{1,2,0:T(8,128)} %convolution_bitcast_fusion, bf16[1024,2048]{1,0:T(8,128)(2,1)S(1)} %copy-done.24, bf16[1536,2048]{1,0:T(8,128)(2,1)} %constant_dynamic-update-slice_fusion.31), kind=kOutput, calls=%fused_computation.77 | convolution fusion | flops 6480199680 | bytes 32505856 | tf_op jit(solution)/shard_map/td,fd->tf/dot_general | solution.py:556
  407.2 17.6 %bitcast_convert_fusion = bf16[1024,2048]{1,0:T(8,128)(2,1)S(1)} fusion(bf16[2,2048,1536]{1,2,0:T(8,128)(2,1)} %copy-done.51, bf16[1,1024,1536]{1,2,0:T(8,128)(2,1)} %get-tuple-element.274, bf16[1,1024,1536]{1,2,0:T(8,128)(2,1)} %get-tuple-element.273), kind=kOutput, calls=%fused_computation.18 | convolution fusion | flops 12890144768 | bytes 23068672 | tf_op jit(solution)/shard_map/gtf,gdf->td/dot_general | solution.py:562
  424.8 10.0 %convolution_convert_fusion = bf16[1024,2048]{1,0:T(8,128)(2,1)S(1)} fusion(bf16[1024,1536]{0,1:T(8,128)(2,1)} %copy-done.76, bf16[1536,2048]{1,0:T(8,128)(2,1)} %constant_dynamic-update-slice_fusion.31), kind=kOutput, calls=%fused_computation.58 | convolution fusion | flops 6444548096 | bytes 13631488 | tf_op jit(solution)/shard_map/dot_general | solution.py:565
  445.9 13.8 %collective-permute-done.75 = bf16[1536,256]{1,0:T(8,128)(2,1)S(1)} collective-permute-done((bf16[1536,256]{1,0:T(8,128)(2,1)S(1)}, bf16[1536,256]{1,0:T(8,128)(2,1)S(1)}, u32[]{:S(2)}, u32[]{:S(2)}) %collective-permute-start.75) | collective-permute-done | bytes 786464 | tf_op jit(solution)/shard_map/ppermute | solution.py:45
  465.8 11.1 %collective-permute-done.76 = bf16[1536,256]{1,0:T(8,128)(2,1)S(1)} collective-permute-done((bf16[1536,256]{1,0:T(8,128)(2,1)S(1)}, bf16[1536,256]{1,0:T(8,128)(2,1)S(1)}, u32[]{:S(2)}, u32[]{:S(2)}) %collective-permute-start.76) | collective-permute-done | bytes 786464 | tf_op jit(solution)/shard_map/ppermute | solution.py:45
  485.3 10.4 %collective-permute-done.77 = bf16[1,256,1536]{1,2,0:T(8,128)(2,1)S(1)} collective-permute-done((bf16[1,256,1536]{1,2,0:T(8,128)(2,1)S(1)}, bf16[1,256,1536]{1,2,0:T(8,128)(2,1)S(1)}, u32[]{:S(2)}, u32[]{:S(2)}) %collective-permute-start.77) | collective-permute-done | bytes 786464 | tf_op jit(solution)/shard_map/ppermute | solution.py:45
  498.0 11.6 %collective-permute-done.78 = bf16[1536,256]{1,0:T(8,128)(2,1)S(1)} collective-permute-done((bf16[1536,256]{1,0:T(8,128)(2,1)S(1)}, bf16[1536,256]{1,0:T(8,128)(2,1)S(1)}, u32[]{:S(2)}, u32[]{:S(2)}) %collective-permute-start.78) | collective-permute-done | bytes 786464 | tf_op jit(solution)/shard_map/ppermute | solution.py:45
  510.1 9.9 %collective-permute-done.57 = bf16[1,256,1536]{1,2,0:T(8,128)(2,1)S(1)} collective-permute-done((bf16[1,256,1536]{1,2,0:T(8,128)(2,1)S(1)}, bf16[1,256,1536]{1,2,0:T(8,128)(2,1)S(1)}, u32[]{:S(2)}, u32[]{:S(2)}) %collective-permute-start.57) | collective-permute-done | bytes 786464 | tf_op jit(solution)/shard_map/ppermute | solution.py:45
  530.4 10.4 %collective-permute-done.79 = bf16[2,256,1536]{1,2,0:T(8,128)(2,1)} collective-permute-done((bf16[2,256,1536]{1,2,0:T(8,128)(2,1)}, bf16[2,256,1536]{1,2,0:T(8,128)(2,1)}, u32[]{:S(2)}, u32[]{:S(2)}) %collective-permute-start.79) | collective-permute-done | bytes 1572896 | tf_op jit(solution)/shard_map/ppermute | solution.py:45
  544.9 12.3 %collective-permute-done.59 = bf16[2,256,1536]{1,2,0:T(8,128)(2,1)} collective-permute-done((bf16[2,256,1536]{1,2,0:T(8,128)(2,1)}, bf16[2,256,1536]{1,2,0:T(8,128)(2,1)}, u32[]{:S(2)}, u32[]{:S(2)}) %collective-permute-start.59) | collective-permute-done | bytes 1572896 | tf_op jit(solution)/shard_map/ppermute | solution.py:45
  561.6 12.2 %collective-permute-done.48 = bf16[512,2048]{1,0:T(8,128)(2,1)} collective-permute-done((bf16[512,2048]{1,0:T(8,128)(2,1)}, bf16[512,2048]{1,0:T(8,128)(2,1)}, u32[]{:S(2)}, u32[]{:S(2)}) %collective-permute-start.48) | collective-permute-done | bytes 2097184 | tf_op jit(solution)/shard_map/ppermute | solution.py:90
  581.6 12.2 %collective-permute-done.46 = bf16[1024,512]{1,0:T(8,128)(2,1)S(1)} collective-permute-done((bf16[1024,512]{1,0:T(8,128)(2,1)S(1)}, bf16[1024,512]{1,0:T(8,128)(2,1)S(1)}, u32[]{:S(2)}, u32[]{:S(2)}) %collective-permute-start.46) | collective-permute-done | bytes 1048608 | tf_op jit(solution)/shard_map/ppermute | solution.py:578
  611.7 7.3 fusion.212
  624.6 7.0 fusion.220.dmix_ref
  631.6 10.9 %shard_map.255 = (f32[1024,640]{1,0:T(8,128)S(1)}, f32[1024,640]{1,0:T(8,128)}, bf16[1024,640]{1,0:T(8,128)(2,1)S(1)}, f32[8,640]{1,0:T(8,128)S(1)}) custom-call(f32[1024,640]{1,0:T(8,128)} %fusion.220.dmix_ref, bf16[1024,1280]{1,0:T(8,128)(2,1)} %convolution_convert_fusion.1.z_ref.zg_ref.z0_ref, f32[1024,640]{1,0:T(8,128)} %copy-done, ...), custom_call_target="tpu_custom_call" | custom-call | tf_op jit(solution)/shard_map/pallas_call | solution.py:353
  657.3 22.8 %shard_map.256 = (bf16[1024,640]{1,0:T(8,128)(2,1)S(1)}, f32[640,1280]{1,0:T(8,128)}, f32[16,640]{1,0:T(8,128)S(1)}, f32[16,640]{1,0:T(8,128)S(1)}) custom-call(f32[1024,640]{1,0:T(8,128)} %copy-done.3, f32[1024,640]{1,0:T(8,128)} %get-tuple-element.146.tail_ref, f32[1,640]{1,0:T(1,128)S(1)} %broadcast_select_fusion.13.arrive_ref, f32[1024,640]{1,0:T(8,128)} %copy-done, ...), custom_call_target="tpu_custom_call" | custom-call | tf_op jit(solution)/shard_map/pallas_call | solution.py:380
  687.8 8.8 %convolution_convert_fusion.2 = bf16[1024,2048]{1,0:T(8,128)(2,1)S(1)} fusion(bf16[2048,1280]{1,0:T(8,128)(2,1)} %constant_dynamic-update-slice_fusion, bf16[8,640]{1,0:T(8,128)(2,1)S(1)} %add_convert_fusion.22, bf16[1016,640]{1,0:T(8,128)(2,1)S(1)} %slice.635, bf16[1024,640]{1,0:T(8,128)(2,1)S(1)} %copy-done.11), kind=kOutput, calls=%fused_computation.60 | convolution fusion | flops 5378670592 | bytes 12058624 | tf_op jit(solution)/shard_map/dot_general | solution.py:615
  800.6 6.8 collective-permute-done.94
  811.2 7.0 fusion.11
  820.9 9.6 %fusion.6 = f32[1024,2048]{1,0:T(8,128)S(1)} fusion(f32[1024,2048]{1,0:T(8,128)} %get-tuple-element.270, f32[1024,2048]{1,0:T(8,128)} %dynamic-slice_dynamic-update-slice_fusion.16, f32[1024]{0:T(1024)S(1)} %broadcast_multiply_fusion, f32[2048]{0:T(1024)S(1)} %bitcast.485, f32[1024]{0:T(1024)S(1)} %copy-done.56, bf16[512,2048]{1,0:T(8,128)(2,1)S(1)} %copy-done.14, ...), kind=kLoop, calls=%fused_computation.12 | loop fusion | flops 20971520 | bytes 29376512 | tf_op jit(solution)/shard_map/add | solution.py:621
  (644 shorter events, 483.1 us)
Async XLA Ops:
  6.1 40.8 %collective-permute-start.4 = (bf16[96,320]{1,0:T(8,128)(2,1)S(1)}, bf16[96,320]{1,0:T(8,128)(2,1)S(1)}, u32[]{:S(2)}, u32[]{:S(2)}) collective-permute-start(bf16[96,320]{1,0:T(8,128)(2,1)S(1)} %fusion.144), channel_id=1, source_target_pairs={{0,4},{4,8},{8,12},{12,14},{14,10},{10,6},{6,2},{2,0},{1,5},{5,9},... | collective-permute-start | bytes 184328 | tf_op jit(solution)/shard_map/ppermute | solution.py:45
  9.2 39.3 %collective-permute-start = (bf16[96,320]{1,0:T(8,128)(2,1)S(1)}, bf16[96,320]{1,0:T(8,128)(2,1)S(1)}, u32[]{:S(2)}, u32[]{:S(2)}) collective-permute-start(bf16[96,320]{1,0:T(8,128)(2,1)S(1)} %fusion.144), channel_id=1, source_target_pairs={{4,0},{8,4},{12,8},{14,12},{10,14},{6,10},{2,6},{0,2},{5,1},{9,5},... | collective-permute-start | bytes 184328 | tf_op jit(solution)/shard_map/ppermute | solution.py:45
  10.2 51.6 %collective-permute-start.7 = (bf16[256,640]{1,0:T(8,128)(2,1)S(1)}, bf16[256,640]{1,0:T(8,128)(2,1)S(1)}, u32[]{:S(2)}, u32[]{:S(2)}) collective-permute-start(bf16[256,640]{1,0:T(8,128)(2,1)S(1)} %dynamic-slice_bitcast_fusion), channel_id=1, source_target_pairs={{0,16},{16,0},{1,17},{17,1},{2,18},{18,2},{3,19},{19,3},{4,20},{20... | collective-permute-start | bytes 983048 | tf_op jit(solution)/shard_map/ppermute | solution.py:473
  135.9 32.9 %collective-permute-start.22 = (bf16[640,256]{1,0:T(8,128)(2,1)}, bf16[640,256]{1,0:T(8,128)(2,1)}, u32[]{:S(2)}, u32[]{:S(2)}) collective-permute-start(bf16[640,256]{1,0:T(8,128)(2,1)} %collective-permute-done.21), channel_id=1, source_target_pairs={{0,4},{4,8},{8,12},{12,14},{14,10},{10,6},{6,2},{2,0},{1,5},{5,9},... | collective-permute-start | bytes 983048 | tf_op jit(solution)/shard_map/ppermute | solution.py:45
  137.8 31.4 %collective-permute-start.19 = (bf16[640,256]{1,0:T(8,128)(2,1)}, bf16[640,256]{1,0:T(8,128)(2,1)}, u32[]{:S(2)}, u32[]{:S(2)}) collective-permute-start(bf16[640,256]{1,0:T(8,128)(2,1)} %collective-permute-done.18), channel_id=1, source_target_pairs={{4,0},{8,4},{12,8},{14,12},{10,14},{6,10},{2,6},{0,2},{5,1},{9,5},... | collective-permute-start | bytes 983048 | tf_op jit(solution)/shard_map/ppermute | solution.py:45
  212.6 34.6 %collective-permute-start.33 = (bf16[2,256,1536]{1,2,0:T(8,128)(2,1)}, bf16[2,256,1536]{1,2,0:T(8,128)(2,1)}, u32[]{:S(2)}, u32[]{:S(2)}) collective-permute-start(bf16[2,256,1536]{1,2,0:T(8,128)(2,1)} %collective-permute-done.32), channel_id=1, source_target_pairs={{0,4},{4,8},{8,12},{12,14},{14,10},{10,6},{6,2},{2,0},{1,5},{5,9},... | collective-permute-start | bytes 4718600 | tf_op jit(solution)/shard_map/ppermute | solution.py:45
  214.9 34.6 %collective-permute-start.30 = (bf16[2,256,1536]{1,2,0:T(8,128)(2,1)}, bf16[2,256,1536]{1,2,0:T(8,128)(2,1)}, u32[]{:S(2)}, u32[]{:S(2)}) collective-permute-start(bf16[2,256,1536]{1,2,0:T(8,128)(2,1)} %collective-permute-done.29), channel_id=1, source_target_pairs={{4,0},{8,4},{12,8},{14,12},{10,14},{6,10},{2,6},{0,2},{5,1},{9,5},... | collective-permute-start | bytes 4718600 | tf_op jit(solution)/shard_map/ppermute | solution.py:45
  221.0 66.6 %collective-permute-start.27 = (bf16[512,2048]{1,0:T(8,128)(2,1)}, bf16[512,2048]{1,0:T(8,128)(2,1)}, u32[]{:S(2)}, u32[]{:S(2)}) collective-permute-start(bf16[512,2048]{1,0:T(8,128)(2,1)} %add_convert_fusion.5), channel_id=1, source_target_pairs={{0,16},{16,0},{1,17},{17,1},{2,18},{18,2},{3,19},{19,3},{4,20},{20... | collective-permute-start | bytes 6291464 | tf_op jit(solution)/shard_map/ppermute | solution.py:90
  247.2 33.5 %collective-permute-start.34 = (bf16[2,256,1536]{1,2,0:T(8,128)(2,1)}, bf16[2,256,1536]{1,2,0:T(8,128)(2,1)}, u32[]{:S(2)}, u32[]{:S(2)}) collective-permute-start(bf16[2,256,1536]{1,2,0:T(8,128)(2,1)} %collective-permute-done.33), channel_id=1, source_target_pairs={{0,4},{4,8},{8,12},{12,14},{14,10},{10,6},{6,2},{2,0},{1,5},{5,9},... | collective-permute-start | bytes 4718600 | tf_op jit(solution)/shard_map/ppermute | solution.py:45
  249.5 33.5 %collective-permute-start.31 = (bf16[2,256,1536]{1,2,0:T(8,128)(2,1)}, bf16[2,256,1536]{1,2,0:T(8,128)(2,1)}, u32[]{:S(2)}, u32[]{:S(2)}) collective-permute-start(bf16[2,256,1536]{1,2,0:T(8,128)(2,1)} %collective-permute-done.30), channel_id=1, source_target_pairs={{4,0},{8,4},{12,8},{14,12},{10,14},{6,10},{2,6},{0,2},{5,1},{9,5},... | collective-permute-start | bytes 4718600 | tf_op jit(solution)/shard_map/ppermute | solution.py:45
  282.3 34.2 %collective-permute-start.40 = (bf16[1536,256]{1,0:T(8,128)(2,1)S(1)}, bf16[1536,256]{1,0:T(8,128)(2,1)S(1)}, u32[]{:S(2)}, u32[]{:S(2)}) collective-permute-start(bf16[1536,256]{1,0:T(8,128)(2,1)S(1)} %copy-done.39), channel_id=1, source_target_pairs={{0,4},{4,8},{8,12},{12,14},{14,10},{10,6},{6,2},{2,0},{1,5},{5,9},... | collective-permute-start | bytes 2359304 | tf_op jit(solution)/shard_map/ppermute | solution.py:45
  284.2 32.6 %collective-permute-start.36 = (bf16[1,256,1536]{1,2,0:T(8,128)(2,1)S(1)}, bf16[1,256,1536]{1,2,0:T(8,128)(2,1)S(1)}, u32[]{:S(2)}, u32[]{:S(2)}) collective-permute-start(bf16[1,256,1536]{1,2,0:T(8,128)(2,1)S(1)} %slice.784), channel_id=1, source_target_pairs={{4,0},{8,4},{12,8},{14,12},{10,14},{6,10},{2,6},{0,2},{5,1},{9,5},... | collective-permute-start | bytes 2359304 | tf_op jit(solution)/shard_map/ppermute | solution.py:45
  285.5 33.3 %collective-permute-start.37 = (bf16[1536,256]{1,0:T(8,128)(2,1)S(1)}, bf16[1536,256]{1,0:T(8,128)(2,1)S(1)}, u32[]{:S(2)}, u32[]{:S(2)}) collective-permute-start(bf16[1536,256]{1,0:T(8,128)(2,1)S(1)} %copy-done.39), channel_id=1, source_target_pairs={{4,0},{8,4},{12,8},{14,12},{10,14},{6,10},{2,6},{0,2},{5,1},{9,5},... | collective-permute-start | bytes 2359304 | tf_op jit(solution)/shard_map/ppermute | solution.py:45
  290.6 48.7 %collective-permute-start.28 = (bf16[512,2048]{1,0:T(8,128)(2,1)S(1)}, bf16[512,2048]{1,0:T(8,128)(2,1)S(1)}, u32[]{:S(2)}, u32[]{:S(2)}) collective-permute-start(bf16[512,2048]{1,0:T(8,128)(2,1)S(1)} %add_convert_fusion.4), channel_id=1, source_target_pairs={{0,1},{1,0},{2,3},{3,2},{4,5},{5,4},{6,7},{7,6},{8,9},{9,8},{10,11... | collective-permute-start | bytes 6291464 | tf_op jit(solution)/shard_map/ppermute | solution.py:91
  461.9 60.9 %collective-permute-start.47 = (bf16[512,2048]{1,0:T(8,128)(2,1)S(1)}, bf16[512,2048]{1,0:T(8,128)(2,1)S(1)}, u32[]{:S(2)}, u32[]{:S(2)}) collective-permute-start(bf16[512,2048]{1,0:T(8,128)(2,1)S(1)} %constant_dynamic-slice_fusion.1), channel_id=1, source_target_pairs={{0,1},{1,0},{2,3},{3,2},{4,5},{5,4},{6,7},{7,6},{8,9},{9,8},{10,11... | collective-permute-start | bytes 6291464 | tf_op jit(solution)/shard_map/ppermute | solution.py:89
  479.4 46.3 %collective-permute-start.45 = (bf16[1024,1024]{1,0:T(8,128)(2,1)}, bf16[1024,1024]{1,0:T(8,128)(2,1)}, u32[]{:S(2)}, u32[]{:S(2)}) collective-permute-start(bf16[1024,1024]{1,0:T(8,128)(2,1)} %pad_maximum_fusion.3), channel_id=1, source_target_pairs={{0,1},{1,0},{2,3},{3,2},{4,5},{5,4},{6,7},{7,6},{8,9},{9,8},{10,11... | collective-permute-start | bytes 6291464 | tf_op jit(solution)/shard_map/ppermute | solution.py:575
  480.4 29.1 %collective-permute-start.78 = (bf16[1536,256]{1,0:T(8,128)(2,1)S(1)}, bf16[1536,256]{1,0:T(8,128)(2,1)S(1)}, u32[]{:S(2)}, u32[]{:S(2)}) collective-permute-start(bf16[1536,256]{1,0:T(8,128)(2,1)S(1)} %add_convert_fusion.10), channel_id=1, source_target_pairs={{4,0},{8,4},{12,8},{14,12},{10,14},{6,10},{2,6},{0,2},{5,1},{9,5},... | collective-permute-start | bytes 2359304 | tf_op jit(solution)/shard_map/ppermute | solution.py:45
  484.0 37.6 %collective-permute-start.58 = (bf16[1536,256]{1,0:T(8,128)(2,1)S(1)}, bf16[1536,256]{1,0:T(8,128)(2,1)S(1)}, u32[]{:S(2)}, u32[]{:S(2)}) collective-permute-start(bf16[1536,256]{1,0:T(8,128)(2,1)S(1)} %add_convert_fusion.12), channel_id=1, source_target_pairs={{0,4},{4,8},{8,12},{12,14},{14,10},{10,6},{6,2},{2,0},{1,5},{5,9},... | collective-permute-start | bytes 2359304 | tf_op jit(solution)/shard_map/ppermute | solution.py:45
  509.6 31.2 %collective-permute-start.79 = (bf16[2,256,1536]{1,2,0:T(8,128)(2,1)}, bf16[2,256,1536]{1,2,0:T(8,128)(2,1)}, u32[]{:S(2)}, u32[]{:S(2)}) collective-permute-start(bf16[2,256,1536]{1,2,0:T(8,128)(2,1)} %pad_maximum_fusion.5), channel_id=1, source_target_pairs={{4,0},{8,4},{12,8},{14,12},{10,14},{6,10},{2,6},{0,2},{5,1},{9,5},... | collective-permute-start | bytes 4718600 | tf_op jit(solution)/shard_map/ppermute | solution.py:45
  521.6 35.6 %collective-permute-start.59 = (bf16[2,256,1536]{1,2,0:T(8,128)(2,1)}, bf16[2,256,1536]{1,2,0:T(8,128)(2,1)}, u32[]{:S(2)}, u32[]{:S(2)}) collective-permute-start(bf16[2,256,1536]{1,2,0:T(8,128)(2,1)} %pad_maximum_fusion.4), channel_id=1, source_target_pairs={{0,4},{4,8},{8,12},{12,14},{14,10},{10,6},{6,2},{2,0},{1,5},{5,9},... | collective-permute-start | bytes 4718600 | tf_op jit(solution)/shard_map/ppermute | solution.py:45
  525.0 48.9 %collective-permute-start.48 = (bf16[512,2048]{1,0:T(8,128)(2,1)}, bf16[512,2048]{1,0:T(8,128)(2,1)}, u32[]{:S(2)}, u32[]{:S(2)}) collective-permute-start(bf16[512,2048]{1,0:T(8,128)(2,1)} %add_convert_fusion.3), channel_id=1, source_target_pairs={{0,16},{16,0},{1,17},{17,1},{2,18},{18,2},{3,19},{19,3},{4,20},{20... | collective-permute-start | bytes 6291464 | tf_op jit(solution)/shard_map/ppermute | solution.py:90
  528.8 65.0 %collective-permute-start.46 = (bf16[1024,512]{1,0:T(8,128)(2,1)S(1)}, bf16[1024,512]{1,0:T(8,128)(2,1)S(1)}, u32[]{:S(2)}, u32[]{:S(2)}) collective-permute-start(bf16[1024,512]{1,0:T(8,128)(2,1)S(1)} %dynamic-slice_convert_fusion), channel_id=1, source_target_pairs={{0,16},{16,0},{1,17},{17,1},{2,18},{18,2},{3,19},{19,3},{4,20},{20... | collective-permute-start | bytes 3145736 | tf_op jit(solution)/shard_map/ppermute | solution.py:578
  544.1 51.6 %collective-permute-start.80 = (bf16[2,256,1536]{1,2,0:T(8,128)(2,1)S(1)}, bf16[2,256,1536]{1,2,0:T(8,128)(2,1)S(1)}, u32[]{:S(2)}, u32[]{:S(2)}) collective-permute-start(bf16[2,256,1536]{1,2,0:T(8,128)(2,1)S(1)} %add_convert_fusion.7), channel_id=1, source_target_pairs={{4,0},{8,4},{12,8},{14,12},{10,14},{6,10},{2,6},{0,2},{5,1},{9,5},... | collective-permute-start | bytes 4718600 | tf_op jit(solution)/shard_map/ppermute | solution.py:45
  560.4 42.2 %collective-permute-start.60 = (bf16[2,256,1536]{1,2,0:T(8,128)(2,1)S(1)}, bf16[2,256,1536]{1,2,0:T(8,128)(2,1)S(1)}, u32[]{:S(2)}, u32[]{:S(2)}) collective-permute-start(bf16[2,256,1536]{1,2,0:T(8,128)(2,1)S(1)} %add_convert_fusion.9), channel_id=1, source_target_pairs={{0,4},{4,8},{8,12},{12,14},{14,10},{10,6},{6,2},{2,0},{1,5},{5,9},... | collective-permute-start | bytes 4718600 | tf_op jit(solution)/shard_map/ppermute | solution.py:45
  577.1 29.7 %collective-permute-start.49 = (bf16[512,2048]{1,0:T(8,128)(2,1)S(1)}, bf16[512,2048]{1,0:T(8,128)(2,1)S(1)}, u32[]{:S(2)}, u32[]{:S(2)}) collective-permute-start(bf16[512,2048]{1,0:T(8,128)(2,1)S(1)} %add_convert_fusion.2), channel_id=1, source_target_pairs={{0,1},{1,0},{2,3},{3,2},{4,5},{5,4},{6,7},{7,6},{8,9},{9,8},{10,11... | collective-permute-start | bytes 6291464 | tf_op jit(solution)/shard_map/ppermute | solution.py:91
  601.7 101.6 %collective-permute-start.82 = (bf16[2,256,1536]{1,2,0:T(8,128)(2,1)}, bf16[2,256,1536]{1,2,0:T(8,128)(2,1)}, u32[]{:S(2)}, u32[]{:S(2)}) collective-permute-start(bf16[2,256,1536]{1,2,0:T(8,128)(2,1)} %add_convert_fusion.6), channel_id=1, source_target_pairs={{4,0},{8,4},{12,8},{14,12},{10,14},{6,10},{2,6},{0,2},{5,1},{9,5},... | collective-permute-start | bytes 4718600 | tf_op jit(solution)/shard_map/ppermute | solution.py:45
  605.5 100.5 %collective-permute-start.62 = (bf16[2,256,1536]{1,2,0:T(8,128)(2,1)}, bf16[2,256,1536]{1,2,0:T(8,128)(2,1)}, u32[]{:S(2)}, u32[]{:S(2)}) collective-permute-start(bf16[2,256,1536]{1,2,0:T(8,128)(2,1)} %add_convert_fusion.8), channel_id=1, source_target_pairs={{0,4},{4,8},{8,12},{12,14},{14,10},{10,6},{6,2},{2,0},{1,5},{5,9},... | collective-permute-start | bytes 4718600 | tf_op jit(solution)/shard_map/ppermute | solution.py:45
  649.8 50.9 %collective-permute-start.81 = (bf16[320,256]{1,0:T(8,128)(2,1)}, bf16[320,256]{1,0:T(8,128)(2,1)}, u32[]{:S(2)}, u32[]{:S(2)}) collective-permute-start(bf16[320,256]{1,0:T(8,128)(2,1)} %get-tuple-element.181), channel_id=1, source_target_pairs={{4,0},{8,4},{12,8},{14,12},{10,14},{6,10},{2,6},{0,2},{5,1},{9,5},... | collective-permute-start | bytes 491528 | tf_op jit(solution)/shard_map/ppermute | solution.py:45
  652.7 49.1 %collective-permute-start.61 = (bf16[320,256]{1,0:T(8,128)(2,1)}, bf16[320,256]{1,0:T(8,128)(2,1)}, u32[]{:S(2)}, u32[]{:S(2)}) collective-permute-start(bf16[320,256]{1,0:T(8,128)(2,1)} %get-tuple-element.161), channel_id=1, source_target_pairs={{0,4},{4,8},{8,12},{12,14},{14,10},{10,6},{6,2},{2,0},{1,5},{5,9},... | collective-permute-start | bytes 491528 | tf_op jit(solution)/shard_map/ppermute | solution.py:45
  706.2 37.8 %collective-permute-start.51 = (bf16[512,2048]{1,0:T(8,128)(2,1)S(1)}, bf16[512,2048]{1,0:T(8,128)(2,1)S(1)}, u32[]{:S(2)}, u32[]{:S(2)}) collective-permute-start(bf16[512,2048]{1,0:T(8,128)(2,1)S(1)} %constant_dynamic-slice_fusion), channel_id=1, source_target_pairs={{0,1},{1,0},{2,3},{3,2},{4,5},{5,4},{6,7},{7,6},{8,9},{9,8},{10,11... | collective-permute-start | bytes 6291464 | tf_op jit(solution)/shard_map/ppermute | solution.py:89
  746.1 34.3 %collective-permute-start.52 = (bf16[512,2048]{1,0:T(8,128)(2,1)}, bf16[512,2048]{1,0:T(8,128)(2,1)}, u32[]{:S(2)}, u32[]{:S(2)}) collective-permute-start(bf16[512,2048]{1,0:T(8,128)(2,1)} %add_convert_fusion.1), channel_id=1, source_target_pairs={{0,16},{16,0},{1,17},{17,1},{2,18},{18,2},{3,19},{19,3},{4,20},{20... | collective-permute-start | bytes 6291464 | tf_op jit(solution)/shard_map/ppermute | solution.py:90
  767.9 27.0 %collective-permute-start.90 = (bf16[256,1280]{1,0:T(8,128)(2,1)}, bf16[256,1280]{1,0:T(8,128)(2,1)S(1)}, u32[]{:S(2)}, u32[]{:S(2)}) collective-permute-start(bf16[256,1280]{1,0:T(8,128)(2,1)} %add_convert_fusion.14), channel_id=1, source_target_pairs={{4,0},{8,4},{12,8},{14,12},{10,14},{6,10},{2,6},{0,2},{5,1},{9,5},... | collective-permute-start | bytes 1966088 | tf_op jit(solution)/shard_map/ppermute | solution.py:45
  (158 other events, 1911.6 us)

commit v2 on v1

--- a/solution.py
+++ b/solution.py
@@ -16,6 +16,13 @@
 SWAP = [(0, 1), (1, 0)]
 F32 = jnp.float32
 BF16 = jnp.bfloat16
+COST = pl.CostEstimate(flops=0, bytes_accessed=0, transcendentals=0)
+
+
+def after(x, *others):
+    if not others:
+        return x
+    return lax.optimization_barrier((x,) + others)[0]
 
 
 def ring_order(count):
@@ -28,69 +35,117 @@
 
 
 class Ring:
-    def __init__(self, count, depth=2):
+    def __init__(self, count, depth=3):
         order = ring_order(count)
         self.count = count
+        self.half = count // 2
+        self.reps = max(1, self.half // 4)
         self.pairs = {
             1: [(order[i], order[(i + 1) % count]) for i in range(count)],
             -1: [(order[(i + 1) % count], order[i]) for i in range(count)],
         }
         self.done = {1: [], -1: []}
         self.depth = depth
-
-    def hop(self, x, way):
-        done = self.done[way]
-        if len(done) >= self.depth:
-            x, _ = lax.optimization_barrier((x, done[-self.depth]))
+        self.mark = ()
+
+    def hop(self, x, way, free=False):
+        if not free:
+            held = self.done[way]
+            others = self.mark + tuple(held[-self.depth :][:1] if len(held) >= self.depth else ())
+            if others:
+                x = after(x, *others)
         got = lax.ppermute(x, "seq", self.pairs[way])
-        done.append(got)
+        if not free:
+            self.done[way].append(got)
         return got
 
-    def gather(self, x):
-        n = self.count
-        parts = [None] * n
-        parts[0] = x
-        ahead = behind = x
-        for step in range(1, n // 2):
-            ahead = self.hop(ahead, 1)
-            behind = self.hop(behind, -1)
-            parts[n - step] = ahead
-            parts[step] = behind
-        cut = x.shape[0] // 2
-        far = [self.hop(ahead[:cut], 1), self.hop(behind[cut:], -1)]
-        parts[n // 2] = jnp.concatenate(far, axis=0)
-        return parts
-
-    def scatter(self, part):
-        n = self.count
-        half = n // 2
-        far = part(half)
-        cut = far.shape[0] // 2
-        ahead = self.hop(far[:cut].astype(BF16), 1)
-        behind = self.hop(far[cut:].astype(BF16), -1)
-        for step in range(1, half):
-            up, down = part(half - step), part(half + step)
-            if step == 1:
-                up = jnp.concatenate([up[:cut] + ahead.astype(F32), up[cut:]], axis=0)
-                down = jnp.concatenate([down[:cut], down[cut:] + behind.astype(F32)], axis=0)
+
+class Gather:
+    def __init__(self, ring, x, free=False):
+        self.ring, self.free = ring, free
+        self.parts = [None] * ring.count
+        self.parts[0] = x
+        self.last = (x, x)
+        self.step = 0
+
+    def pieces(self):
+        far = self.ring.half
+        every = [(part, k, None) for k, part in enumerate(self.parts) if k != far]
+        return every + [(self.last[0], far, 0), (self.last[1], far, 1)]
+
+    def hop(self):
+        ring = self.ring
+        for _ in range(ring.reps):
+            self.step += 1
+            ahead, behind = self.last
+            if self.step < ring.half:
+                self.last = (ring.hop(ahead, 1, self.free), ring.hop(behind, -1, self.free))
+                self.parts[ring.count - self.step], self.parts[self.step] = self.last
             else:
-                up = up + ahead.astype(F32)
-                down = down + behind.astype(F32)
-            ahead = self.hop(up.astype(BF16), 1)
-            behind = self.hop(down.astype(BF16), -1)
-        return part(0) + (ahead.astype(F32) + behind.astype(F32))
-
-
-def group_sum(part):
-    half = part.shape[0] // 2
-    core = lax.axis_index("ch")
-    mine = lax.dynamic_slice_in_dim(part, core * half, half, 0)
-    theirs = lax.dynamic_slice_in_dim(part, (1 - core) * half, half, 0)
-    chip = (mine.astype(F32) + lax.ppermute(theirs, "ch", SWAP).astype(F32)).astype(BF16)
-    both = (chip.astype(F32) + lax.ppermute(chip, "br", SWAP).astype(F32)).astype(BF16)
-    other = lax.ppermute(both, "ch", SWAP)
-    first = core == 0
-    return jnp.concatenate([jnp.where(first, both, other), jnp.where(first, other, both)], axis=0)
+                cut = ahead.shape[0] // 2
+                self.last = (
+                    ring.hop(ahead[:cut], 1, self.free),
+                    ring.hop(behind[cut:], -1, self.free),
+                )
+                self.parts[ring.half] = jnp.concatenate(self.last, axis=0)
+
+
+class Scatter:
+    def __init__(self, ring, part, free=False):
+        self.ring, self.part, self.free = ring, part, free
+        self.last = None
+        self.step = 0
+
+    def hop(self):
+        ring = self.ring
+        for _ in range(ring.reps):
+            self.step += 1
+            mark = () if self.free else ring.mark
+            if self.step == 1:
+                far = self.part(ring.half, *mark)
+                self.cut = cut = far.shape[0] // 2
+                up, down = far[:cut], far[cut:]
+            else:
+                ahead, behind = (x.astype(F32) for x in self.last)
+                cut, at = self.cut, self.step - 1
+                up = self.part(ring.half - at, *mark, self.last[0])
+                down = self.part(ring.half + at, *mark, self.last[1])
+                if at == 1:
+                    up = jnp.concatenate([up[:cut] + ahead, up[cut:]], axis=0)
+                    down = jnp.concatenate([down[:cut], down[cut:] + behind], axis=0)
+                else:
+                    up, down = up + ahead, down + behind
+            self.last = (
+                ring.hop(up.astype(BF16), 1, self.free),
+                ring.hop(down.astype(BF16), -1, self.free),
+            )
+
+    def result(self):
+        return self.part(0, *self.last) + (self.last[0].astype(F32) + self.last[1].astype(F32))
+
+
+class TokenSum:
+    def second(self, mine, others):
+        got = lax.ppermute(others, "ch", SWAP)
+        self.chip = (mine.astype(F32) + got.astype(F32)).astype(BF16)
+
+    def cross(self, *others):
+        self.far = lax.ppermute(after(self.chip, *others), "br", SWAP)
+
+    def first(self, mine, others):
+        self.own = mine
+        self.core = lax.ppermute(others, "ch", SWAP)
+
+
+class TokenGather:
+    def __init__(self, own):
+        self.own = own
+        self.far = lax.ppermute(own, "br", SWAP)
+        self.core = lax.ppermute(own, "ch", SWAP)
+        self.far_core = lax.ppermute(self.far, "ch", SWAP)
+
+    def parts(self):
+        return [self.own, self.core, self.far, self.far_core]
 
 
 def tiny_group_sum(x):
@@ -184,13 +239,13 @@
         last_ref[1:2, own] = loc[rows - 1 :]
 
 
-def adjoint_kernel(
-    dmix_ref, zg_ref, loc_ref, prod_ref, gate_ref, mask_ref, enter_ref, rate_ref,
-    adj_ref, tail_ref, dzg_ref, head_ref, after,
+def adjoint_body(
+    where, weight, d_ref, z_ref, loc_ref, prod_ref, gate_ref, mask_ref, enter_ref, rate_ref,
+    adj_ref, tail_ref, dzg_ref, head_ref, dmix_ref, after,
 ):
     step = pl.program_id(0)
-    rows, channels = zg_ref.shape
-    reset_col = mask_ref.shape[1] - 1
+    rows, channels = loc_ref.shape
+    dmix_ref[...] = lax.dot_general(d_ref[...], weight[...], NT, preferred_element_type=F32)
 
     @pl.when(step == 0)
     def _():
@@ -203,8 +258,8 @@
     for lane in range(0, channels, LANES):
         own = slice(lane, lane + LANES)
         state = loc_ref[:, own] + prod_ref[:, own] * enter_ref[0:1, own]
-        act, slope = gelu_both(zg_ref[:, own].astype(F32))
-        dmix = dmix_ref[:, own].astype(F32)
+        act, slope = gelu_both(z_ref[:, own].astype(F32))
+        dmix = dmix_ref[:, own]
         dzg_ref[:, own] = (dmix * state * slope).astype(BF16)
         keep = jnp.where(reset, 0.0, jnp.exp(gate_ref[:, own] * rate_ref[0:1, own]))
         at = lax.broadcasted_iota(jnp.int32, keep.shape, 0)
@@ -341,29 +396,8 @@
         ],
         scratch_shapes=[pltpu.VMEM((rows + 8, channels), F32)],
         compiler_params=kernel_params(),
+        cost_estimate=COST,
     )(z, rim, mask, conv, wide, bias, rate)
-
-
-def adjoint_local(dmix, z, loc, prod, gate, mask, enter, rate):
-    tokens, channels = loc.shape
-    rows = min(ROWS, tokens)
-    last = tokens // rows - 1
-    whole = lambda x: pl.BlockSpec(x.shape, lambda i: (0,) * x.ndim)
-    time = lambda width: pl.BlockSpec((rows, width), lambda i: (last - i, 0))
-    return pl.pallas_call(
-        adjoint_kernel,
-        grid=(tokens // rows,),
-        in_specs=[time(channels)] * 5 + [time(mask.shape[1]), whole(enter), whole(rate)],
-        out_specs=[time(channels)] * 3 + [pl.BlockSpec((8, channels), lambda i: (0, 0))],
-        out_shape=[
-            jax.ShapeDtypeStruct((tokens, channels), F32),
-            jax.ShapeDtypeStruct((tokens, channels), F32),
-            jax.ShapeDtypeStruct((tokens, channels), BF16),
-            jax.ShapeDtypeStruct((8, channels), F32),
-        ],
-        scratch_shapes=[pltpu.VMEM((8, channels), F32)],
-        compiler_params=kernel_params(),
-    )(dmix, z, loc, prod, gate, mask, enter, rate)
 
 
 def backward_local(adj, tail, arrive, loc, prod, enter, gate, unit, mask, z, rim, conv, wide, rate):
@@ -399,12 +433,308 @@
             pltpu.VMEM((span, rows + 8, channels), F32),
         ],
         compiler_params=kernel_params(),
+        cost_estimate=COST,
     )(adj, tail, arrive, loc, prod, loc, prod, enter, gate, unit, mask, z, z, rim, conv, wide, rate)
 
 
 def pad_rows(x, rows, before=False):
     extra = rows - x.shape[0]
     return jnp.pad(x, ((extra, 0) if before else (0, extra), (0, 0)))
+
+
+def pieces_of(width, where, count):
+    cols = width // count
+    for k in range(count):
+        true = pl.ds(pl.multiple_of(where[k] * cols, LANES), cols) if count > 1 else slice(0, width)
+        yield slice(k * cols, (k + 1) * cols), true
+
+
+def norm_one_kernel(count, where, x_ref, gain_ref, h_ref):
+    width = x_ref.shape[1]
+    x = x_ref[...]
+    rstd = lax.rsqrt(jnp.sum(x * x, axis=1, keepdims=True) * (1.0 / width) + NORM_EPS)
+    for own, true in pieces_of(width, where, count):
+        h_ref[:, own] = (x_ref[:, true] * rstd * gain_ref[:, own]).astype(BF16)
+
+
+def low_kernel(count, where, x_ref, low_ref, true_ref):
+    true_ref[...] = x_ref[...].astype(BF16)
+    for own, true in pieces_of(x_ref.shape[1], where, count):
+        low_ref[:, own] = true_ref[:, true]
+
+
+def summed(refs, own):
+    return sum(ref[:, own].astype(F32) for ref in refs[1:]) + refs[0][:, own].astype(F32)
+
+
+def norm_two_kernel(count, where, x_ref, a_ref, b_ref, c_ref, gain_ref, resid_ref, h_ref):
+    width = x_ref.shape[1]
+    square = 0.0
+    for own, true in pieces_of(width, where, count):
+        resid = x_ref[:, true] + summed((a_ref, b_ref, c_ref), own)
+        resid_ref[:, own] = resid
+        square = square + jnp.sum(resid * resid, axis=1, keepdims=True)
+    rstd = lax.rsqrt(square * (1.0 / width) + NORM_EPS)
+    h_ref[...] = (resid_ref[...] * rstd * gain_ref[...]).astype(BF16)
+
+
+def norm_two_back_kernel(count, where, cot_ref, a_ref, b_ref, c_ref, gain_ref, resid_ref, d_resid_ref, low_ref):
+    width = cot_ref.shape[1]
+    resid = resid_ref[...]
+    rstd = lax.rsqrt(jnp.sum(resid * resid, axis=1, keepdims=True) * (1.0 / width) + NORM_EPS)
+    along = 0.0
+    for own, _ in pieces_of(width, where, count):
+        d_normed = summed((a_ref, b_ref, c_ref), own) * gain_ref[:, own]
+        d_resid_ref[:, own] = d_normed
+        along = along + jnp.sum(d_normed * resid_ref[:, own], axis=1, keepdims=True)
+    along = along * rstd * (1.0 / width)
+    for own, true in pieces_of(width, where, count):
+        d_resid = cot_ref[:, true] + rstd * (d_resid_ref[:, own] - resid_ref[:, own] * rstd * along)
+        d_resid_ref[:, own] = d_resid
+        low_ref[:, own] = d_resid.astype(BF16)
+
+
+def norm_one_back_kernel(count, where, x_ref, a_ref, b_ref, c_ref, gain_ref, d_resid_ref, out_ref, kept):
+    width = x_ref.shape[1]
+    x = x_ref[...]
+    rstd = lax.rsqrt(jnp.sum(x * x, axis=1, keepdims=True) * (1.0 / width) + NORM_EPS)
+    along = 0.0
+    for own, true in pieces_of(width, where, count):
+        d_normed = summed((a_ref, b_ref, c_ref), own) * gain_ref[:, own]
+        kept[:, own] = d_normed
+        along = along + jnp.sum(d_normed * x_ref[:, true], axis=1, keepdims=True)
+    along = along * rstd * (1.0 / width)
+    for own, true in pieces_of(width, where, count):
+        out = d_resid_ref[:, own] + rstd * (kept[:, own] - x_ref[:, true] * rstd * along)
+        out_ref[:, true] = out.astype(BF16)
+
+
+def spread_kernel(count, where, a_ref, b_ref, c_ref, d_ref, out_ref):
+    for slot, ref in enumerate((a_ref, b_ref, c_ref, d_ref)):
+
+        @pl.when(where[count + 4 + pl.program_id(0)] == slot)
+        def _():
+            out_ref[...] = ref[...].astype(F32)
+
+
+def norm_call(kernel, count, where, x, gain, outputs=1, slots=False):
+    tokens, width = x.shape
+    rows = min(ROWS, tokens // 4)
+    per = tokens // 4 // rows
+    time = pl.BlockSpec((rows, width), lambda i, w: (i, 0))
+    moved = pl.BlockSpec((rows, width), lambda i, w: (w[count + i // per] * per + i % per, 0))
+    args = (x,) if gain is None else (x, gain)
+    return pl.pallas_call(
+        functools.partial(kernel, count),
+        grid_spec=pltpu.PrefetchScalarGridSpec(
+            num_scalar_prefetch=1,
+            grid=(tokens // rows,),
+            in_specs=[moved if slots else time] + [pl.BlockSpec(a.shape, lambda i, w: (0, 0)) for a in args[1:]],
+            out_specs=[time] * outputs,
+        ),
+        out_shape=[jax.ShapeDtypeStruct((tokens, width), BF16)] * outputs,
+        compiler_params=kernel_params(),
+        cost_estimate=COST,
+    )(where, *args)
+
+
+def own_call(kernel, count, where, x, total, gain, extra, out_types, scratch=False):
+    tokens, width = x.shape
+    rows = min(64, tokens // 4)
+    per = tokens // 4 // rows
+    time = pl.BlockSpec((rows, width), lambda i, w: (i, 0))
+    true = pl.BlockSpec((rows, width), lambda i, w: (w[count] * per + i, 0))
+    args = (x, total.own, total.core, total.far, gain) + extra
+    return pl.pallas_call(
+        functools.partial(kernel, count),
+        grid_spec=pltpu.PrefetchScalarGridSpec(
+            num_scalar_prefetch=1,
+            grid=(per,),
+            in_specs=[true, time, time, time, pl.BlockSpec(gain.shape, lambda i, w: (0, 0))] + [time] * len(extra),
+            out_specs=[time] * len(out_types),
+            scratch_shapes=[pltpu.VMEM((rows, width), F32)] if scratch else [],
+        ),
+        out_shape=[jax.ShapeDtypeStruct((tokens // 4, width), t) for t in out_types],
+        compiler_params=kernel_params(),
+        cost_estimate=COST,
+    )(where, *args)
+
+
+def spread_call(count, where, parts):
+    rows, width = parts[0].shape
+    whole = pl.BlockSpec((rows, width), lambda i, w: (0, 0))
+    return pl.pallas_call(
+        functools.partial(spread_kernel, count),
+        grid_spec=pltpu.PrefetchScalarGridSpec(
+            num_scalar_prefetch=1,
+            grid=(4,),
+            in_specs=[whole] * 4,
+            out_specs=pl.BlockSpec((rows, width), lambda i, w: (i, 0)),
+        ),
+        out_shape=jax.ShapeDtypeStruct((4 * rows, width), F32),
+        compiler_params=kernel_params(),
+        cost_estimate=COST,
+    )(where, *parts)
+
+
+def weight_call(
+    body, pieces, target, rows, inputs, fixed, outputs, scalars, scratch=(), steps=None, spots=None, earlier=()
+):
+    tokens = inputs[0].shape[0]
+    steps = tokens // rows if steps is None else steps
+    same = lambda i, s: i
+    read, write = spots if spots else (None, same)
+    read = read or [same] * len(inputs)
+    count = len(pieces)
+
+    def kernel(scalar_ref, *refs):
+        shard_refs, refs = refs[:count], refs[count:]
+        weight, sem = refs[-2:]
+
+        @pl.when(pl.program_id(0) == 0)
+        def _():
+            copies = []
+            for n, (ref, (_, place)) in enumerate(zip(shard_refs, pieces)):
+                for m, (source, to) in enumerate(place(scalar_ref)):
+                    copies.append(pltpu.make_async_copy(ref.at[source], weight.at[to], sem.at[n, m]))
+            for copy in copies:
+                copy.start()
+            for copy in copies:
+                copy.wait()
+
+        skip = len(inputs) + len(fixed)
+        body(scalar_ref, weight, *refs[:skip], *refs[skip + len(earlier) : -2])
+
+    whole = lambda x: pl.BlockSpec(x.shape, lambda i, s: (0,) * x.ndim)
+    in_specs = [pl.BlockSpec(memory_space=pl.ANY)] * count
+    for x, at in zip(inputs, read):
+        in_specs.append(pl.BlockSpec((rows, x.shape[1]), lambda i, s, at=at: (at(i, s), 0)))
+    in_specs += [whole(x) for x in fixed] + [pl.BlockSpec(memory_space=pl.ANY)] * len(earlier)
+    out_specs, out_shape = [], []
+    for o in outputs:
+        if len(o) == 2:
+            out_specs.append(pl.BlockSpec((rows, o[0]), lambda i, s: (write(i, s), 0)))
+            out_shape.append(jax.ShapeDtypeStruct((tokens, o[0]), o[1]))
+        else:
+            out_specs.append(pl.BlockSpec(o[:2], lambda i, s: (0, 0)))
+            out_shape.append(jax.ShapeDtypeStruct(o[:2], o[2]))
+    first = 1 + count + len(inputs) + len(fixed)
+    return pl.pallas_call(
+        kernel,
+        grid_spec=pltpu.PrefetchScalarGridSpec(
+            num_scalar_prefetch=1,
+            grid=(steps,),
+            in_specs=in_specs,
+            out_specs=out_specs,
+            scratch_shapes=list(scratch) + [pltpu.VMEM(target, BF16), pltpu.SemaphoreType.DMA((count, 16))],
+        ),
+        out_shape=out_shape,
+        input_output_aliases={first + i: i for i in range(len(earlier))},
+        compiler_params=kernel_params(),
+        cost_estimate=COST,
+    )(scalars, *[array for array, _ in pieces], *inputs, *fixed, *earlier)
+
+
+def row_pieces(ring_gather, cols, lane=lambda s: slice(None)):
+    out = []
+    for array, k, half in ring_gather.pieces():
+        first = array.shape[0] if half == 1 else 0
+        size = min(array.shape[0], cols - first)
+        if size > 0:
+            place = lambda s, start=k * cols + first, size=size: [
+                ((pl.ds(0, size),), (pl.ds(start, size), lane(s)))
+            ]
+            out.append((array, place))
+    return out
+
+
+def col_pieces(ring_gather, cols):
+    if cols % LANES:
+        return [(jnp.concatenate(ring_gather.parts, axis=1), lambda s: [((slice(None),), (slice(None),))])]
+    out = []
+    for array, k, half in ring_gather.pieces():
+        size = array.shape[0]
+        start = size if half == 1 else 0
+        out.append(
+            (
+                array,
+                lambda s, start=start, size=size, k=k: [
+                    ((slice(None),), (pl.ds(start, size), pl.ds(k * cols, cols)))
+                ],
+            )
+        )
+    return out
+
+
+NT = (((1,), (1,)), ((), ()))
+
+
+def product_body(where, weight, x_ref, out_ref):
+    out_ref[...] = jnp.dot(x_ref[...], weight[...], preferred_element_type=F32).astype(BF16)
+
+
+def to_quarter(slot, refs, value):
+    for s, ref in enumerate(refs):
+
+        @pl.when(slot == s)
+        def _():
+            ref[...] = value.astype(BF16)
+
+
+def product_nt_body(where, weight, x_ref, *out_refs):
+    part = lax.dot_general(x_ref[...], weight[...], NT, preferred_element_type=F32)
+    to_quarter(pl.program_id(0), out_refs, part)
+
+
+def output_body(count, where, weight, hidden_ref, *refs):
+    attn_refs, out_ref, part = refs[:4], refs[4], refs[5]
+    part[...] = jnp.dot(hidden_ref[...], weight[...], preferred_element_type=F32)
+    width = part.shape[1]
+    for slot, ref in enumerate(attn_refs):
+
+        @pl.when(pl.program_id(0) == slot)
+        def _():
+            part[...] += ref[...].astype(F32)
+
+    cols = width // count
+    for k in range(count):
+        own = slice(k * cols, (k + 1) * cols)
+        to = pl.ds(pl.multiple_of(where[count + 8 + k] * cols, LANES), cols) if count > 1 else own
+        out_ref[:, to] = part[:, own].astype(BF16)
+
+
+def mixed_body(count, where, weight, z_ref, loc_ref, prod_ref, enter_ref, mixed_ref, *out_refs):
+    channels = loc_ref.shape[1]
+    act, _ = gelu_both(z_ref[:, :channels].astype(F32))
+    mixed_ref[...] = (act * (loc_ref[...] + prod_ref[...] * enter_ref[...])).astype(BF16)
+    part = jnp.dot(mixed_ref[...], weight[...], preferred_element_type=F32)
+    to_quarter(where[count + 4 + pl.program_id(0)], out_refs, part)
+
+
+def gate_up_body(where, weight, h_ref, hidden_ref, act_ref, slope_ref, both):
+    units = hidden_ref.shape[1]
+    both[...] = jnp.dot(h_ref[...], weight[...], preferred_element_type=F32)
+    for lane in range(0, units, LANES):
+        own = slice(lane, lane + LANES)
+        act, slope = gelu_both(both[:, own])
+        up = both[:, units + lane : units + lane + LANES]
+        hidden_ref[:, own] = (act * up).astype(BF16)
+        act_ref[:, own] = act.astype(BF16)
+        slope_ref[:, own] = (slope * up).astype(BF16)
+
+
+def d_hidden_body(where, weight, d_ref, act_ref, slope_ref, out_ref):
+    units = act_ref.shape[1]
+    d_hidden = lax.dot_general(d_ref[...], weight[...], NT, preferred_element_type=F32)
+    out_ref[:, :units] = (d_hidden * slope_ref[...].astype(F32)).astype(BF16)
+    out_ref[:, units:] = (d_hidden * act_ref[...].astype(F32)).astype(BF16)
+
+
+def d_h_one_body(where, weight, dzg_ref, dzr_ref, *out_refs):
+    channels = dzg_ref.shape[1]
+    gate = lax.dot_general(dzg_ref[...], weight[:, :channels], NT, preferred_element_type=F32)
+    rec = lax.dot_general(dzr_ref[...], weight[:, channels:], NT, preferred_element_type=F32)
+    to_quarter(pl.program_id(0), out_refs, gate + rec)
 
 
 def per_device(
@@ -427,25 +757,42 @@
     count, index = lax.axis_size("seq"), lax.axis_index("seq")
     br, ch = lax.axis_index("br"), lax.axis_index("ch")
     place = ring_place(index, count)
-    order = jnp.asarray(ring_order(count), jnp.int32)
     cols = width // count
     taps = conv_weight.shape[0]
     span = taps - 1
     part_ch = conv_weight.shape[3]
     channels = part_ch * count
+    hidden_units = mlp_down.shape[0]
     heads, part_in, block = gate_weight.shape[3], gate_weight.shape[4], gate_weight.shape[5]
-    true_of = [order[(place + k) % count] for k in range(count)]
-    ring_of = [(ring_place(jnp.int32(s), count) - place) % count for s in range(count)]
-
-    def to_ring(x):
+    ahead = (place + jnp.arange(count, dtype=jnp.int32)) % count
+    true_all = jnp.where(ahead < count // 2, 2 * ahead, 2 * (count - 1 - ahead) + 1)
+    ring_index = (ring_place(jnp.arange(count, dtype=jnp.int32), count) - place) % count
+    true_of = [true_all[k] for k in range(count)]
+    ring_of = [ring_index[k] for k in range(count)]
+    aligned = cols % LANES == 0
+
+    def move(x, at):
         return jnp.concatenate(
-            [lax.dynamic_slice_in_dim(x, true_of[k] * cols, cols, 1) for k in range(count)], axis=1
+            [lax.dynamic_slice_in_dim(x, a * cols, cols, 1) for a in at], axis=1
         )
 
-    def from_ring(x):
-        return jnp.concatenate(
-            [lax.dynamic_slice_in_dim(x, ring_of[s] * cols, cols, 1) for s in range(count)], axis=1
-        )
+    quarter = tokens // 4
+    me = ch * 2 + br
+    quarters = me ^ jnp.asarray([0, 2, 1, 3], jnp.int32)
+    slots = me ^ jnp.arange(4, dtype=jnp.int32)
+    slots = (slots % 2) * 2 + slots // 2
+    per_device_cols = count // 4
+    to = true_all // per_device_cols
+    dealt = (((to % 2) ^ ch) * 2 + ((to // 2) ^ br)) * per_device_cols + true_all % per_device_cols
+    whole_inputs = inputs
+    if aligned:
+        n_pieces = count
+        where = jnp.concatenate([true_all, quarters, slots, dealt, br[None]]).astype(jnp.int32)
+    else:
+        n_pieces = 1
+        zero = jnp.zeros((1,), jnp.int32)
+        where = jnp.concatenate([zero, quarters, slots, zero, br[None]]).astype(jnp.int32)
+        inputs, cotangent = move(inputs, true_of), move(cotangent, true_of)
 
     ring = Ring(count)
 
@@ -467,19 +814,32 @@
         [gate_weight[:, 0, 0].transpose(1, 2, 0, 3).reshape(gate_rows, fold), small], axis=0
     )
     packed = pad_rows(packed, -(-packed.shape[0] // 32) * 32)
-    packed_all = ring.gather(packed)
+    packed_rows = packed.shape[0] * fold // channels
+    packed_shape = packed.shape
 
     own_cols = lax.dynamic_slice_in_dim(in_weight[0], br * channels, channels, 1)
     far_cols = lax.ppermute(
         lax.dynamic_slice_in_dim(in_weight[0], (1 - br) * channels, channels, 1), "br", SWAP
     )
-    w_in_own = jnp.concatenate(
-        [jnp.where(br == 0, own_cols, far_cols), jnp.where(br == 0, far_cols, own_cols)], axis=1
-    )
-    w_in = ring.gather(w_in_own)
-    w_out = ring.gather(out_weight[0, 0])
-    w_mlp = ring.gather(mlp_in)
-    w_down = ring.gather(mlp_down)
+    extra_rows = -(-(cols + packed_rows) // 32) * 32 - cols - packed_rows
+    own_and_packed = jnp.concatenate(
+        [own_cols, packed.reshape(packed_rows, channels), jnp.zeros((extra_rows, channels), BF16)], axis=0
+    )
+    in_own, in_far = Gather(ring, own_and_packed), Gather(ring, far_cols)
+    out_ring = Gather(ring, out_weight[0, 0])
+    down_ring = Gather(ring, mlp_down)
+    in_own.hop()
+    in_far.hop()
+    own_first, far_first = in_own.last, in_far.last
+    in_own.hop()
+    in_far.hop()
+    own_second, far_second = in_own.last, in_far.last
+    in_own.hop()
+    in_far.hop()
+    mlp_all = lax.all_gather(after(mlp_in, *in_far.last), "seq", axis=1, tiled=True)
+    in_own.hop()
+    in_far.hop()
+    out_ring.hop()
 
     doc_starts = jnp.cumsum(lengths) - lengths
     positions = jnp.arange(tokens + span, dtype=jnp.int32) + index * tokens - span
@@ -490,10 +850,10 @@
     reset = jnp.any(positions[span:, None] == doc_starts[None, :], axis=1).astype(F32)
     mask = jnp.stack(lags + [reset], axis=1)
 
+    packed_all = [part[cols : cols + packed_rows].reshape(packed_shape) for part in in_own.parts]
     small_all = jnp.stack([part[gate_rows : gate_rows + small_rows].reshape(-1) for part in packed_all])
     gain_one = small_all[:, :cols].astype(F32).reshape(1, width)
     gain_two = small_all[:, cols : 2 * cols].astype(F32).reshape(1, width)
-    ring_index = jnp.stack(ring_of)
     place_hot = (ring_index[:, None] == jnp.arange(count)[None, :]).astype(BF16)
     chan = jnp.dot(place_hot, small_all[:, 2 * cols :], preferred_element_type=F32)
     chan = chan[:, : (taps + 4) * part_ch].reshape(count, taps + 4, part_ch)
@@ -519,110 +879,209 @@
     compact = jnp.dot(row_hot, stacked, preferred_element_type=F32).astype(BF16)
     wide = jnp.dot(compact, spread_hot, preferred_element_type=F32).astype(BF16) * on_block
 
-    x_in = to_ring(inputs)
-    rstd_one = lax.rsqrt(jnp.mean(x_in * x_in, axis=1, keepdims=True) + NORM_EPS)
-    h_one = (x_in * rstd_one * gain_one).astype(BF16)
-    z = jnp.dot(h_one, jnp.concatenate(w_in, axis=0), preferred_element_type=F32).astype(BF16)
-
+    (h_one,) = norm_call(norm_one_kernel, n_pieces, where, inputs, gain_one)
+    scalars = where
+    last_at = where.shape[0] - 1
+    in_pieces = row_pieces(in_own, cols, lambda s: pl.ds(pl.multiple_of(s[last_at] * channels, LANES), channels))
+    in_pieces += row_pieces(
+        in_far, cols, lambda s: pl.ds(pl.multiple_of((1 - s[last_at]) * channels, LANES), channels)
+    )
+    in_shape = (width, 2 * channels)
+    (z_last,) = weight_call(
+        product_body, in_pieces, in_shape, 16, (h_one[tokens - 16 :],), (), [(2 * channels, BF16)], scalars
+    )
     forward_pairs = [(i, i + 1) for i in range(count - 1)]
-    rim = lax.ppermute(z[tokens - 8 :, channels:], "seq", forward_pairs).astype(F32)
-    unit, gates, loc, prod, last, total = forward_local(z, rim, mask, conv, wide, gate_bias_all, rate)
-    enter = entering(last[:2], False)[None]
-    act = jax.nn.gelu(z[:, :channels].astype(F32))
-    mixed = (act * (loc + prod * enter)).astype(BF16)
-
-    w_out_all = jnp.concatenate(w_out, axis=1)
-    attn = group_sum(jnp.dot(mixed, w_out_all, preferred_element_type=F32).astype(BF16))
-    resid = x_in + attn.astype(F32)
-    rstd_two = lax.rsqrt(jnp.mean(resid * resid, axis=1, keepdims=True) + NORM_EPS)
-    h_two = (resid * rstd_two * gain_two).astype(BF16)
-
-    w_mlp_all = jnp.concatenate(w_mlp, axis=1)
-    gate_up = jnp.einsum("td,gdf->gtf", h_two, w_mlp_all, preferred_element_type=F32)
-    act_gate, act_slope = gelu_both(gate_up[0])
-    hidden = (act_gate * gate_up[1]).astype(BF16)
-    cot = to_ring(cotangent)
-    d_mlp = cot.astype(BF16)
+    rim = lax.ppermute(z_last[8:, channels:], "seq", forward_pairs).astype(F32)
+    (z,) = weight_call(
+        product_body, in_pieces, in_shape, quarter, (after(h_one, z_last),), (), [(2 * channels, BF16)], scalars
+    )
+    ring.mark = (z, rim)
+    out_first = out_ring.last
+    out_ring.hop()
+
+    unit, gates, loc, prod, last, total = forward_local(
+        after(z, *out_first), rim, mask, conv, wide, gate_bias_all, rate
+    )
+    ring.mark = (last,)
+    out_second = out_ring.last
+    out_ring.hop()
+    enter = entering(after(last[:2], *out_second), False)[None]
+    ring.mark = (enter,)
+    out_third = out_ring.last
+    out_ring.hop()
+    down_ring.hop()
+
+    to_slot = lambda i, s: s[n_pieces + 4 + i]
+    from_slot = lambda i, s: s[n_pieces + i]
+    out_pieces = col_pieces(out_ring, cols)
+    out_shape = (channels, width)
+    one_quarter = (quarter, width, BF16)
+    mixed, *attn_parts = weight_call(
+        functools.partial(mixed_body, n_pieces), out_pieces, out_shape, quarter, (z, loc, prod),
+        (after(enter, *out_third),), [(channels, BF16)] + [one_quarter] * 4, scalars, spots=(None, to_slot),
+    )
+    attn = TokenSum()
+    attn.second(*attn_parts[2:])
+    attn.cross()
+    attn.first(*attn_parts[:2])
+    down_first = down_ring.last
+    ring.mark = (attn.chip,)
+    down_ring.hop()
+    d_mlp, slot_cot = norm_call(low_kernel, n_pieces, where, after(cotangent, attn.chip), None, 2, slots=True)
+    if not aligned:
+        slot_cot = move(slot_cot, ring_of)
+
+    resid, h_own = own_call(
+        norm_two_kernel, n_pieces, where, inputs, attn, after(gain_two, d_mlp, *down_first), (), (F32, BF16)
+    )
+    h_two = TokenGather(h_own)
+    down_second = down_ring.last
+    ring.mark = (h_own,)
+    down_ring.hop()
+    h_two = after(jnp.concatenate(h_two.parts(), axis=0), *down_second)
+    down_third = down_ring.last
+    ring.mark = (h_two,)
+    down_ring.hop()
+
+
+    def mlp_place(s):
+        out = []
+        for k in range(count):
+            rows = pl.ds(pl.multiple_of(s[k] * cols, 8), cols)
+            for g in range(2):
+                out.append(
+                    ((g, rows), (pl.ds(k * cols, cols), pl.ds(g * hidden_units, hidden_units)))
+                )
+        return out
+
+    if aligned:
+        mlp_pieces = [(mlp_all, mlp_place)]
+    else:
+        moved = [lax.dynamic_slice_in_dim(mlp_all, a * cols, cols, 1) for a in true_of]
+        mlp_pieces = [
+            (
+                jnp.concatenate(moved, axis=1),
+                lambda s: [
+                    ((g,), (slice(None), pl.ds(g * hidden_units, hidden_units))) for g in range(2)
+                ],
+            )
+        ]
+    mlp_shape = (width, 2 * hidden_units)
+    hidden, act, slope = weight_call(
+        gate_up_body, mlp_pieces, mlp_shape, quarter, (after(h_two, *down_third),), (),
+        [(hidden_units, BF16)] * 3, scalars, scratch=(pltpu.VMEM((quarter, 2 * hidden_units), F32),),
+    )
 
     def chunk(x, k):
         return x[:, k * cols : (k + 1) * cols]
 
-    g_down = ring.scatter(
-        lambda k: lax.dot_general(
-            hidden, chunk(d_mlp, k), (((0,), (0,)), ((), ())), preferred_element_type=F32
-        )
-    )
-    w_down_all = jnp.concatenate(w_down, axis=1)
-    d_hidden = jnp.einsum("td,fd->tf", d_mlp, w_down_all, preferred_element_type=F32)
-    d_gate_up = jnp.stack([d_hidden * gate_up[1] * act_slope, d_hidden * act_gate]).astype(BF16)
-    g_mlp = ring.scatter(
-        lambda k: jnp.einsum("td,gtf->gdf", chunk(h_two, k), d_gate_up, preferred_element_type=F32)
-    )
-    d_h_two = group_sum(
-        jnp.einsum("gtf,gdf->td", d_gate_up, w_mlp_all, preferred_element_type=F32).astype(BF16)
-    ).astype(F32)
-
-    mlp_part = jnp.dot(hidden, w_down_all, preferred_element_type=F32).astype(BF16)
-    per = width // 4 // cols
-
-    def columns(x, b, c):
-        first = (b * 2 + c) * per
-        at = [(ring_place(first + j, count) - place) % count for j in range(per)]
-        return jnp.concatenate([lax.dynamic_slice_in_dim(x, a * cols, cols, 1) for a in at], axis=1)
-
-    mine = jnp.concatenate([columns(mlp_part, b, ch) for b in range(2)], axis=1)
-    theirs = jnp.concatenate([columns(mlp_part, b, 1 - ch) for b in range(2)], axis=1)
-    chip = mine.astype(F32) + lax.ppermute(theirs, "ch", SWAP).astype(F32)
-    own = lax.dynamic_slice_in_dim(chip, br * (width // 4), width // 4, 1)
-    far = lax.dynamic_slice_in_dim(chip, (1 - br) * (width // 4), width // 4, 1).astype(BF16)
-    output = columns(resid, br, ch) + own + lax.ppermute(far, "br", SWAP).astype(F32)
-
-    normed_two = resid * rstd_two
-    g_gain_two = jnp.sum(d_h_two * normed_two, axis=0)
-    d_normed = d_h_two * gain_two
-    d_resid = cot + rstd_two * (d_normed - normed_two * jnp.mean(d_normed * normed_two, axis=1, keepdims=True))
-    d_attn = d_resid.astype(BF16)
-    g_out = ring.scatter(
-        lambda k: lax.dot_general(
-            mixed, chunk(d_attn, k), (((0,), (0,)), ((), ())), preferred_element_type=F32
-        )
-    )
-    d_mixed = jnp.einsum("td,kd->tk", d_attn, w_out_all, preferred_element_type=F32)
-
-    adj, tail, d_z_gate, head = adjoint_local(d_mixed, z, loc, prod, gates, mask, enter, rate)
-    arrive = entering(head[:2], True)[None]
+    def outer(left, right):
+        return lax.dot_general(left, right, (((0,), (0,)), ((), ())), preferred_element_type=F32)
+
+    down_pieces = col_pieces(down_ring, cols)
+    down_shape = (hidden_units, width)
+    (d_gate_up,) = weight_call(
+        d_hidden_body, down_pieces, down_shape, quarter, (after(d_mlp, hidden), act, slope), (),
+        [(2 * hidden_units, BF16)], scalars,
+    )
+    ring.mark = (d_gate_up,)
+    g_mlp = Scatter(ring, lambda k, *t: outer(chunk(h_two, k), after(d_gate_up, *t)))
+    g_mlp.hop()
+    mlp_hop = [g_mlp.last]
+    upper, lower = lambda i, s: i + 2, lambda i, s: i
+    part = weight_call(
+        product_nt_body, mlp_pieces, mlp_shape, quarter, (d_gate_up,), (), [one_quarter] * 2, scalars,
+        steps=2, spots=([upper], upper),
+    )
+    d_h_two = TokenSum()
+    d_h_two.second(*part)
+    d_h_two.cross()
+    part = weight_call(
+        product_nt_body, mlp_pieces, mlp_shape, quarter, (after(d_gate_up, d_h_two.chip),), (), [one_quarter] * 2,
+        scalars, steps=2, spots=([lower], lower),
+    )
+    d_h_two.first(*part)
+    ring.mark = (part[0],)
+    g_mlp.hop()
+    mlp_hop.append(g_mlp.last)
+    g_down_part = outer(after(hidden, part[0], *g_mlp.last), slot_cot).astype(BF16)
+    g_down = lax.psum_scatter(g_down_part, "seq", scatter_dimension=1, tiled=True)
+    d_resid, d_attn = own_call(
+        norm_two_back_kernel, n_pieces, where, cotangent, d_h_two, gain_two, (resid,), (F32, BF16)
+    )
+    d_attn = TokenGather(d_attn)
+
+    (o_part,) = weight_call(
+        functools.partial(output_body, n_pieces), down_pieces, down_shape, quarter,
+        (after(hidden, d_attn.own),), tuple(attn_parts), [(width, BF16)], scalars, spots=(None, from_slot),
+        scratch=(pltpu.VMEM((quarter, width), F32),),
+    )
+    if not aligned:
+        at = jnp.arange(count)
+        o_part = move(o_part, [jnp.sum(jnp.where(dealt == k, at, 0)) for k in range(count)])
+    o_cols = width // 4
+    swapped = lax.ppermute(o_part[:, 2 * o_cols :], "ch", SWAP).astype(F32)
+    o_far = lax.ppermute((o_part[:, o_cols : 2 * o_cols].astype(F32) + swapped[:, o_cols:]).astype(BF16), "br", SWAP)
+    o_inputs = lax.dynamic_slice_in_dim(whole_inputs, (br * 2 + ch) * o_cols, o_cols, 1)
+    output = o_inputs + o_part[:, :o_cols].astype(F32) + swapped[:, :o_cols] + o_far.astype(F32)
+
+    ring.mark = (d_attn.own,)
+    mlp_first = mlp_hop[1]
+    g_mlp.hop()
+    mlp_hop.append(g_mlp.last)
+    d_attn = jnp.concatenate(d_attn.parts(), axis=0)
+    rows = min(ROWS, quarter)
+    per = quarter // rows
+    last_step = tokens // rows - 1
+    back = lambda i, s: last_step - i
+    back_slot = lambda i, s: s[n_pieces + 4 + (last_step - i) // per] * per + (last_step - i) % per
+    adj, tail, d_z_gate, head = weight_call(
+        adjoint_body, out_pieces, out_shape, rows, (d_attn, z, loc, prod, gates, mask), (enter, rate),
+        [(channels, F32), (channels, F32), (channels, BF16), (8, channels, F32)], scalars,
+        scratch=(pltpu.VMEM((rows, channels), F32), pltpu.VMEM((8, channels), F32)),
+        spots=([back_slot] + [back] * 5, back),
+    )
+    ring.mark = (head,)
+    g_out = Scatter(ring, lambda k, *t: outer(after(mixed, *t), chunk(d_attn, k)))
+    g_out.hop()
+    out_hop = [g_out.last]
+    arrive = entering(after(head[:2], *mlp_hop[2]), True)[None]
+    g_mlp.hop()
+    mlp_hop.append(g_mlp.last)
     d_z_rec, g_wide, sums, edge = backward_local(
-        adj, tail, arrive, loc, prod, enter, gates, unit, mask, z, rim, conv, wide, rate
-    )
+        adj, tail, after(arrive, *out_hop[0]), loc, prod, enter, gates, unit, mask, z, rim, conv, wide, rate
+    )
+    ring.mark = (edge,)
     backward_pairs = [(i + 1, i) for i in range(count - 1)]
     from_next = lax.ppermute(edge[:8], "seq", backward_pairs)
+    g_out.hop()
+    out_hop.append(g_out.last)
     fixed = (edge[8:] + from_next).astype(BF16)
-    d_z_rec = jnp.concatenate([d_z_rec[: tokens - 8], fixed], axis=0)
+    d_z_rec = d_z_rec.at[tokens - 8 :].set(fixed)
+
     d_z = jnp.concatenate([d_z_gate, d_z_rec], axis=1)
-
-    w_in_all = jnp.concatenate(w_in, axis=0)
-    g_in = ring.scatter(
-        lambda k: lax.dot_general(
-            chunk(h_one, k), d_z, (((0,), (0,)), ((), ())), preferred_element_type=F32
+    d_h_one = TokenSum()
+    for first in (2, 0):
+        read = lambda i, s, first=first: s[n_pieces + i + first]
+        rec = after(d_z_rec, *out_hop[1]) if first else after(d_z_rec, d_h_one.chip, *mlp_hop[3])
+        part = weight_call(
+            d_h_one_body, in_pieces, in_shape, quarter, (d_z_gate, rec), (), [one_quarter] * 2, scalars,
+            steps=2, spots=([read, read], None),
         )
-    )
-    keep_half = lax.dynamic_slice_in_dim(g_in, br * channels, channels, 1)
-    send_half = lax.dynamic_slice_in_dim(g_in, (1 - br) * channels, channels, 1).astype(BF16)
-    got_half = lax.ppermute(send_half, "br", SWAP).astype(F32)
-    g_in = jnp.concatenate(
-        [jnp.where(br == 0, keep_half, got_half), jnp.where(br == 0, got_half, keep_half)], axis=1
-    )
-    d_h_part = lax.dot_general(d_z, w_in_all, (((1,), (1,)), ((), ())), preferred_element_type=F32)
-    d_h_one = group_sum(d_h_part.astype(BF16)).astype(F32)
-    normed_one = x_in * rstd_one
-    g_gain_one = jnp.sum(d_h_one * normed_one, axis=0)
-    d_normed = d_h_one * gain_one
-    inputs_grad = from_ring(
-        d_resid + rstd_one * (d_normed - normed_one * jnp.mean(d_normed * normed_one, axis=1, keepdims=True))
-    )
+        if first:
+            d_h_one.second(*part)
+            d_h_one.cross()
+        else:
+            d_h_one.first(*part)
+    ring.mark = (part[0], d_z)
+    g_in_ring = Scatter(ring, lambda k, *t: outer(chunk(h_one, k), after(d_z, *t)))
+    g_in_ring.hop()
+    in_hop = [g_in_ring.last]
+    g_out.hop()
+    out_hop.append(g_out.last)
 
     g_compact = lax.dot_general(
-        (g_wide * on_block.astype(F32)).astype(BF16),
+        (after(g_wide, d_h_one.chip) * on_block.astype(F32)).astype(BF16),
         spread_hot,
         (((1,), (1,)), ((), ())),
         preferred_element_type=F32,
@@ -631,36 +1090,72 @@
     g_decay = sums[0:1] * -DECAY_SCALE * -jax.nn.sigmoid(-decay_rate)
     g_chan = jnp.concatenate([sums[4 : 4 + taps], sums[3:4], sums[1:3], g_decay, total[0:1]], axis=0)
     g_chan = g_chan.reshape(taps + 5, count, part_ch).transpose(1, 0, 2).reshape(count, -1)
-    g_chan = lax.dot_general(
+    g_small = lax.dot_general(
         place_hot.astype(F32), g_chan, (((0,), (0,)), ((), ())), precision=lax.Precision.HIGHEST
-    )
-    g_small = jnp.concatenate(
-        [g_gain_one.reshape(count, cols), g_gain_two.reshape(count, cols), g_chan], axis=1
     )
     g_rows = -(-g_small.shape[1] // fold)
     g_small = jnp.pad(g_small, ((0, 0), (0, g_rows * fold - g_small.shape[1]))).reshape(count, g_rows, fold)
     g_packed = jnp.concatenate([g_gates.reshape(count, gate_rows, fold), g_small], axis=1)
     total_rows = -(-g_packed.shape[1] // 32) * 32
     g_packed = jnp.pad(g_packed, ((0, 0), (0, total_rows - g_packed.shape[1]), (0, 0)))
-    g_own = ring.scatter(lambda k: g_packed[k])
+    g_packed_ring = Scatter(ring, lambda k, *t: g_packed[k], free=True)
+    for _ in range(4):
+        g_packed_ring.hop()
+    (grad_own,) = own_call(
+        norm_one_back_kernel, n_pieces, where, inputs, d_h_one, after(gain_one, *in_hop[0]), (d_resid,), (BF16,),
+        scratch=True,
+    )
+    grad_parts = TokenGather(grad_own).parts()
+    ring.mark = (grad_own,)
+    g_in_ring.hop()
+    in_hop.append(g_in_ring.last)
+    g_out.hop()
+    ring.mark = g_packed_ring.last
+    g_in_ring.hop()
+    in_hop.append(g_in_ring.last)
+    inputs_grad = spread_call(n_pieces, where, [after(grad_parts[0], *in_hop[1])] + grad_parts[1:])
+    if not aligned:
+        inputs_grad = move(inputs_grad, ring_of)
+    g_in_ring.hop()
+
+    g_in_own = g_in_ring.result()
+    g_in_gate, g_in_rec = g_in_own[:, :channels], g_in_own[:, channels:]
+    keep_half = jnp.where(br == 0, g_in_gate, g_in_rec)
+    send_half = jnp.where(br == 0, g_in_rec, g_in_gate).astype(BF16)
+    got_half = lax.ppermute(send_half, "br", SWAP).astype(F32)
+    g_in = jnp.concatenate(
+        [jnp.where(br == 0, keep_half, got_half), jnp.where(br == 0, got_half, keep_half)], axis=1
+    )
+    g_mlp_own = g_mlp.result()
+    g_gate_own, g_up_own = g_mlp_own[:, :hidden_units], g_mlp_own[:, hidden_units:]
+    w_gate = jnp.where(br == 0, own_cols, far_cols).astype(F32)
+    w_rec = jnp.where(br == 0, far_cols, own_cols).astype(F32)
+    gains = jnp.stack(
+        [
+            jnp.sum(g_in_gate * w_gate, axis=1) + jnp.sum(g_in_rec * w_rec, axis=1),
+            jnp.sum(g_gate_own * mlp_in[0].astype(F32), axis=1)
+            + jnp.sum(g_up_own * mlp_in[1].astype(F32), axis=1),
+        ]
+    )
+    gains = tiny_group_sum(gains)
+    g_own = g_packed_ring.result()
     g_gate_w = g_own[:gate_rows].reshape(heads, part_in, 2, block).transpose(2, 0, 1, 3)[:, None, None]
     g_flat = g_own[gate_rows : gate_rows + g_rows].reshape(-1)
-    g_gain_one, g_gain_two = g_flat[:cols], g_flat[cols : 2 * cols]
-    g_chan = g_flat[2 * cols : 2 * cols + (taps + 5) * part_ch].reshape(taps + 5, part_ch)
+    g_chan = g_flat[: (taps + 5) * part_ch].reshape(taps + 5, part_ch)
     return (
         output,
         inputs_grad,
-        g_gain_one,
+        gains[0] / norm_gain1.astype(F32),
         g_in[None],
         g_chan[:taps][:, None, None],
         g_chan[taps][None, None],
         g_gate_w,
         g_chan[taps + 1 : taps + 3][:, None, None],
         g_chan[taps + 3][None, None],
-        g_out[None, None],
-        g_gain_two,
-        g_mlp,
-        g_down,
+        g_out.result()[None, None],
+        gains[1] / norm_gain2.astype(F32),
+        jnp.stack([g_gate_own, g_up_own]),
+        g_down.astype(F32),
         g_chan[taps + 4][None, None] / (tokens * count),
     )
 

time: 861 us -> 820 us (0.952)
  Pallas kernels: 47.9 us -> 227 us
  matrix products: 170 us -> 78.5 us
  other arithmetic: 99.6 us -> 48.9 us
  waiting for transfers between devices: 286 us -> 240 us
  local copies, waits for them, and re-layouts: 126 us -> 83.9 us
    pallas_call x1 -> x17, Pallas kernels: 10.9 us -> 190 us  [the longest x11 154 us: weight_call(): pl.pallas_call(kernel, grid_spec=pltpu.PrefetchScalarGridSpec(num_scalar_...]
    dot_general x40 -> x25, matrix products: 161 us -> 70.4 us  [outer(): lax.dot_general(left, right, (((0,), (0,)), ((), ())), preferred_element_...]
    ppermute x80 -> x64, waiting for transfers between devices: 246 us -> 193 us  [hop(): got = lax.ppermute(x, 'seq', self.pairs[way])]
    unnamed x242 -> x299, local copies, waits for them, and re-layouts: 88.4 us -> 43.2 us
    convert_element_type x15 -> x11, other arithmetic: 44.3 us -> 16.1 us  [the longest x3 4.43 us: second(): self.chip = (mine.astype(F32) + got.astype(F32)).astype(BF16)]
    reduce_sum x4 -> x0, other arithmetic: 19.3 us -> none  [the longest x1 7 us: per_device(): g_gain_one = jnp.sum(d_h_one * normed_one, axis=0)]
    slice x35 -> x39, local copies, waits for them, and re-layouts: 6.18 us -> 20.1 us  [the longest x14 7.56 us: per_device(): stacked = jnp.concatenate([part[:gate_rows] for part in packed_all], axis=0)]
    ppermute x80 -> x64, starting transfers between devices: 94.8 us -> 84.3 us  [hop(): got = lax.ppermute(x, 'seq', self.pairs[way])]
  transfers between devices with their start and end apart: 97 -> 94, of which waited for: 51 -> 33; matrix products, arithmetic and copies ran while one was open for 35% -> 23% of each run, Pallas kernels for 6% -> 24%
where the time goes in v2:
time: 820 us; the launch traced here: 811 us
  waiting for transfers between devices  240 us (29%)
  Pallas kernels  227 us (28%)
  starting transfers between devices  116 us (14%)
  local copies, waits for them, and re-layouts  83.9 us (10%)
  matrix products  78.5 us (10%)
  other arithmetic  48.9 us (6%)
  between operations  16.8 us (2%)
    ppermute x64, waiting for transfers between devices, hop(): got = lax.ppermute(x, 'seq', self.pairs[way])  193 us
    pallas_call x11, Pallas kernels, weight_call(): pl.pallas_call(kernel, grid_spec=pltpu.PrefetchScalarGridSpec(num_scalar_...  154 us
    ppermute x64, starting transfers between devices, hop(): got = lax.ppermute(x, 'seq', self.pairs[way])  84.3 us
    dot_general x25, matrix products, outer(): lax.dot_general(left, right, (((0,), (0,)), ((), ())), preferred_element_...  70.4 us
    unnamed x299, local copies, waits for them, and re-layouts  43.2 us
    pallas_call x1, Pallas kernels, backward_local(): pl.pallas_call(backward_kernel, grid=(tokens // rows,), in_specs=[time(ch...  22.9 us
    ppermute x3, waiting for transfers between devices, __init__(): self.far = lax.ppermute(own, 'br', SWAP)  20.9 us
    all_to_all x2, waiting for transfers between devices, entering(): every = lax.all_to_all(spread, 'seq', 0, 0, tiled=True)  18.2 us
  transfers between devices with their start and end apart: 94, of which 33 were waited for; matrix products, arithmetic and copies ran while one was open for 23% of the time, Pallas kernels for 24%

profile of v2, /device:TPU:0, one launch (start us, length us, event | category | flops | bytes accessed | tf_op | source)
XLA Modules:
  0.0 810.6 jit_solution(8247055166559475382)
XLA Ops:
  21.3 8.3 %collective-permute-done.5.refs_6_ = bf16[320,640]{1,0:T(8,128)(2,1)S(1)} collective-permute-done((bf16[320,640]{1,0:T(8,128)(2,1)S(1)}, bf16[320,640]{1,0:T(8,128)(2,1)S(1)}, u32[]{:S(2)}, u32[]{:S(2)}) %collective-permute-start.5) | collective-permute-done | bytes 409632 | tf_op jit(solution)/shard_map/ppermute | solution.py:57
  79.3 13.6 %collective-permute-done.8.refs_4_ = bf16[320,640]{1,0:T(8,128)(2,1)S(1)} collective-permute-done((bf16[320,640]{1,0:T(8,128)(2,1)S(1)}, bf16[320,640]{1,0:T(8,128)(2,1)S(1)}, u32[]{:S(2)}, u32[]{:S(2)}) %collective-permute-start.8) | collective-permute-done | bytes 409632 | tf_op jit(solution)/shard_map/ppermute | solution.py:57
  94.9 9.4 %collective-permute-start.10 = (bf16[160,640]{1,0:T(8,128)(2,1)}, bf16[160,640]{1,0:T(8,128)(2,1)}, u32[]{:S(2)}, u32[]{:S(2)}) collective-permute-start(bf16[160,640]{1,0:T(8,128)(2,1)} %slice.774), channel_id=1, source_target_pairs={{0,4},{4,8},{8,12},{12,14},{14,10},{10,6},{6,2},{2,0},{1,5},{5,9},... | collective-permute-start | bytes 614408 | tf_op jit(solution)/shard_map/ppermute | solution.py:57
  132.4 6.9 shard_map.254.refs_18_
  140.1 7.4 collective-permute-done.16.refs_17_
  155.9 12.9 %shard_map.256.z_ref.refs_9_.refs_10_.z0_ref = bf16[1024,1280]{1,0:T(8,128)(2,1)} custom-call(s32[25]{0:T(128)S(1)} %concatenate.67.where.scalar_ref, bf16[320,640]{1,0:T(8,128)(2,1)S(1)} %maximum_maximum_fusion.refs_0_, bf16[320,640]{1,0:T(8,128)(2,1)S(1)} %collective-permute-done.refs_1_, bf16[320,640]{1,0:T(8,128)(2,1)S(1)} %copy-done.23, ...), custom_call_target="tpu_custom_call" | custom-call | tf_op jit(solution)/shard_map/pallas_call | solution.py:622
  175.9 14.1 %shard_map.257 = (bf16[1024,640]{1,0:T(8,128)(2,1)S(1)}, f32[1024,1280]{1,0:T(8,128)}, f32[1024,640]{1,0:T(8,128)S(1)}, f32[1024,640]{1,0:T(8,128)}, f32[8,640]{1,0:T(8,128)S(1)}, /*index=5*/f32[8,640]{1,0:T(8,128)S(1)}) custom-call(bf16[1024,1280]{1,0:T(8,128)(2,1)} %shard_map.256.z_ref.refs_9_.refs_10_.z0_ref, f32[8,640]{1,0:T(8,128)S(1)} %convert_element_type.304.rim_ref, ...), custom_call_target="tpu_custom_call" | custom-call | tf_op jit(solution)/shard_map/pallas_call | solution.py:384
  197.9 6.3 all-to-all-start
  204.3 18.2 %all-to-all-done = f32[8,2,640]{2,1,0:T(2,128)S(1)} async-done(((f32[8,2,640]{2,1,0:T(2,128)}), f32[8,2,640]{2,1,0:T(2,128)S(1)}, u32[]{:S(2)}, u32[]{:S(2)}) %all-to-all-start) | async-done | bytes 40992 | tf_op jit(solution)/shard_map/all_to_all | solution.py:159
  225.6 10.8 %collective-permute-done.26.refs_8_ = bf16[320,256]{1,0:T(8,128)(2,1)S(1)} collective-permute-done((bf16[320,256]{1,0:T(8,128)(2,1)S(1)}, bf16[320,256]{1,0:T(8,128)(2,1)S(1)}, u32[]{:S(2)}, u32[]{:S(2)}) %collective-permute-start.26) | collective-permute-done | bytes 163872 | tf_op jit(solution)/shard_map/ppermute | solution.py:57
  238.4 11.3 %shard_map.258 = (bf16[1024,640]{1,0:T(8,128)(2,1)}, bf16[256,2048]{1,0:T(8,128)(2,1)S(1)}, bf16[256,2048]{1,0:T(8,128)(2,1)S(1)}, bf16[256,2048]{1,0:T(8,128)(2,1)S(1)}, bf16[256,2048]{1,0:T(8,128)(2,1)}) custom-call(s32[25]{0:T(128)S(1)} %concatenate.67.where.scalar_ref, bf16[640,256]{1,0:T(8,128)(2,1)S(1)} %bitcast.436, ...), custom_call_target="tpu_custom_call" | custom-call | tf_op jit(solution)/shard_map/pallas_call | solution.py:622
  258.7 8.1 %shard_map.259 = (bf16[1024,2048]{1,0:T(8,128)(2,1)S(1)}, bf16[1024,2048]{1,0:T(8,128)(2,1)}) custom-call(s32[25]{0:T(128)S(1)} %concatenate.67.where.scalar_ref, f32[1024,2048]{1,0:T(8,128)} %cot_ref.1), custom_call_target="tpu_custom_call" | custom-call | tf_op jit(solution)/shard_map/pallas_call | solution.py:527
  268.8 21.9 %collective-permute-done.22.refs_1_ = bf16[1536,256]{1,0:T(8,128)(2,1)S(1)} collective-permute-done((bf16[1536,256]{1,0:T(8,128)(2,1)S(1)}, bf16[1536,256]{1,0:T(8,128)(2,1)S(1)}, u32[]{:S(2)}, u32[]{:S(2)}) %collective-permute-start.22) | collective-permute-done | bytes 786464 | tf_op jit(solution)/shard_map/ppermute | solution.py:57
  299.6 20.9 %collective-permute-done.36 = bf16[256,2048]{1,0:T(8,128)(2,1)S(1)} collective-permute-done((bf16[256,2048]{1,0:T(8,128)(2,1)S(1)}, bf16[256,2048]{1,0:T(8,128)(2,1)S(1)}, u32[]{:S(2)}, u32[]{:S(2)}) %collective-permute-start.36) | collective-permute-done | bytes 1048608 | tf_op jit(solution)/shard_map/ppermute | solution.py:143
  324.1 17.2 %collective-permute-done.32.refs_3_ = bf16[1536,256]{1,0:T(8,128)(2,1)S(1)} collective-permute-done((bf16[1536,256]{1,0:T(8,128)(2,1)S(1)}, bf16[1536,256]{1,0:T(8,128)(2,1)S(1)}, u32[]{:S(2)}, u32[]{:S(2)}) %collective-permute-start.32) | collective-permute-done | bytes 786464 | tf_op jit(solution)/shard_map/ppermute | solution.py:57
  350.3 22.1 %shard_map.261 = (bf16[1024,1536]{1,0:T(8,128)(2,1)S(1)}, bf16[1024,1536]{1,0:T(8,128)(2,1)}, bf16[1024,1536]{1,0:T(8,128)(2,1)}) custom-call(s32[25]{0:T(128)S(1)} %concatenate.67.where.scalar_ref, bf16[2,2048,1536]{2,1,0:T(8,128)(2,1)} %all-gather.2.cloned.1.call-done.refs_0_, bf16[1024,2048]{1,0:T(8,128)(2,1)} %pad_maximum_fusion.refs_1_), custom_call_target="tpu_custom_call" | custom-call | tf_op jit(solution)/shard_map/pallas_call | solution.py:622
  374.1 14.8 %shard_map.262.refs_1_ = bf16[1024,3072]{1,0:T(8,128)(2,1)} custom-call(s32[25]{0:T(128)S(1)} %concatenate.67.where.scalar_ref, bf16[1536,256]{1,0:T(8,128)(2,1)S(1)} %copy-done.55, bf16[1536,256]{1,0:T(8,128)(2,1)S(1)} %copy-done.58, bf16[1536,256]{1,0:T(8,128)(2,1)S(1)} %copy-done.64, bf16[1536,256]{1,0:T(8,128)(2,1)S(1)} %copy-done.43, ...), custom_call_target="tpu_custom_call" | custom-call | tf_op jit(solution)/shard_map/pallas_call | solution.py:622
  389.0 14.9 %shard_map.263 = (bf16[256,2048]{1,0:T(8,128)(2,1)S(1)}, bf16[256,2048]{1,0:T(8,128)(2,1)S(1)}) custom-call(s32[25]{0:T(128)S(1)} %concatenate.67.where.scalar_ref, bf16[2,2048,1536]{2,1,0:T(8,128)(2,1)} %all-gather.2.cloned.1.call-done.refs_0_, bf16[1024,3072]{1,0:T(8,128)(2,1)} %shard_map.262.refs_1_), custom_call_target="tpu_custom_call" | custom-call | tf_op jit(solution)/shard_map/pallas_call | solution.py:622
  412.0 14.9 %shard_map.264 = (bf16[256,2048]{1,0:T(8,128)(2,1)S(1)}, bf16[256,2048]{1,0:T(8,128)(2,1)}) custom-call(s32[25]{0:T(128)S(1)} %concatenate.67.where.scalar_ref, bf16[2,2048,1536]{2,1,0:T(8,128)(2,1)} %all-gather.2.cloned.1.call-done.refs_0_, bf16[1024,3072]{1,0:T(8,128)(2,1)} %shard_map.262.refs_1_), custom_call_target="tpu_custom_call" | custom-call | tf_op jit(solution)/shard_map/pallas_call | solution.py:622
  442.5 6.5 shard_map.265
  450.4 15.9 %shard_map.266 = bf16[1024,2048]{1,0:T(8,128)(2,1)} custom-call(s32[25]{0:T(128)S(1)} %concatenate.67.where.scalar_ref, bf16[1536,256]{1,0:T(8,128)(2,1)S(1)} %copy-done.56, bf16[1536,256]{1,0:T(8,128)(2,1)S(1)} %copy-done.59, bf16[1536,256]{1,0:T(8,128)(2,1)S(1)} %copy-done.65, bf16[1536,256]{1,0:T(8,128)(2,1)S(1)} %copy-done.44, ...), custom_call_target="tpu_custom_call" | custom-call | tf_op jit(solution)/shard_map/pallas_call | solution.py:622
  484.0 8.8 %convolution_convert_fusion = bf16[1536,2048]{1,0:T(8,128)(2,1)} fusion(bf16[1024,1536]{1,0:T(8,128)(2,1)S(1)} %copy-done.67, bf16[1024,2048]{1,0:T(8,128)(2,1)S(1)} %copy-done.118), kind=kOutput, calls=%fused_computation | convolution fusion | flops 6445596672 | bytes 13631488 | tf_op jit(solution)/shard_map/dot_general | solution.py:979
  506.3 20.0 %shard_map.267 = (f32[1024,640]{1,0:T(8,128)}, f32[1024,640]{1,0:T(8,128)}, bf16[1024,640]{1,0:T(8,128)(2,1)S(1)}, f32[8,640]{1,0:T(8,128)S(1)}) custom-call(s32[25]{0:T(128)S(1)} %concatenate.67.where.scalar_ref, bf16[640,256]{1,0:T(8,128)(2,1)S(1)} %bitcast.437, bf16[640,256]{1,0:T(8,128)(2,1)} %collective-permute-done.18.refs_1_, ...), custom_call_target="tpu_custom_call" | custom-call | tf_op jit(solution)/shard_map/pallas_call | solution.py:622
  527.3 24.8 %collective-permute-done.53 = bf16[256,3072]{1,0:T(8,128)(2,1)} collective-permute-done((bf16[256,3072]{1,0:T(8,128)(2,1)}, bf16[256,3072]{1,0:T(8,128)(2,1)}, u32[]{:S(2)}, u32[]{:S(2)}) %collective-permute-start.53) | collective-permute-done | bytes 1572896 | tf_op jit(solution)/shard_map/ppermute | solution.py:57
  560.3 6.5 fusion.2
  577.2 22.9 %shard_map.268 = (bf16[1024,640]{1,0:T(8,128)(2,1)S(1)}, f32[640,1280]{1,0:T(8,128)}, f32[16,640]{1,0:T(8,128)S(1)}, f32[16,640]{1,0:T(8,128)S(1)}) custom-call(f32[1024,640]{1,0:T(8,128)} %get-tuple-element.214.adj_ref, f32[1024,640]{1,0:T(8,128)} %get-tuple-element.215.tail_ref, f32[1,640]{1,0:T(1,128)S(1)} %broadcast_select_fusion.7.arrive_ref, ...), custom_call_target="tpu_custom_call" | custom-call | tf_op jit(solution)/shard_map/pallas_call | solution.py:414
  609.9 6.5 fusion.3
  623.1 12.1 %collective-permute-done.58 = bf16[640,256]{1,0:T(8,128)(2,1)S(1)} collective-permute-done((bf16[640,256]{1,0:T(8,128)(2,1)S(1)}, bf16[640,256]{1,0:T(8,128)(2,1)S(1)}, u32[]{:S(2)}, u32[]{:S(2)}) %collective-permute-start.58) | collective-permute-done | bytes 327712 | tf_op jit(solution)/shard_map/ppermute | solution.py:57
  636.0 11.1 %shard_map.269 = (bf16[256,2048]{1,0:T(8,128)(2,1)}, bf16[256,2048]{1,0:T(8,128)(2,1)}) custom-call(s32[25]{0:T(128)S(1)} %concatenate.67.where.scalar_ref, bf16[320,640]{1,0:T(8,128)(2,1)S(1)} %maximum_maximum_fusion.refs_0_, bf16[320,640]{1,0:T(8,128)(2,1)S(1)} %copy-done.17, bf16[320,640]{1,0:T(8,128)(2,1)S(1)} %copy-done.24, ...), custom_call_target="tpu_custom_call" | custom-call | tf_op jit(solution)/shard_map/pallas_call | solution.py:622
  673.2 11.0 %shard_map.270 = (bf16[256,2048]{1,0:T(8,128)(2,1)}, bf16[256,2048]{1,0:T(8,128)(2,1)}) custom-call(s32[25]{0:T(128)S(1)} %concatenate.67.where.scalar_ref, bf16[320,640]{1,0:T(8,128)(2,1)S(1)} %maximum_maximum_fusion.refs_0_, bf16[320,640]{1,0:T(8,128)(2,1)S(1)} %copy-done.18, bf16[320,640]{1,0:T(8,128)(2,1)S(1)} %copy-done.25, ...), custom_call_target="tpu_custom_call" | custom-call | tf_op jit(solution)/shard_map/pallas_call | solution.py:622
  723.3 9.8 %collective-permute-done.74 = bf16[96,320]{1,0:T(8,128)(2,1)S(1)} collective-permute-done((bf16[96,320]{1,0:T(8,128)(2,1)S(1)}, bf16[96,320]{1,0:T(8,128)(2,1)S(1)}, u32[]{:S(2)}, u32[]{:S(2)}) %collective-permute-start.74) | collective-permute-done | bytes 61472 | tf_op jit(solution)/shard_map/ppermute | solution.py:57
  744.4 8.2 %collective-permute-done.80 = bf16[256,1280]{1,0:T(8,128)(2,1)S(1)} collective-permute-done((bf16[256,1280]{1,0:T(8,128)(2,1)S(1)}, bf16[256,1280]{1,0:T(8,128)(2,1)S(1)}, u32[]{:S(2)}, u32[]{:S(2)}) %collective-permute-start.80) | collective-permute-done | bytes 655392 | tf_op jit(solution)/shard_map/ppermute | solution.py:57
  (665 shorter events, 375.8 us)
Async XLA Ops:
  7.2 343.0 %all-gather.2.cloned.1.call-start = ((), (), s32[]{:S(2)}) async-start(), calls=%async_computation.3 | async-start | bytes 14155776 | tf_op jit(solution)/shard_map/all_gather | solution.py:839
  74.7 29.7 %collective-permute-start.4 = (bf16[320,640]{1,0:T(8,128)(2,1)}, bf16[320,640]{1,0:T(8,128)(2,1)S(1)}, u32[]{:S(2)}, u32[]{:S(2)}) collective-permute-start(bf16[320,640]{1,0:T(8,128)(2,1)} %copy-done.22), channel_id=1, source_target_pairs={{4,0},{8,4},{12,8},{14,12},{10,14},{6,10},{2,6},{0,2},{5,1},{9,5},... | collective-permute-start | bytes 1228808 | tf_op jit(solution)/shard_map/ppermute | solution.py:57
  94.9 45.1 %collective-permute-start.10 = (bf16[160,640]{1,0:T(8,128)(2,1)}, bf16[160,640]{1,0:T(8,128)(2,1)}, u32[]{:S(2)}, u32[]{:S(2)}) collective-permute-start(bf16[160,640]{1,0:T(8,128)(2,1)} %slice.774), channel_id=1, source_target_pairs={{0,4},{4,8},{8,12},{12,14},{14,10},{10,6},{6,2},{2,0},{1,5},{5,9},... | collective-permute-start | bytes 614408 | tf_op jit(solution)/shard_map/ppermute | solution.py:57
  110.7 58.2 %collective-permute-start.17 = (bf16[640,256]{1,0:T(8,128)(2,1)}, bf16[640,256]{1,0:T(8,128)(2,1)}, u32[]{:S(2)}, u32[]{:S(2)}) collective-permute-start(bf16[640,256]{1,0:T(8,128)(2,1)} %bitcast.434), channel_id=1, source_target_pairs={{0,4},{4,8},{8,12},{12,14},{14,10},{10,6},{6,2},{2,0},{1,5},{5,9},... | collective-permute-start | bytes 983048 | tf_op jit(solution)/shard_map/ppermute | solution.py:57
  113.4 26.6 %collective-permute-start.15 = (bf16[128,640]{1,0:T(8,128)(2,1)}, bf16[128,640]{1,0:T(8,128)(2,1)}, u32[]{:S(2)}, u32[]{:S(2)}) collective-permute-start(bf16[128,640]{1,0:T(8,128)(2,1)} %slice.776), channel_id=1, source_target_pairs={{0,4},{4,8},{8,12},{12,14},{14,10},{10,6},{6,2},{2,0},{1,5},{5,9},... | collective-permute-start | bytes 491528 | tf_op jit(solution)/shard_map/ppermute | solution.py:57
  116.3 52.6 %collective-permute-start.18 = (bf16[640,256]{1,0:T(8,128)(2,1)}, bf16[640,256]{1,0:T(8,128)(2,1)}, u32[]{:S(2)}, u32[]{:S(2)}) collective-permute-start(bf16[640,256]{1,0:T(8,128)(2,1)} %bitcast.435), channel_id=1, source_target_pairs={{4,0},{8,4},{12,8},{14,12},{10,14},{6,10},{2,6},{0,2},{5,1},{9,5},... | collective-permute-start | bytes 983048 | tf_op jit(solution)/shard_map/ppermute | solution.py:57
  168.9 27.0 %collective-permute-start.20 = (bf16[640,256]{1,0:T(8,128)(2,1)}, bf16[640,256]{1,0:T(8,128)(2,1)}, u32[]{:S(2)}, u32[]{:S(2)}) collective-permute-start(bf16[640,256]{1,0:T(8,128)(2,1)} %collective-permute-done.17.refs_6_), channel_id=1, source_target_pairs={{0,4},{4,8},{8,12},{12,14},{14,10},{10,6},{6,2},{2,0},{1,5},{5,9},... | collective-permute-start | bytes 983048 | tf_op jit(solution)/shard_map/ppermute | solution.py:57
  195.3 27.2 %collective-permute-start.23 = (bf16[640,256]{1,0:T(8,128)(2,1)}, bf16[640,256]{1,0:T(8,128)(2,1)S(1)}, u32[]{:S(2)}, u32[]{:S(2)}) collective-permute-start(bf16[640,256]{1,0:T(8,128)(2,1)} %copy-done.72), channel_id=1, source_target_pairs={{4,0},{8,4},{12,8},{14,12},{10,14},{6,10},{2,6},{0,2},{5,1},{9,5},... | collective-permute-start | bytes 983048 | tf_op jit(solution)/shard_map/ppermute | solution.py:57
  195.9 27.6 %collective-permute-start.24 = (bf16[640,256]{1,0:T(8,128)(2,1)}, bf16[640,256]{1,0:T(8,128)(2,1)}, u32[]{:S(2)}, u32[]{:S(2)}) collective-permute-start(bf16[640,256]{1,0:T(8,128)(2,1)} %collective-permute-done.20.refs_5_), channel_id=1, source_target_pairs={{0,4},{4,8},{8,12},{12,14},{14,10},{10,6},{6,2},{2,0},{1,5},{5,9},... | collective-permute-start | bytes 983048 | tf_op jit(solution)/shard_map/ppermute | solution.py:57
  204.2 596.7 %reduce-scatter.2.cloned.1.call-start = ((), (), s32[]{:S(2)}) async-start(), calls=%async_computation.4 | async-start | bytes 7077888 | tf_op jit(solution)/shard_map/reduce_scatter | solution.py:1008
  249.9 41.4 %collective-permute-start.29 = (bf16[256,2048]{1,0:T(8,128)(2,1)S(1)}, bf16[256,2048]{1,0:T(8,128)(2,1)S(1)}, u32[]{:S(2)}, u32[]{:S(2)}) collective-permute-start(bf16[256,2048]{1,0:T(8,128)(2,1)S(1)} %get-tuple-element.186.refs_11_), channel_id=1, source_target_pairs={{0,1},{1,0},{2,3},{3,2},{4,5},{5,4},{6,7},{7,6},{8,9},{9,8},{10,11... | collective-permute-start | bytes 3145736 | tf_op jit(solution)/shard_map/ppermute | solution.py:137
  253.8 37.4 %collective-permute-start.30 = (bf16[256,2048]{1,0:T(8,128)(2,1)S(1)}, bf16[256,2048]{1,0:T(8,128)(2,1)S(1)}, u32[]{:S(2)}, u32[]{:S(2)}) collective-permute-start(bf16[256,2048]{1,0:T(8,128)(2,1)S(1)} %add_convert_fusion.2), channel_id=1, source_target_pairs={{0,16},{16,0},{1,17},{17,1},{2,18},{18,2},{3,19},{19,3},{4,20},{20... | collective-permute-start | bytes 3145736 | tf_op jit(solution)/shard_map/ppermute | solution.py:133
  256.6 34.1 %collective-permute-start.22 = (bf16[1536,256]{1,0:T(8,128)(2,1)S(1)}, bf16[1536,256]{1,0:T(8,128)(2,1)S(1)}, u32[]{:S(2)}, u32[]{:S(2)}) collective-permute-start(bf16[1536,256]{1,0:T(8,128)(2,1)S(1)} %copy-done.54), channel_id=1, source_target_pairs={{4,0},{8,4},{12,8},{14,12},{10,14},{6,10},{2,6},{0,2},{5,1},{9,5},... | collective-permute-start | bytes 2359304 | tf_op jit(solution)/shard_map/ppermute | solution.py:57
  258.3 32.9 %collective-permute-start.31 = (bf16[1536,256]{1,0:T(8,128)(2,1)S(1)}, bf16[1536,256]{1,0:T(8,128)(2,1)S(1)}, u32[]{:S(2)}, u32[]{:S(2)}) collective-permute-start(bf16[1536,256]{1,0:T(8,128)(2,1)S(1)} %copy-done.54), channel_id=1, source_target_pairs={{0,4},{4,8},{8,12},{12,14},{14,10},{10,6},{6,2},{2,0},{1,5},{5,9},... | collective-permute-start | bytes 2359304 | tf_op jit(solution)/shard_map/ppermute | solution.py:57
  295.8 24.8 %collective-permute-start.36 = (bf16[256,2048]{1,0:T(8,128)(2,1)S(1)}, bf16[256,2048]{1,0:T(8,128)(2,1)S(1)}, u32[]{:S(2)}, u32[]{:S(2)}) collective-permute-start(bf16[256,2048]{1,0:T(8,128)(2,1)S(1)} %get-tuple-element.191), channel_id=1, source_target_pairs={{0,16},{16,0},{1,17},{17,1},{2,18},{18,2},{3,19},{19,3},{4,20},{20... | collective-permute-start | bytes 3145736 | tf_op jit(solution)/shard_map/ppermute | solution.py:143
  299.6 45.0 %collective-permute-start.35 = (bf16[256,2048]{1,0:T(8,128)(2,1)S(1)}, bf16[256,2048]{1,0:T(8,128)(2,1)S(1)}, u32[]{:S(2)}, u32[]{:S(2)}) collective-permute-start(bf16[256,2048]{1,0:T(8,128)(2,1)S(1)} %get-tuple-element.191), channel_id=1, source_target_pairs={{0,1},{1,0},{2,3},{3,2},{4,5},{5,4},{6,7},{7,6},{8,9},{9,8},{10,11... | collective-permute-start | bytes 3145736 | tf_op jit(solution)/shard_map/ppermute | solution.py:144
  346.9 27.2 %collective-permute-start.38 = (bf16[768,256]{1,0:T(8,128)(2,1)}, bf16[768,256]{1,0:T(8,128)(2,1)}, u32[]{:S(2)}, u32[]{:S(2)}) collective-permute-start(bf16[768,256]{1,0:T(8,128)(2,1)} %slice.823), channel_id=1, source_target_pairs={{0,4},{4,8},{8,12},{12,14},{14,10},{10,6},{6,2},{2,0},{1,5},{5,9},... | collective-permute-start | bytes 1179656 | tf_op jit(solution)/shard_map/ppermute | solution.py:57
  410.7 30.6 %collective-permute-start.42 = (bf16[256,2048]{1,0:T(8,128)(2,1)}, bf16[256,2048]{1,0:T(8,128)(2,1)}, u32[]{:S(2)}, u32[]{:S(2)}) collective-permute-start(bf16[256,2048]{1,0:T(8,128)(2,1)} %add_convert_fusion.1), channel_id=1, source_target_pairs={{0,16},{16,0},{1,17},{17,1},{2,18},{18,2},{3,19},{19,3},{4,20},{20... | collective-permute-start | bytes 3145736 | tf_op jit(solution)/shard_map/ppermute | solution.py:133
  433.2 39.0 %collective-permute-start.49 = (bf16[256,3072]{1,0:T(8,128)(2,1)}, bf16[256,3072]{1,0:T(8,128)(2,1)}, u32[]{:S(2)}, u32[]{:S(2)}) collective-permute-start(bf16[256,3072]{1,0:T(8,128)(2,1)} %pad_maximum_fusion.3), channel_id=1, source_target_pairs={{0,4},{4,8},{8,12},{12,14},{14,10},{10,6},{6,2},{2,0},{1,5},{5,9},... | collective-permute-start | bytes 4718600 | tf_op jit(solution)/shard_map/ppermute | solution.py:57
  438.6 39.1 %collective-permute-start.52 = (bf16[256,3072]{1,0:T(8,128)(2,1)}, bf16[256,3072]{1,0:T(8,128)(2,1)}, u32[]{:S(2)}, u32[]{:S(2)}) collective-permute-start(bf16[256,3072]{1,0:T(8,128)(2,1)} %pad_maximum_fusion.4), channel_id=1, source_target_pairs={{4,0},{8,4},{12,8},{14,12},{10,14},{6,10},{2,6},{0,2},{5,1},{9,5},... | collective-permute-start | bytes 4718600 | tf_op jit(solution)/shard_map/ppermute | solution.py:57
  449.0 34.9 %collective-permute-start.46 = (bf16[256,2048]{1,0:T(8,128)(2,1)}, bf16[256,2048]{1,0:T(8,128)(2,1)}, u32[]{:S(2)}, u32[]{:S(2)}) collective-permute-start(bf16[256,2048]{1,0:T(8,128)(2,1)} %get-tuple-element.210), channel_id=1, source_target_pairs={{0,16},{16,0},{1,17},{17,1},{2,18},{18,2},{3,19},{19,3},{4,20},{20... | collective-permute-start | bytes 3145736 | tf_op jit(solution)/shard_map/ppermute | solution.py:143
  450.4 42.4 %collective-permute-start.45 = (bf16[256,2048]{1,0:T(8,128)(2,1)}, bf16[256,2048]{1,0:T(8,128)(2,1)}, u32[]{:S(2)}, u32[]{:S(2)}) collective-permute-start(bf16[256,2048]{1,0:T(8,128)(2,1)} %get-tuple-element.210), channel_id=1, source_target_pairs={{0,1},{1,0},{2,3},{3,2},{4,5},{5,4},{6,7},{7,6},{8,9},{9,8},{10,11... | collective-permute-start | bytes 3145736 | tf_op jit(solution)/shard_map/ppermute | solution.py:144
  469.4 28.1 %collective-permute-start.43 = (bf16[1024,1024]{1,0:T(8,128)(2,1)}, bf16[1024,1024]{1,0:T(8,128)(2,1)}, u32[]{:S(2)}, u32[]{:S(2)}) collective-permute-start(bf16[1024,1024]{1,0:T(8,128)(2,1)} %slice.826), channel_id=1, source_target_pairs={{0,1},{1,0},{2,3},{3,2},{4,5},{5,4},{6,7},{7,6},{8,9},{9,8},{10,11... | collective-permute-start | bytes 6291464 | tf_op jit(solution)/shard_map/ppermute | solution.py:1023
  476.8 50.5 %collective-permute-start.50 = (bf16[256,3072]{1,0:T(8,128)(2,1)}, bf16[256,3072]{1,0:T(8,128)(2,1)}, u32[]{:S(2)}, u32[]{:S(2)}) collective-permute-start(bf16[256,3072]{1,0:T(8,128)(2,1)} %fusion), channel_id=1, source_target_pairs={{0,4},{4,8},{8,12},{12,14},{14,10},{10,6},{6,2},{2,0},{1,5},{5,9},... | collective-permute-start | bytes 4718600 | tf_op jit(solution)/shard_map/ppermute | solution.py:57
  482.7 69.4 %collective-permute-start.53 = (bf16[256,3072]{1,0:T(8,128)(2,1)}, bf16[256,3072]{1,0:T(8,128)(2,1)}, u32[]{:S(2)}, u32[]{:S(2)}) collective-permute-start(bf16[256,3072]{1,0:T(8,128)(2,1)} %fusion.1), channel_id=1, source_target_pairs={{4,0},{8,4},{12,8},{14,12},{10,14},{6,10},{2,6},{0,2},{5,1},{9,5},... | collective-permute-start | bytes 4718600 | tf_op jit(solution)/shard_map/ppermute | solution.py:57
  503.1 150.6 %collective-permute-start.44 = (bf16[1024,512]{1,0:T(8,128)(2,1)}, bf16[1024,512]{1,0:T(8,128)(2,1)}, u32[]{:S(2)}, u32[]{:S(2)}) collective-permute-start(bf16[1024,512]{1,0:T(8,128)(2,1)} %fusion.8), channel_id=1, source_target_pairs={{0,16},{16,0},{1,17},{17,1},{2,18},{18,2},{3,19},{19,3},{4,20},{20... | collective-permute-start | bytes 3145736 | tf_op jit(solution)/shard_map/ppermute | solution.py:1024
  609.8 25.3 %collective-permute-start.58 = (bf16[640,256]{1,0:T(8,128)(2,1)S(1)}, bf16[640,256]{1,0:T(8,128)(2,1)S(1)}, u32[]{:S(2)}, u32[]{:S(2)}) collective-permute-start(bf16[640,256]{1,0:T(8,128)(2,1)S(1)} %pad_maximum_fusion.8), channel_id=1, source_target_pairs={{4,0},{8,4},{12,8},{14,12},{10,14},{6,10},{2,6},{0,2},{5,1},{9,5},... | collective-permute-start | bytes 983048 | tf_op jit(solution)/shard_map/ppermute | solution.py:57
  616.4 56.7 %collective-permute-start.61 = (bf16[256,3072]{1,0:T(8,128)(2,1)}, bf16[256,3072]{1,0:T(8,128)(2,1)}, u32[]{:S(2)}, u32[]{:S(2)}) collective-permute-start(bf16[256,3072]{1,0:T(8,128)(2,1)} %fusion.3), channel_id=1, source_target_pairs={{4,0},{8,4},{12,8},{14,12},{10,14},{6,10},{2,6},{0,2},{5,1},{9,5},... | collective-permute-start | bytes 4718600 | tf_op jit(solution)/shard_map/ppermute | solution.py:57
  616.9 56.2 %collective-permute-start.60 = (bf16[256,3072]{1,0:T(8,128)(2,1)}, bf16[256,3072]{1,0:T(8,128)(2,1)}, u32[]{:S(2)}, u32[]{:S(2)}) collective-permute-start(bf16[256,3072]{1,0:T(8,128)(2,1)} %fusion.2), channel_id=1, source_target_pairs={{0,4},{4,8},{8,12},{12,14},{14,10},{10,6},{6,2},{2,0},{1,5},{5,9},... | collective-permute-start | bytes 4718600 | tf_op jit(solution)/shard_map/ppermute | solution.py:57
  661.9 46.6 %collective-permute-start.63 = (bf16[256,2048]{1,0:T(8,128)(2,1)}, bf16[256,2048]{1,0:T(8,128)(2,1)S(1)}, u32[]{:S(2)}, u32[]{:S(2)}) collective-permute-start(bf16[256,2048]{1,0:T(8,128)(2,1)} %add_convert_fusion), channel_id=1, source_target_pairs={{0,16},{16,0},{1,17},{17,1},{2,18},{18,2},{3,19},{19,3},{4,20},{20... | collective-permute-start | bytes 3145736 | tf_op jit(solution)/shard_map/ppermute | solution.py:133
  669.8 25.9 %collective-permute-start.72 = (bf16[96,320]{1,0:T(8,128)(2,1)S(1)}, bf16[96,320]{1,0:T(8,128)(2,1)S(1)}, u32[]{:S(2)}, u32[]{:S(2)}) collective-permute-start(bf16[96,320]{1,0:T(8,128)(2,1)S(1)} %pad_maximum_fusion.9), channel_id=1, source_target_pairs={{0,4},{4,8},{8,12},{12,14},{14,10},{10,6},{6,2},{2,0},{1,5},{5,9},... | collective-permute-start | bytes 184328 | tf_op jit(solution)/shard_map/ppermute | solution.py:57
  759.1 31.2 %collective-permute-start.68 = (bf16[256,2048]{1,0:T(8,128)(2,1)S(1)}, bf16[256,2048]{1,0:T(8,128)(2,1)}, u32[]{:S(2)}, u32[]{:S(2)}) collective-permute-start(bf16[256,2048]{1,0:T(8,128)(2,1)S(1)} %shard_map.271.a_ref), channel_id=1, source_target_pairs={{0,1},{1,0},{2,3},{3,2},{4,5},{5,4},{6,7},{7,6},{8,9},{9,8},{10,11... | collective-permute-start | bytes 3145736 | tf_op jit(solution)/shard_map/ppermute | solution.py:144
  (198 other events, 3067.8 us)
Sparse Core Ops, SparseCore 0:
  61.6 229.0 all-gather.1
  492.9 158.5 reduce-scatter.1

commit v3 on v2

--- a/solution.py
+++ b/solution.py
@@ -2,6 +2,7 @@
 
 import jax
 import jax.numpy as jnp
+import numpy as np
 from jax import lax
 from jax.experimental import pallas as pl
 from jax.experimental.pallas import tpu as pltpu
@@ -135,6 +136,30 @@
     def first(self, mine, others):
         self.own = mine
         self.core = lax.ppermute(others, "ch", SWAP)
+
+
+class GroupSum:
+    def __init__(self, part):
+        self.half = part.shape[0] // 2
+        core = lax.axis_index("ch")
+        self.own = lax.dynamic_slice_in_dim(part, core * self.half, self.half, 0)
+        theirs = lax.dynamic_slice_in_dim(part, (1 - core) * self.half, self.half, 0)
+        self.got = lax.ppermute(theirs, "ch", SWAP)
+
+    def chip(self, *others):
+        got = after(self.got, *others) if others else self.got
+        self.chip_sum = (self.own.astype(F32) + got.astype(F32)).astype(BF16)
+        return self.chip_sum
+
+    def cross(self, *others):
+        x = after(self.chip_sum, *others) if others else self.chip_sum
+        self.far = lax.ppermute(x, "br", SWAP)
+
+    def total(self, *others):
+        far = after(self.far, *others) if others else self.far
+        self.mine = (self.chip_sum.astype(F32) + far.astype(F32)).astype(BF16)
+        self.other = lax.ppermute(self.mine, "ch", SWAP)
+        return self.mine
 
 
 class TokenGather:
@@ -368,10 +393,8 @@
             edge_ref[8:16, own] = dz[rows - 8 :]
 
 
-def kernel_params():
-    return pltpu.CompilerParams(
-        dimension_semantics=("arbitrary",), vmem_limit_bytes=48 * 1024 * 1024
-    )
+def kernel_params(mib=48):
+    return pltpu.CompilerParams(dimension_semantics=("arbitrary",), vmem_limit_bytes=mib * 1024 * 1024)
 
 
 def forward_local(z, rim, mask, conv, wide, bias, rate):
@@ -400,9 +423,10 @@
     )(z, rim, mask, conv, wide, bias, rate)
 
 
-def backward_local(adj, tail, arrive, loc, prod, enter, gate, unit, mask, z, rim, conv, wide, rate):
+def backward_local(adj, tail, arrive, loc, prod, enter, gate, unit, mask, z, rim, conv, wide, rate, first_rows=0):
     tokens, channels = loc.shape
-    rows = min(ROWS, tokens)
+    rows = first_rows or min(ROWS, tokens)
+    tokens = first_rows or tokens
     last = tokens // rows - 1
     whole = lambda x: pl.BlockSpec(x.shape, lambda i: (0,) * x.ndim)
     time = lambda width, at=0: pl.BlockSpec((rows, width), lambda i: (last - i, at))
@@ -457,6 +481,99 @@
         h_ref[:, own] = (x_ref[:, true] * rstd * gain_ref[:, own]).astype(BF16)
 
 
+def first_norm_kernel(count, row, where, x_ref, *refs):
+    parts, h_ref, gain_ref = refs[:count], refs[count], refs[count + 1]
+    width = x_ref.shape[1]
+    cols = width // count
+    x = x_ref[...]
+    rstd = lax.rsqrt(jnp.sum(x * x, axis=1, keepdims=True) * (1.0 / width) + NORM_EPS)
+    for part, (own, true) in zip(parts, pieces_of(width, where, count)):
+        gain = part[row : row + 1, 0:cols].astype(F32)
+        h_ref[:, own] = (x_ref[:, true] * rstd * gain).astype(BF16)
+        gain_ref[0:1, own] = gain
+        gain_ref[1:2, own] = part[row : row + 1, cols : 2 * cols].astype(F32)
+
+
+def first_norm_call(count, where, x, parts, part_rows, row):
+    tokens, width = x.shape
+    rows = min(ROWS, tokens)
+    time = pl.BlockSpec((rows, width), lambda i, w: (i, 0))
+    fixed = lambda shape: pl.BlockSpec(shape, lambda i, w: (0, 0))
+    return pl.pallas_call(
+        functools.partial(first_norm_kernel, count, row),
+        grid_spec=pltpu.PrefetchScalarGridSpec(
+            num_scalar_prefetch=1,
+            grid=(tokens // rows,),
+            in_specs=[time] + [fixed((part_rows, p.shape[1])) for p in parts],
+            out_specs=[time, fixed((8, width))],
+        ),
+        out_shape=[jax.ShapeDtypeStruct((tokens, width), BF16), jax.ShapeDtypeStruct((8, width), F32)],
+        compiler_params=kernel_params(),
+        cost_estimate=COST,
+    )(where, x, *parts)
+
+
+def prepare_kernel(count, gates, part_ch, taps, cols, *refs):
+    parts, (row_ref, head_ref, code_ref, col_ref, hot_ref, wide_ref, chan_ref, small) = refs[:count], refs[count:]
+    channels = wide_ref.shape[0]
+    stacked = jnp.concatenate([p[0:gates].astype(F32) for p in parts], axis=0).astype(BF16)
+    inside = head_ref[...] == col_ref[0:1]
+    for g in range(2):
+        hot = (row_ref[...] == code_ref[g : g + 1]).astype(F32).astype(BF16)
+        placed = jnp.dot(hot, stacked, preferred_element_type=F32)
+        wide_ref[:, g * channels : (g + 1) * channels] = jnp.where(inside, placed, 0.0).astype(BF16)
+    for k, part in enumerate(parts):
+        small[k : k + 1] = part[gates : gates + 1].astype(F32)
+        small[count + k : count + k + 1] = part[gates + 1 : gates + 2].astype(F32)
+    ordered = [
+        jnp.dot(hot_ref[...], small[s * count : (s + 1) * count].astype(BF16), preferred_element_type=F32).astype(BF16)
+        for s in range(2)
+    ]
+    lane = lax.broadcasted_iota(jnp.int32, (channels, channels), 0)
+    seq = lax.broadcasted_iota(jnp.int32, (count, channels), 0)
+    wanted = [(1, y * part_ch) for y in range(taps + 3)] + [(0, 2 * cols)]
+    for y, (s, offset) in enumerate(wanted):
+        hot = (lane == col_ref[1:2] + offset).astype(F32).astype(BF16)
+        spread = jnp.dot(ordered[s], hot, preferred_element_type=F32)
+        chan_ref[y : y + 1] = jnp.sum(jnp.where(seq == col_ref[2:3], spread, 0.0), axis=0, keepdims=True)
+
+
+def prepare_call(parts, true_all, place_hot, part_rows, part_in, block, part_ch, taps, cols):
+    count = len(parts)
+    channels = parts[0].shape[1]
+    gates = 2 * part_in
+    at = np.arange(channels)
+    row_code = jnp.asarray((at % block // part_in * part_in + at % part_in)[:, None], jnp.int32)
+    row_head = jnp.asarray((at // block)[:, None], jnp.int32)
+    col = jnp.asarray(np.stack([at // block, at % part_ch, at // part_ch]), jnp.int32)
+    code = true_all[:, None] * part_in + jnp.arange(part_in, dtype=jnp.int32)[None, :]
+    none = jnp.full_like(code, -1)
+    code = jnp.stack(
+        [
+            jnp.concatenate([code, none], axis=1).reshape(-1),
+            jnp.concatenate([none, code], axis=1).reshape(-1),
+        ]
+    )
+    whole = lambda x: pl.BlockSpec(x.shape, lambda i: (0, 0))
+    args = (row_code, row_head, code, col, place_hot)
+    return pl.pallas_call(
+        functools.partial(prepare_kernel, count, gates, part_ch, taps, cols),
+        grid=(1,),
+        in_specs=[pl.BlockSpec((part_rows, channels), lambda i: (0, 0)) for _ in parts] + [whole(a) for a in args],
+        out_specs=[
+            pl.BlockSpec((channels, 2 * channels), lambda i: (0, 0)),
+            pl.BlockSpec((taps + 4, channels), lambda i: (0, 0)),
+        ],
+        out_shape=[
+            jax.ShapeDtypeStruct((channels, 2 * channels), BF16),
+            jax.ShapeDtypeStruct((taps + 4, channels), F32),
+        ],
+        scratch_shapes=[pltpu.VMEM((2 * count, channels), F32)],
+        compiler_params=kernel_params(),
+        cost_estimate=COST,
+    )(*parts, *args)
+
+
 def low_kernel(count, where, x_ref, low_ref, true_ref):
     true_ref[...] = x_ref[...].astype(BF16)
     for own, true in pieces_of(x_ref.shape[1], where, count):
@@ -494,27 +611,24 @@
         low_ref[:, own] = d_resid.astype(BF16)
 
 
-def norm_one_back_kernel(count, where, x_ref, a_ref, b_ref, c_ref, gain_ref, d_resid_ref, out_ref, kept):
+def pick(where, mine_ref, other_ref, own, per):
+    is_mine = (pl.program_id(0) // per) == where[where.shape[0] - 1]
+    return jnp.where(is_mine, mine_ref[:, own], other_ref[:, own]).astype(F32)
+
+
+def norm_one_whole_kernel(count, per, where, x_ref, mine_ref, other_ref, gain_ref, d_resid_ref, *refs):
+    out_ref = refs[-1]
     width = x_ref.shape[1]
     x = x_ref[...]
     rstd = lax.rsqrt(jnp.sum(x * x, axis=1, keepdims=True) * (1.0 / width) + NORM_EPS)
     along = 0.0
     for own, true in pieces_of(width, where, count):
-        d_normed = summed((a_ref, b_ref, c_ref), own) * gain_ref[:, own]
-        kept[:, own] = d_normed
+        d_normed = pick(where, mine_ref, other_ref, own, per) * gain_ref[:, own]
         along = along + jnp.sum(d_normed * x_ref[:, true], axis=1, keepdims=True)
     along = along * rstd * (1.0 / width)
     for own, true in pieces_of(width, where, count):
-        out = d_resid_ref[:, own] + rstd * (kept[:, own] - x_ref[:, true] * rstd * along)
-        out_ref[:, true] = out.astype(BF16)
-
-
-def spread_kernel(count, where, a_ref, b_ref, c_ref, d_ref, out_ref):
-    for slot, ref in enumerate((a_ref, b_ref, c_ref, d_ref)):
-
-        @pl.when(where[count + 4 + pl.program_id(0)] == slot)
-        def _():
-            out_ref[...] = ref[...].astype(F32)
+        d_normed = pick(where, mine_ref, other_ref, own, per) * gain_ref[:, own]
+        out_ref[:, true] = d_resid_ref[:, own].astype(F32) + rstd * (d_normed - x_ref[:, true] * rstd * along)
 
 
 def norm_call(kernel, count, where, x, gain, outputs=1, slots=False):
@@ -560,21 +674,30 @@
     )(where, *args)
 
 
-def spread_call(count, where, parts):
-    rows, width = parts[0].shape
-    whole = pl.BlockSpec((rows, width), lambda i, w: (0, 0))
+def sum_call(kernel, count, where, summed, x, gain, extra, out_types):
+    tokens, width = x.shape
+    rows = min(ROWS, tokens // 4)
+    per = tokens // 2 // rows
+    last = where.shape[0] - 1
+    time = pl.BlockSpec((rows, width), lambda i, w: (i, 0))
+    each = tokens // 4 // rows
+    slot = pl.BlockSpec((rows, width), lambda i, w: (w[count + 4 + i // each] * each + i % each, 0))
+    mine = pl.BlockSpec((rows, width), lambda i, w: (jnp.clip(i - w[last] * per, 0, per - 1), 0))
+    other = pl.BlockSpec((rows, width), lambda i, w: (jnp.clip(i - (1 - w[last]) * per, 0, per - 1), 0))
+    args = (x, summed.mine, summed.other, gain) + extra
+    gain_spec = pl.BlockSpec(gain.shape, lambda i, w: (0, 0))
     return pl.pallas_call(
-        functools.partial(spread_kernel, count),
+        functools.partial(kernel, count, per),
         grid_spec=pltpu.PrefetchScalarGridSpec(
             num_scalar_prefetch=1,
-            grid=(4,),
-            in_specs=[whole] * 4,
-            out_specs=pl.BlockSpec((rows, width), lambda i, w: (i, 0)),
+            grid=(tokens // rows,),
+            in_specs=[time, mine, other, gain_spec] + [slot] * len(extra),
+            out_specs=[time] * len(out_types),
         ),
-        out_shape=jax.ShapeDtypeStruct((4 * rows, width), F32),
+        out_shape=[jax.ShapeDtypeStruct((tokens, width), t) for t in out_types],
         compiler_params=kernel_params(),
         cost_estimate=COST,
-    )(where, *parts)
+    )(where, *args)
 
 
 def weight_call(
@@ -630,19 +753,20 @@
         ),
         out_shape=out_shape,
         input_output_aliases={first + i: i for i in range(len(earlier))},
-        compiler_params=kernel_params(),
+        compiler_params=kernel_params(60 if count > 12 else 48),
         cost_estimate=COST,
     )(scalars, *[array for array, _ in pieces], *inputs, *fixed, *earlier)
 
 
-def row_pieces(ring_gather, cols, lane=lambda s: slice(None)):
+def row_pieces(ring_gather, cols, lane, skip=0):
     out = []
     for array, k, half in ring_gather.pieces():
         first = array.shape[0] if half == 1 else 0
-        size = min(array.shape[0], cols - first)
+        begin = max(skip - first, 0)
+        size = array.shape[0] - begin
         if size > 0:
-            place = lambda s, start=k * cols + first, size=size: [
-                ((pl.ds(0, size),), (pl.ds(start, size), lane(s)))
+            place = lambda s, begin=begin, start=k * cols + first + begin - skip, size=size: [
+                ((pl.ds(begin, size),), (pl.ds(start, size), lane(s)))
             ]
             out.append((array, place))
     return out
@@ -730,11 +854,11 @@
     out_ref[:, units:] = (d_hidden * act_ref[...].astype(F32)).astype(BF16)
 
 
-def d_h_one_body(where, weight, dzg_ref, dzr_ref, *out_refs):
+def d_h_one_body(where, weight, dzg_ref, dzr_ref, out_ref):
     channels = dzg_ref.shape[1]
     gate = lax.dot_general(dzg_ref[...], weight[:, :channels], NT, preferred_element_type=F32)
     rec = lax.dot_general(dzr_ref[...], weight[:, channels:], NT, preferred_element_type=F32)
-    to_quarter(pl.program_id(0), out_refs, gate + rec)
+    out_ref[...] = (gate + rec).astype(BF16)
 
 
 def per_device(
@@ -787,44 +911,39 @@
     whole_inputs = inputs
     if aligned:
         n_pieces = count
-        where = jnp.concatenate([true_all, quarters, slots, dealt, br[None]]).astype(jnp.int32)
+        where = jnp.concatenate([true_all, quarters, slots, dealt, br[None], ch[None]]).astype(jnp.int32)
     else:
         n_pieces = 1
         zero = jnp.zeros((1,), jnp.int32)
-        where = jnp.concatenate([zero, quarters, slots, zero, br[None]]).astype(jnp.int32)
+        where = jnp.concatenate([zero, quarters, slots, zero, br[None], ch[None]]).astype(jnp.int32)
         inputs, cotangent = move(inputs, true_of), move(cotangent, true_of)
 
     ring = Ring(count)
 
-    small = jnp.concatenate(
+    fold = 2 * block
+    gate_rows = heads * part_in
+    packed_gates = 2 * part_in
+
+    def one_row(*arrays):
+        row = jnp.concatenate([a.reshape(-1) for a in arrays])
+        return jnp.pad(row, (0, channels - row.shape[0]))[None]
+
+    packed = jnp.concatenate(
         [
-            norm_gain1,
-            norm_gain2,
-            conv_weight.reshape(-1),
-            conv_bias.reshape(-1),
-            gate_bias.reshape(-1),
-            decay_param.reshape(-1),
-        ]
-    )
-    fold = 2 * block
-    small_rows = -(-small.shape[0] // fold)
-    small = jnp.pad(small, (0, small_rows * fold - small.shape[0])).reshape(small_rows, fold)
-    gate_rows = heads * part_in
-    packed = jnp.concatenate(
-        [gate_weight[:, 0, 0].transpose(1, 2, 0, 3).reshape(gate_rows, fold), small], axis=0
-    )
-    packed = pad_rows(packed, -(-packed.shape[0] // 32) * 32)
-    packed_rows = packed.shape[0] * fold // channels
-    packed_shape = packed.shape
+            gate_weight[:, 0, 0].transpose(0, 2, 1, 3).reshape(packed_gates, channels),
+            one_row(norm_gain1, norm_gain2, decay_param),
+            one_row(conv_weight, conv_bias, gate_bias),
+        ],
+        axis=0,
+    )
+    packed_rows = -(-(cols + packed.shape[0]) // 32) * 32 - cols
+    packed = pad_rows(packed, packed_rows)
 
     own_cols = lax.dynamic_slice_in_dim(in_weight[0], br * channels, channels, 1)
     far_cols = lax.ppermute(
         lax.dynamic_slice_in_dim(in_weight[0], (1 - br) * channels, channels, 1), "br", SWAP
     )
-    extra_rows = -(-(cols + packed_rows) // 32) * 32 - cols - packed_rows
-    own_and_packed = jnp.concatenate(
-        [own_cols, packed.reshape(packed_rows, channels), jnp.zeros((extra_rows, channels), BF16)], axis=0
-    )
+    own_and_packed = jnp.concatenate([packed, own_cols], axis=0)
     in_own, in_far = Gather(ring, own_and_packed), Gather(ring, far_cols)
     out_ring = Gather(ring, out_weight[0, 0])
     down_ring = Gather(ring, mlp_down)
@@ -834,11 +953,10 @@
     in_own.hop()
     in_far.hop()
     own_second, far_second = in_own.last, in_far.last
-    in_own.hop()
-    in_far.hop()
-    mlp_all = lax.all_gather(after(mlp_in, *in_far.last), "seq", axis=1, tiled=True)
-    in_own.hop()
-    in_far.hop()
+    for _ in range(2):
+        in_own.hop()
+        in_far.hop()
+    mlp_all = lax.all_gather(after(mlp_in, *in_own.last, *in_far.last), "seq", axis=1, tiled=True)
     out_ring.hop()
 
     doc_starts = jnp.cumsum(lengths) - lengths
@@ -850,23 +968,12 @@
     reset = jnp.any(positions[span:, None] == doc_starts[None, :], axis=1).astype(F32)
     mask = jnp.stack(lags + [reset], axis=1)
 
-    packed_all = [part[cols : cols + packed_rows].reshape(packed_shape) for part in in_own.parts]
-    small_all = jnp.stack([part[gate_rows : gate_rows + small_rows].reshape(-1) for part in packed_all])
-    gain_one = small_all[:, :cols].astype(F32).reshape(1, width)
-    gain_two = small_all[:, cols : 2 * cols].astype(F32).reshape(1, width)
     place_hot = (ring_index[:, None] == jnp.arange(count)[None, :]).astype(BF16)
-    chan = jnp.dot(place_hot, small_all[:, 2 * cols :], preferred_element_type=F32)
-    chan = chan[:, : (taps + 4) * part_ch].reshape(count, taps + 4, part_ch)
-    chan = chan.transpose(1, 0, 2).reshape(taps + 4, channels)
-    conv = chan[: taps + 1]
-    gate_bias_all = chan[taps + 1 : taps + 3].reshape(1, 2 * channels)
-    decay_rate = chan[taps + 3 : taps + 4]
-    rate = -DECAY_SCALE * jax.nn.softplus(-decay_rate)
-
-    stacked = jnp.concatenate([part[:gate_rows] for part in packed_all], axis=0)
     row = jnp.arange(channels)
     row_head, row_in = row // block, row % block
-    source = ring_index[row_in // part_in] * gate_rows + row_head * part_in + row_in % part_in
+    row_seq = row_in // part_in
+    row_place = (jnp.where(row_seq % 2 == 0, row_seq // 2, count - 1 - row_seq // 2) - place) % count
+    source = row_place * gate_rows + row_head * part_in + row_in % part_in
     row_hot = (source[:, None] == jnp.arange(channels)[None, :]).astype(BF16)
     wide_col = jnp.arange(2 * channels)
     wide_gate, wide_head, wide_out = (
@@ -876,13 +983,19 @@
     )
     spread_hot = (jnp.arange(fold)[:, None] == (wide_gate * block + wide_out)[None, :]).astype(BF16)
     on_block = (row_head[:, None] == wide_head[None, :]).astype(BF16)
-    compact = jnp.dot(row_hot, stacked, preferred_element_type=F32).astype(BF16)
-    wide = jnp.dot(compact, spread_hot, preferred_element_type=F32).astype(BF16) * on_block
-
-    (h_one,) = norm_call(norm_one_kernel, n_pieces, where, inputs, gain_one)
     scalars = where
-    last_at = where.shape[0] - 1
-    in_pieces = row_pieces(in_own, cols, lambda s: pl.ds(pl.multiple_of(s[last_at] * channels, LANES), channels))
+    last_at = where.shape[0] - 2
+    firsts = [in_own.last[0] if k == count // 2 else in_own.parts[k] for k in range(count)]
+    if aligned:
+        h_one, gains = first_norm_call(n_pieces, where, inputs, firsts, packed_rows, packed_gates)
+        gain_one, gain_two = gains[0:1], gains[1:2]
+    else:
+        rows = jnp.stack([part[packed_gates] for part in firsts]).astype(F32)
+        gain_one, gain_two = rows[:, :cols].reshape(1, width), rows[:, cols : 2 * cols].reshape(1, width)
+        (h_one,) = norm_call(norm_one_kernel, n_pieces, where, inputs, gain_one)
+    in_pieces = row_pieces(
+        in_own, cols, lambda s: pl.ds(pl.multiple_of(s[last_at] * channels, LANES), channels), packed_rows
+    )
     in_pieces += row_pieces(
         in_far, cols, lambda s: pl.ds(pl.multiple_of((1 - s[last_at]) * channels, LANES), channels)
     )
@@ -890,12 +1003,30 @@
     (z_last,) = weight_call(
         product_body, in_pieces, in_shape, 16, (h_one[tokens - 16 :],), (), [(2 * channels, BF16)], scalars
     )
+    if aligned:
+        wide, chan = prepare_call(
+            [after(firsts[0], z_last)] + firsts[1:], true_all, place_hot, packed_rows, part_in, block, part_ch, taps, cols
+        )
+    else:
+        rows = jnp.stack([part[packed_gates : packed_gates + 2] for part in firsts])
+        chan = jnp.concatenate([rows[:, 1, : (taps + 3) * part_ch], rows[:, 0, 2 * cols : 2 * cols + part_ch]], axis=1)
+        chan = jnp.dot(place_hot, chan, preferred_element_type=F32).reshape(count, taps + 4, part_ch)
+        chan = chan.transpose(1, 0, 2).reshape(taps + 4, channels)
+        every = jnp.stack([part[:packed_gates].reshape(-1) for part in firsts])
+        every = jnp.dot(place_hot, every, preferred_element_type=F32).astype(BF16)
+        every = every.reshape(count, 2, part_in, heads, block).transpose(3, 0, 2, 1, 4)
+        wide = every[:, :, :, :, None, :] * jnp.eye(heads, dtype=BF16)[:, None, None, None, :, None]
+        wide = wide.reshape(channels, 2 * channels)
+    conv = chan[: taps + 1]
+    gate_bias_all = chan[taps + 1 : taps + 3].reshape(1, 2 * channels)
+    decay_rate = chan[taps + 3 : taps + 4]
+    rate = -DECAY_SCALE * jax.nn.softplus(-decay_rate)
     forward_pairs = [(i, i + 1) for i in range(count - 1)]
     rim = lax.ppermute(z_last[8:, channels:], "seq", forward_pairs).astype(F32)
     (z,) = weight_call(
         product_body, in_pieces, in_shape, quarter, (after(h_one, z_last),), (), [(2 * channels, BF16)], scalars
     )
-    ring.mark = (z, rim)
+    ring.mark = (z, rim, wide)
     out_first = out_ring.last
     out_ring.hop()
 
@@ -1004,8 +1135,6 @@
     ring.mark = (part[0],)
     g_mlp.hop()
     mlp_hop.append(g_mlp.last)
-    g_down_part = outer(after(hidden, part[0], *g_mlp.last), slot_cot).astype(BF16)
-    g_down = lax.psum_scatter(g_down_part, "seq", scatter_dimension=1, tiled=True)
     d_resid, d_attn = own_call(
         norm_two_back_kernel, n_pieces, where, cotangent, d_h_two, gain_two, (resid,), (F32, BF16)
     )
@@ -1020,11 +1149,6 @@
         at = jnp.arange(count)
         o_part = move(o_part, [jnp.sum(jnp.where(dealt == k, at, 0)) for k in range(count)])
     o_cols = width // 4
-    swapped = lax.ppermute(o_part[:, 2 * o_cols :], "ch", SWAP).astype(F32)
-    o_far = lax.ppermute((o_part[:, o_cols : 2 * o_cols].astype(F32) + swapped[:, o_cols:]).astype(BF16), "br", SWAP)
-    o_inputs = lax.dynamic_slice_in_dim(whole_inputs, (br * 2 + ch) * o_cols, o_cols, 1)
-    output = o_inputs + o_part[:, :o_cols].astype(F32) + swapped[:, :o_cols] + o_far.astype(F32)
-
     ring.mark = (d_attn.own,)
     mlp_first = mlp_hop[1]
     g_mlp.hop()
@@ -1041,47 +1165,53 @@
         scratch=(pltpu.VMEM((rows, channels), F32), pltpu.VMEM((8, channels), F32)),
         spots=([back_slot] + [back] * 5, back),
     )
+    swapped = lax.ppermute(after(o_part[:, 2 * o_cols :], head), "ch", SWAP).astype(F32)
+    g_down_part = outer(after(hidden, head), slot_cot).astype(BF16)
+    o_far = (o_part[:, o_cols : 2 * o_cols].astype(F32) + after(swapped, g_down_part)[:, o_cols:]).astype(BF16)
     ring.mark = (head,)
     g_out = Scatter(ring, lambda k, *t: outer(after(mixed, *t), chunk(d_attn, k)))
     g_out.hop()
     out_hop = [g_out.last]
-    arrive = entering(after(head[:2], *mlp_hop[2]), True)[None]
+    arrive = entering(after(head[:2], *mlp_hop[2], g_down_part, o_far), True)[None]
+    g_down = lax.psum_scatter(after(g_down_part, arrive), "seq", scatter_dimension=1, tiled=True)
+    o_far = lax.ppermute(after(o_far, arrive), "br", SWAP)
+    o_inputs = lax.dynamic_slice_in_dim(whole_inputs, (br * 2 + ch) * o_cols, o_cols, 1)
+    output = o_inputs + o_part[:, :o_cols].astype(F32) + swapped[:, :o_cols] + o_far.astype(F32)
+    back_args = (loc, prod, enter, gates, unit, mask, z, rim, conv, wide, rate)
+    edge = backward_local(adj, tail, arrive, *back_args, first_rows=16)[3]
+    backward_pairs = [(i + 1, i) for i in range(count - 1)]
+    from_next = lax.ppermute(edge[:8], "seq", backward_pairs)
+    ring.mark = (from_next,)
     g_mlp.hop()
     mlp_hop.append(g_mlp.last)
     d_z_rec, g_wide, sums, edge = backward_local(
-        adj, tail, after(arrive, *out_hop[0]), loc, prod, enter, gates, unit, mask, z, rim, conv, wide, rate
-    )
+        adj, tail, after(arrive, from_next, *out_hop[0]), *back_args
+    )
+    edge = after(edge, o_far)
     ring.mark = (edge,)
-    backward_pairs = [(i + 1, i) for i in range(count - 1)]
-    from_next = lax.ppermute(edge[:8], "seq", backward_pairs)
     g_out.hop()
     out_hop.append(g_out.last)
     fixed = (edge[8:] + from_next).astype(BF16)
     d_z_rec = d_z_rec.at[tokens - 8 :].set(fixed)
 
     d_z = jnp.concatenate([d_z_gate, d_z_rec], axis=1)
-    d_h_one = TokenSum()
-    for first in (2, 0):
-        read = lambda i, s, first=first: s[n_pieces + i + first]
-        rec = after(d_z_rec, *out_hop[1]) if first else after(d_z_rec, d_h_one.chip, *mlp_hop[3])
-        part = weight_call(
-            d_h_one_body, in_pieces, in_shape, quarter, (d_z_gate, rec), (), [one_quarter] * 2, scalars,
-            steps=2, spots=([read, read], None),
-        )
-        if first:
-            d_h_one.second(*part)
-            d_h_one.cross()
-        else:
-            d_h_one.first(*part)
-    ring.mark = (part[0], d_z)
     g_in_ring = Scatter(ring, lambda k, *t: outer(chunk(h_one, k), after(d_z, *t)))
+    ring.mark = (d_z,)
     g_in_ring.hop()
+    (d_h_part,) = weight_call(
+        d_h_one_body, in_pieces, in_shape, quarter, (d_z_gate, d_z_rec), (), [(width, BF16)], scalars
+    )
+    d_h_one = GroupSum(d_h_part)
+    ring.mark = (d_h_part,)
     in_hop = [g_in_ring.last]
+    g_in_ring.hop()
+    d_h_one.chip(*in_hop[0])
+    d_h_one.cross()
+    ring.mark = (d_h_one.chip_sum,)
     g_out.hop()
-    out_hop.append(g_out.last)
 
     g_compact = lax.dot_general(
-        (after(g_wide, d_h_one.chip) * on_block.astype(F32)).astype(BF16),
+        (after(g_wide, d_h_one.chip_sum) * on_block.astype(F32)).astype(BF16),
         spread_hot,
         (((1,), (1,)), ((), ())),
         preferred_element_type=F32,
@@ -1101,22 +1231,18 @@
     g_packed_ring = Scatter(ring, lambda k, *t: g_packed[k], free=True)
     for _ in range(4):
         g_packed_ring.hop()
-    (grad_own,) = own_call(
-        norm_one_back_kernel, n_pieces, where, inputs, d_h_one, after(gain_one, *in_hop[0]), (d_resid,), (BF16,),
-        scratch=True,
-    )
-    grad_parts = TokenGather(grad_own).parts()
-    ring.mark = (grad_own,)
+    in_hop.append(g_in_ring.last)
     g_in_ring.hop()
     in_hop.append(g_in_ring.last)
+    d_h_one.total(*in_hop[1])
     g_out.hop()
-    ring.mark = g_packed_ring.last
     g_in_ring.hop()
-    in_hop.append(g_in_ring.last)
-    inputs_grad = spread_call(n_pieces, where, [after(grad_parts[0], *in_hop[1])] + grad_parts[1:])
+    (inputs_grad,) = sum_call(
+        functools.partial(norm_one_whole_kernel), n_pieces, where, d_h_one, inputs, after(gain_one, *in_hop[2]),
+        (d_attn,), (F32,)
+    )
     if not aligned:
         inputs_grad = move(inputs_grad, ring_of)
-    g_in_ring.hop()
 
     g_in_own = g_in_ring.result()
     g_in_gate, g_in_rec = g_in_own[:, :channels], g_in_own[:, channels:]

time: 820 us -> 789 us (0.962)
  local copies, waits for them, and re-layouts: 83.9 us -> 55.8 us
  starting transfers between devices: 116 us -> 96.1 us
  matrix products: 78.5 us -> 86.9 us
    pallas_call x1 -> x3, Pallas kernels: 5.73 us -> 24.4 us  [the longest x1 12.9 us: sum_call(): pl.pallas_call(functools.partial(kernel, count, per), grid_spec=pltpu.Pre...]
    ppermute x64, starting transfers between devices: 84.3 us -> 70.2 us  [hop(): got = lax.ppermute(x, 'seq', self.pairs[way])]
    dot_general x25, matrix products: 70.4 us -> 82.2 us  [outer(): lax.dot_general(left, right, (((0,), (0,)), ((), ())), preferred_element_...]
    unnamed x299 -> x222, local copies, waits for them, and re-layouts: 43.2 us -> 35.1 us
    pallas_call x11 -> x10, Pallas kernels: 154 us -> 150 us  [weight_call(): pl.pallas_call(kernel, grid_spec=pltpu.PrefetchScalarGridSpec(num_scalar_...]
    pallas_call x1 -> x2, Pallas kernels: 22.9 us -> 26.7 us  [backward_local(): pl.pallas_call(backward_kernel, grid=(tokens // rows,), in_specs=[time(ch...]
    ppermute x3 -> x2, waiting for transfers between devices: 20.9 us -> 21.7 us  [__init__(): self.far = lax.ppermute(own, 'br', SWAP)]
  transfers between devices with their start and end apart: 94 -> 91, of which waited for: 33 -> 32; matrix products, arithmetic and copies ran while one was open for 23% -> 20% of each run, Pallas kernels for 24% -> 26%
where the time goes in v3:
time: 789 us; the launch traced here: 778 us
  waiting for transfers between devices  246 us (31%)
  Pallas kernels  233 us (30%)
  starting transfers between devices  96.1 us (12%)
  matrix products  86.9 us (11%)
  local copies, waits for them, and re-layouts  55.8 us (7%)
  other arithmetic  43.3 us (5%)
  between operations  15.9 us (2%)
    ppermute x64, waiting for transfers between devices, hop(): got = lax.ppermute(x, 'seq', self.pairs[way])  200 us
    pallas_call x10, Pallas kernels, weight_call(): pl.pallas_call(kernel, grid_spec=pltpu.PrefetchScalarGridSpec(num_scalar_...  150 us
    dot_general x25, matrix products, outer(): lax.dot_general(left, right, (((0,), (0,)), ((), ())), preferred_element_...  82.2 us
    ppermute x64, starting transfers between devices, hop(): got = lax.ppermute(x, 'seq', self.pairs[way])  70.2 us
    unnamed x222, local copies, waits for them, and re-layouts  35.1 us
    pallas_call x2, Pallas kernels, backward_local(): pl.pallas_call(backward_kernel, grid=(tokens // rows,), in_specs=[time(ch...  26.7 us
    ppermute x2, waiting for transfers between devices, __init__(): self.far = lax.ppermute(own, 'br', SWAP)  21.7 us
    all_to_all x2, waiting for transfers between devices, entering(): every = lax.all_to_all(spread, 'seq', 0, 0, tiled=True)  16.8 us
  transfers between devices with their start and end apart: 91, of which 32 were waited for; matrix products, arithmetic and copies ran while one was open for 20% of the time, Pallas kernels for 26%

profile of v3, /device:TPU:0, one launch (start us, length us, event | category | flops | bytes accessed | tf_op | source)
XLA Modules:
  0.0 777.8 jit_solution(9754866460492069038)
XLA Ops:
  21.1 6.8 collective-permute-done.5.refs_7_.refs_6_
  30.0 6.6 collective-permute-done.3.refs_10_
  45.8 6.6 collective-permute-done.11.refs_11_
  78.2 9.3 %shard_map.281 = (bf16[1024,2048]{1,0:T(8,128)(2,1)}, f32[8,2048]{1,0:T(8,128)S(1)}) custom-call(s32[26]{0:T(128)S(1)} %concatenate.73.where.scalar_ref, f32[1024,2048]{1,0:T(8,128)} %x_ref.6, bf16[320,640]{1,0:T(8,128)(2,1)S(1)} %pad_maximum_fusion.7.refs_0_, bf16[320,640]{1,0:T(8,128)(2,1)S(1)} %collective-permute-done.refs_1_, ...), custom_call_target="tpu_custom_call" | custom-call | tf_op jit(solution)/shard_map/pallas_call | solution.py:502
  89.1 8.0 %shard_map.282 = bf16[16,1280]{1,0:T(8,128)(2,1)} custom-call(s32[26]{0:T(128)} %copy-done.58, bf16[320,640]{1,0:T(8,128)(2,1)} %copy-done.1, bf16[320,640]{1,0:T(8,128)(2,1)} %copy-done.9, bf16[320,640]{1,0:T(8,128)(2,1)} %copy-done.13, bf16[320,640]{1,0:T(8,128)(2,1)} %copy-done.5, bf16[320,640]{1,0:T(8,128)(2,1)} %copy-done.3, ...), custom_call_target="tpu_custom_call" | custom-call | tf_op jit(solution)/shard_map/pallas_call | solution.py:745
  100.5 14.3 %shard_map.283.z_ref.refs_9_.refs_10_.z0_ref = bf16[1024,1280]{1,0:T(8,128)(2,1)} custom-call(s32[26]{0:T(128)} %copy-done.58, bf16[320,640]{1,0:T(8,128)(2,1)} %copy-done.1, bf16[320,640]{1,0:T(8,128)(2,1)} %copy-done.9, bf16[320,640]{1,0:T(8,128)(2,1)} %copy-done.13, bf16[320,640]{1,0:T(8,128)(2,1)} %copy-done.5, bf16[320,640]{1,0:T(8,128)(2,1)} %copy-done.3, ...), custom_call_target="tpu_custom_call" | custom-call | tf_op jit(solution)/shard_map/pallas_call | solution.py:745
  125.6 14.1 %shard_map.285 = (bf16[1024,640]{1,0:T(8,128)(2,1)S(1)}, f32[1024,1280]{1,0:T(8,128)}, f32[1024,640]{1,0:T(8,128)S(1)}, f32[1024,640]{1,0:T(8,128)}, f32[8,640]{1,0:T(8,128)S(1)}, /*index=5*/f32[8,640]{1,0:T(8,128)S(1)}) custom-call(bf16[1024,1280]{1,0:T(8,128)(2,1)} %shard_map.283.z_ref.refs_9_.refs_10_.z0_ref, f32[8,640]{1,0:T(8,128)S(1)} %convert_element_type.309.rim_ref, ...), custom_call_target="tpu_custom_call" | custom-call | tf_op jit(solution)/shard_map/pallas_call | solution.py:407
  152.1 12.0 %all-to-all-done = f32[8,2,640]{2,1,0:T(2,128)} async-done(((f32[8,2,640]{2,1,0:T(2,128)}), f32[8,2,640]{2,1,0:T(2,128)}, u32[]{:S(2)}, u32[]{:S(2)}) %all-to-all-start) | async-done | bytes 40992 | tf_op jit(solution)/shard_map/all_to_all | solution.py:184
  167.7 10.3 %collective-permute-done.26.refs_8_ = bf16[320,256]{1,0:T(8,128)(2,1)S(1)} collective-permute-done((bf16[320,256]{1,0:T(8,128)(2,1)S(1)}, bf16[320,256]{1,0:T(8,128)(2,1)S(1)}, u32[]{:S(2)}, u32[]{:S(2)}) %collective-permute-start.26) | collective-permute-done | bytes 163872 | tf_op jit(solution)/shard_map/ppermute | solution.py:58
  178.1 11.1 %shard_map.286 = (bf16[1024,640]{1,0:T(8,128)(2,1)}, bf16[256,2048]{1,0:T(8,128)(2,1)S(1)}, bf16[256,2048]{1,0:T(8,128)(2,1)S(1)}, bf16[256,2048]{1,0:T(8,128)(2,1)S(1)}, bf16[256,2048]{1,0:T(8,128)(2,1)}) custom-call(s32[26]{0:T(128)S(1)} %copy-done.59, bf16[640,256]{1,0:T(8,128)(2,1)} %bitcast.8.refs_0_, bf16[640,256]{1,0:T(8,128)(2,1)} %collective-permute-done.18.refs_1_, ...), custom_call_target="tpu_custom_call" | custom-call | tf_op jit(solution)/shard_map/pallas_call | solution.py:745
  197.3 8.2 %shard_map.287 = (bf16[1024,2048]{1,0:T(8,128)(2,1)S(1)}, bf16[1024,2048]{1,0:T(8,128)(2,1)}) custom-call(s32[26]{0:T(128)S(1)} %copy-done.59, f32[1024,2048]{1,0:T(8,128)} %cot_ref.1), custom_call_target="tpu_custom_call" | custom-call | tf_op jit(solution)/shard_map/pallas_call | solution.py:641
  207.5 23.8 %collective-permute-done.31.refs_6_ = bf16[1536,256]{1,0:T(8,128)(2,1)S(1)} collective-permute-done((bf16[1536,256]{1,0:T(8,128)(2,1)S(1)}, bf16[1536,256]{1,0:T(8,128)(2,1)S(1)}, u32[]{:S(2)}, u32[]{:S(2)}) %collective-permute-start.31) | collective-permute-done | bytes 786464 | tf_op jit(solution)/shard_map/ppermute | solution.py:58
  231.3 20.4 %collective-permute-done.22.refs_1_ = bf16[1536,256]{1,0:T(8,128)(2,1)S(1)} collective-permute-done((bf16[1536,256]{1,0:T(8,128)(2,1)S(1)}, bf16[1536,256]{1,0:T(8,128)(2,1)S(1)}, u32[]{:S(2)}, u32[]{:S(2)}) %collective-permute-start.22) | collective-permute-done | bytes 786464 | tf_op jit(solution)/shard_map/ppermute | solution.py:58
  259.8 21.7 %collective-permute-done.36 = bf16[256,2048]{1,0:T(8,128)(2,1)S(1)} collective-permute-done((bf16[256,2048]{1,0:T(8,128)(2,1)S(1)}, bf16[256,2048]{1,0:T(8,128)(2,1)S(1)}, u32[]{:S(2)}, u32[]{:S(2)}) %collective-permute-start.36) | collective-permute-done | bytes 1048608 | tf_op jit(solution)/shard_map/ppermute | solution.py:168
  281.5 11.0 %collective-permute-done.33.refs_5_ = bf16[1536,256]{1,0:T(8,128)(2,1)S(1)} collective-permute-done((bf16[1536,256]{1,0:T(8,128)(2,1)S(1)}, bf16[1536,256]{1,0:T(8,128)(2,1)S(1)}, u32[]{:S(2)}, u32[]{:S(2)}) %collective-permute-start.33) | collective-permute-done | bytes 786464 | tf_op jit(solution)/shard_map/ppermute | solution.py:58
  295.1 16.7 %collective-permute-done.32.refs_3_ = bf16[1536,256]{1,0:T(8,128)(2,1)S(1)} collective-permute-done((bf16[1536,256]{1,0:T(8,128)(2,1)S(1)}, bf16[1536,256]{1,0:T(8,128)(2,1)S(1)}, u32[]{:S(2)}, u32[]{:S(2)}) %collective-permute-start.32) | collective-permute-done | bytes 786464 | tf_op jit(solution)/shard_map/ppermute | solution.py:58
  320.3 22.1 %shard_map.289 = (bf16[1024,1536]{1,0:T(8,128)(2,1)S(1)}, bf16[1024,1536]{1,0:T(8,128)(2,1)}, bf16[1024,1536]{1,0:T(8,128)(2,1)}) custom-call(s32[26]{0:T(128)S(1)} %copy-done.59, bf16[2,2048,1536]{2,1,0:T(8,128)(2,1)} %all-gather.2.cloned.1.call-done.refs_0_, bf16[1024,2048]{1,0:T(8,128)(2,1)} %pad_maximum_fusion.refs_1_), custom_call_target="tpu_custom_call" | custom-call | tf_op jit(solution)/shard_map/pallas_call | solution.py:745
  344.1 14.8 %shard_map.290.refs_1_ = bf16[1024,3072]{1,0:T(8,128)(2,1)} custom-call(s32[26]{0:T(128)S(1)} %copy-done.59, bf16[1536,256]{1,0:T(8,128)(2,1)S(1)} %copy-done.32, bf16[1536,256]{1,0:T(8,128)(2,1)S(1)} %copy-done.35, bf16[1536,256]{1,0:T(8,128)(2,1)S(1)} %copy-done.41, bf16[1536,256]{1,0:T(8,128)(2,1)S(1)} %collective-permute-done.32.refs_3_, ...), custom_call_target="tpu_custom_call" | custom-call | tf_op jit(solution)/shard_map/pallas_call | solution.py:745
  358.9 14.4 %shard_map.291 = (bf16[256,2048]{1,0:T(8,128)(2,1)S(1)}, bf16[256,2048]{1,0:T(8,128)(2,1)S(1)}) custom-call(s32[26]{0:T(128)S(1)} %copy-done.59, bf16[2,2048,1536]{2,1,0:T(8,128)(2,1)} %all-gather.2.cloned.1.call-done.refs_0_, bf16[1024,3072]{1,0:T(8,128)(2,1)} %shard_map.290.refs_1_), custom_call_target="tpu_custom_call" | custom-call | tf_op jit(solution)/shard_map/pallas_call | solution.py:745
  381.0 13.9 %shard_map.292 = (bf16[256,2048]{1,0:T(8,128)(2,1)S(1)}, bf16[256,2048]{1,0:T(8,128)(2,1)S(1)}) custom-call(s32[26]{0:T(128)S(1)} %copy-done.59, bf16[2,2048,1536]{2,1,0:T(8,128)(2,1)} %all-gather.2.cloned.1.call-done.refs_0_, bf16[1024,3072]{1,0:T(8,128)(2,1)} %shard_map.290.refs_1_), custom_call_target="tpu_custom_call" | custom-call | tf_op jit(solution)/shard_map/pallas_call | solution.py:745
  423.4 15.9 %shard_map.294 = bf16[1024,2048]{1,0:T(8,128)(2,1)} custom-call(s32[26]{0:T(128)S(1)} %copy-done.59, bf16[1536,256]{1,0:T(8,128)(2,1)S(1)} %copy-done.33, bf16[1536,256]{1,0:T(8,128)(2,1)S(1)} %copy-done.36, bf16[1536,256]{1,0:T(8,128)(2,1)S(1)} %copy-done.42, bf16[1536,256]{1,0:T(8,128)(2,1)S(1)} %collective-permute-done.32.refs_3_, ...), custom_call_target="tpu_custom_call" | custom-call | tf_op jit(solution)/shard_map/pallas_call | solution.py:745
  444.9 6.5 fusion.1
  463.2 20.1 %shard_map.295 = (f32[1024,640]{1,0:T(8,128)}, f32[1024,640]{1,0:T(8,128)}, bf16[1024,640]{1,0:T(8,128)(2,1)S(1)}, f32[8,640]{1,0:T(8,128)S(1)}) custom-call(s32[26]{0:T(128)S(1)} %copy-done.59, bf16[640,256]{1,0:T(8,128)(2,1)} %bitcast.8.refs_0_, bf16[640,256]{1,0:T(8,128)(2,1)} %collective-permute-done.18.refs_1_, bf16[640,256]{1,0:T(8,128)(2,1)S(1)} %copy-done.48, ...), custom_call_target="tpu_custom_call" | custom-call | tf_op jit(solution)/shard_map/pallas_call | solution.py:745
  486.4 8.8 %convolution_convert_fusion = bf16[1536,2048]{1,0:T(8,128)(2,1)} fusion(bf16[1024,1536]{1,0:T(8,128)(2,1)S(1)} %copy-done.44, bf16[1024,2048]{1,0:T(8,128)(2,1)S(1)} %copy-done.95), kind=kOutput, calls=%fused_computation | convolution fusion | flops 6445596672 | bytes 13631488 | tf_op jit(solution)/shard_map/dot_general | solution.py:1110
  525.1 23.1 %shard_map.297 = (bf16[1024,640]{1,0:T(8,128)(2,1)S(1)}, f32[640,1280]{1,0:T(8,128)}, f32[16,640]{1,0:T(8,128)S(1)}, f32[16,640]{1,0:T(8,128)S(1)}) custom-call(f32[1024,640]{1,0:T(8,128)} %get-tuple-element.242.adj_ref, f32[1024,640]{1,0:T(8,128)} %get-tuple-element.243.tail_ref, f32[1,640]{1,0:T(1,128)S(1)} %broadcast_select_fusion.7.arrive_ref, ...), custom_call_target="tpu_custom_call" | custom-call | tf_op jit(solution)/shard_map/pallas_call | solution.py:438
  548.2 7.1 fusion.3
  556.1 6.4 fusion.2
  581.3 15.3 %shard_map.298 = bf16[1024,2048]{1,0:T(8,128)(2,1)} custom-call(s32[26]{0:T(128)} %copy-done.58, bf16[320,640]{1,0:T(8,128)(2,1)} %copy-done.1, bf16[320,640]{1,0:T(8,128)(2,1)} %copy-done.9, bf16[320,640]{1,0:T(8,128)(2,1)} %copy-done.13, bf16[320,640]{1,0:T(8,128)(2,1)} %copy-done.5, bf16[320,640]{1,0:T(8,128)(2,1)} %copy-done.3, ...), custom_call_target="tpu_custom_call" | custom-call | tf_op jit(solution)/shard_map/pallas_call | solution.py:745
  598.6 27.8 %collective-permute-done.59 = bf16[128,1280]{1,0:T(8,128)(2,1)S(1)} collective-permute-done((bf16[128,1280]{1,0:T(8,128)(2,1)}, bf16[128,1280]{1,0:T(8,128)(2,1)S(1)}, u32[]{:S(2)}, u32[]{:S(2)}) %collective-permute-start.59) | collective-permute-done | bytes 327712 | tf_op jit(solution)/shard_map/ppermute | solution.py:58
  656.1 18.5 %collective-permute-done.64 = bf16[256,1280]{1,0:T(8,128)(2,1)} collective-permute-done((bf16[256,1280]{1,0:T(8,128)(2,1)}, bf16[256,1280]{1,0:T(8,128)(2,1)}, u32[]{:S(2)}, u32[]{:S(2)}) %collective-permute-start.64) | collective-permute-done | bytes 655392 | tf_op jit(solution)/shard_map/ppermute | solution.py:58
  692.5 10.4 %collective-permute-done.83 = bf16[96,320]{1,0:T(8,128)(2,1)S(1)} collective-permute-done((bf16[96,320]{1,0:T(8,128)(2,1)S(1)}, bf16[96,320]{1,0:T(8,128)(2,1)S(1)}, u32[]{:S(2)}, u32[]{:S(2)}) %collective-permute-start.83) | collective-permute-done | bytes 61472 | tf_op jit(solution)/shard_map/ppermute | solution.py:58
  755.5 12.9 %shard_map.299 = f32[1024,2048]{1,0:T(8,128)} custom-call(s32[26]{0:T(128)S(1)} %copy-done.60, f32[1024,2048]{1,0:T(8,128)} %x_ref.6, bf16[512,2048]{1,0:T(8,128)(2,1)S(1)} %add_convert_fusion.mine_ref, bf16[512,2048]{1,0:T(8,128)(2,1)} %collective-permute-done.65.other_ref, f32[1,2048]{1,0:T(1,128)S(1)} %get-tuple-element.271.gain_ref, ...), custom_call_target="tpu_custom_call" | custom-call | tf_op jit(solution)/shard_map/pallas_call | solution.py:689
  (557 shorter events, 323.1 us)
Async XLA Ops:
  7.2 313.1 %all-gather.2.cloned.1.call-start = ((), (), s32[]{:S(2)}) async-start(), calls=%async_computation.3 | async-start | bytes 14155776 | tf_op jit(solution)/shard_map/all_gather | solution.py:959
  76.1 46.9 %collective-permute-start.18 = (bf16[640,256]{1,0:T(8,128)(2,1)}, bf16[640,256]{1,0:T(8,128)(2,1)}, u32[]{:S(2)}, u32[]{:S(2)}) collective-permute-start(bf16[640,256]{1,0:T(8,128)(2,1)} %bitcast.8.refs_0_), channel_id=1, source_target_pairs={{4,0},{8,4},{12,8},{14,12},{10,14},{6,10},{2,6},{0,2},{5,1},{9,5},... | collective-permute-start | bytes 983048 | tf_op jit(solution)/shard_map/ppermute | solution.py:58
  76.8 48.7 %collective-permute-start.17 = (bf16[640,256]{1,0:T(8,128)(2,1)}, bf16[640,256]{1,0:T(8,128)(2,1)}, u32[]{:S(2)}, u32[]{:S(2)}) collective-permute-start(bf16[640,256]{1,0:T(8,128)(2,1)} %bitcast.8.refs_0_), channel_id=1, source_target_pairs={{0,4},{4,8},{8,12},{12,14},{14,10},{10,6},{6,2},{2,0},{1,5},{5,9},... | collective-permute-start | bytes 983048 | tf_op jit(solution)/shard_map/ppermute | solution.py:58
  189.3 62.3 %collective-permute-start.29 = (bf16[256,2048]{1,0:T(8,128)(2,1)S(1)}, bf16[256,2048]{1,0:T(8,128)(2,1)S(1)}, u32[]{:S(2)}, u32[]{:S(2)}) collective-permute-start(bf16[256,2048]{1,0:T(8,128)(2,1)S(1)} %get-tuple-element.195.refs_11_), channel_id=1, source_target_pairs={{0,1},{1,0},{2,3},{3,2},{4,5},{5,4},{6,7},{7,6},{8,9},{9,8},{10,11... | collective-permute-start | bytes 3145736 | tf_op jit(solution)/shard_map/ppermute | solution.py:138
  193.3 58.3 %collective-permute-start.30 = (bf16[256,2048]{1,0:T(8,128)(2,1)S(1)}, bf16[256,2048]{1,0:T(8,128)(2,1)S(1)}, u32[]{:S(2)}, u32[]{:S(2)}) collective-permute-start(bf16[256,2048]{1,0:T(8,128)(2,1)S(1)} %add_convert_fusion.4), channel_id=1, source_target_pairs={{0,16},{16,0},{1,17},{17,1},{2,18},{18,2},{3,19},{19,3},{4,20},{20... | collective-permute-start | bytes 3145736 | tf_op jit(solution)/shard_map/ppermute | solution.py:134
  194.1 37.1 %collective-permute-start.31 = (bf16[1536,256]{1,0:T(8,128)(2,1)S(1)}, bf16[1536,256]{1,0:T(8,128)(2,1)S(1)}, u32[]{:S(2)}, u32[]{:S(2)}) collective-permute-start(bf16[1536,256]{1,0:T(8,128)(2,1)S(1)} %copy-done.31), channel_id=1, source_target_pairs={{0,4},{4,8},{8,12},{12,14},{14,10},{10,6},{6,2},{2,0},{1,5},{5,9},... | collective-permute-start | bytes 2359304 | tf_op jit(solution)/shard_map/ppermute | solution.py:58
  195.5 56.2 %collective-permute-start.22 = (bf16[1536,256]{1,0:T(8,128)(2,1)S(1)}, bf16[1536,256]{1,0:T(8,128)(2,1)S(1)}, u32[]{:S(2)}, u32[]{:S(2)}) collective-permute-start(bf16[1536,256]{1,0:T(8,128)(2,1)S(1)} %copy-done.31), channel_id=1, source_target_pairs={{4,0},{8,4},{12,8},{14,12},{10,14},{6,10},{2,6},{0,2},{5,1},{9,5},... | collective-permute-start | bytes 2359304 | tf_op jit(solution)/shard_map/ppermute | solution.py:58
  257.8 34.7 %collective-permute-start.33 = (bf16[1536,256]{1,0:T(8,128)(2,1)S(1)}, bf16[1536,256]{1,0:T(8,128)(2,1)S(1)}, u32[]{:S(2)}, u32[]{:S(2)}) collective-permute-start(bf16[1536,256]{1,0:T(8,128)(2,1)S(1)} %collective-permute-done.31.refs_6_), channel_id=1, source_target_pairs={{0,4},{4,8},{8,12},{12,14},{14,10},{10,6},{6,2},{2,0},{1,5},{5,9},... | collective-permute-start | bytes 2359304 | tf_op jit(solution)/shard_map/ppermute | solution.py:58
  258.1 34.4 %collective-permute-start.28 = (bf16[1536,256]{1,0:T(8,128)(2,1)S(1)}, bf16[1536,256]{1,0:T(8,128)(2,1)S(1)}, u32[]{:S(2)}, u32[]{:S(2)}) collective-permute-start(bf16[1536,256]{1,0:T(8,128)(2,1)S(1)} %collective-permute-done.22.refs_1_), channel_id=1, source_target_pairs={{4,0},{8,4},{12,8},{14,12},{10,14},{6,10},{2,6},{0,2},{5,1},{9,5},... | collective-permute-start | bytes 2359304 | tf_op jit(solution)/shard_map/ppermute | solution.py:58
  259.8 56.2 %collective-permute-start.35 = (bf16[256,2048]{1,0:T(8,128)(2,1)S(1)}, bf16[256,2048]{1,0:T(8,128)(2,1)S(1)}, u32[]{:S(2)}, u32[]{:S(2)}) collective-permute-start(bf16[256,2048]{1,0:T(8,128)(2,1)S(1)} %get-tuple-element.201), channel_id=1, source_target_pairs={{0,1},{1,0},{2,3},{3,2},{4,5},{5,4},{6,7},{7,6},{8,9},{9,8},{10,11... | collective-permute-start | bytes 3145736 | tf_op jit(solution)/shard_map/ppermute | solution.py:169
  281.5 34.6 %collective-permute-start.37 = (bf16[256,2048]{1,0:T(8,128)(2,1)S(1)}, bf16[256,2048]{1,0:T(8,128)(2,1)S(1)}, u32[]{:S(2)}, u32[]{:S(2)}) collective-permute-start(bf16[256,2048]{1,0:T(8,128)(2,1)S(1)} %collective-permute-done.36), channel_id=1, source_target_pairs={{0,1},{1,0},{2,3},{3,2},{4,5},{5,4},{6,7},{7,6},{8,9},{9,8},{10,11... | collective-permute-start | bytes 3145736 | tf_op jit(solution)/shard_map/ppermute | solution.py:170
  318.3 25.8 %collective-permute-start.39 = (bf16[768,256]{1,0:T(8,128)(2,1)}, bf16[768,256]{1,0:T(8,128)(2,1)}, u32[]{:S(2)}, u32[]{:S(2)}) collective-permute-start(bf16[768,256]{1,0:T(8,128)(2,1)} %slice.662), channel_id=1, source_target_pairs={{4,0},{8,4},{12,8},{14,12},{10,14},{6,10},{2,6},{0,2},{5,1},{9,5},... | collective-permute-start | bytes 1179656 | tf_op jit(solution)/shard_map/ppermute | solution.py:58
  379.0 25.9 %collective-permute-start.47 = (bf16[128,3072]{1,0:T(8,128)(2,1)S(1)}, bf16[128,3072]{1,0:T(8,128)(2,1)}, u32[]{:S(2)}, u32[]{:S(2)}) collective-permute-start(bf16[128,3072]{1,0:T(8,128)(2,1)S(1)} %get-tuple-element.229), channel_id=1, source_target_pairs={{0,4},{4,8},{8,12},{12,14},{14,10},{10,6},{6,2},{2,0},{1,5},{5,9},... | collective-permute-start | bytes 2359304 | tf_op jit(solution)/shard_map/ppermute | solution.py:58
  379.9 31.2 %collective-permute-start.42 = (bf16[256,2048]{1,0:T(8,128)(2,1)S(1)}, bf16[256,2048]{1,0:T(8,128)(2,1)S(1)}, u32[]{:S(2)}, u32[]{:S(2)}) collective-permute-start(bf16[256,2048]{1,0:T(8,128)(2,1)S(1)} %add_convert_fusion.3), channel_id=1, source_target_pairs={{0,16},{16,0},{1,17},{17,1},{2,18},{18,2},{3,19},{19,3},{4,20},{20... | collective-permute-start | bytes 3145736 | tf_op jit(solution)/shard_map/ppermute | solution.py:134
  403.2 41.7 %collective-permute-start.51 = (bf16[256,3072]{1,0:T(8,128)(2,1)}, bf16[256,3072]{1,0:T(8,128)(2,1)}, u32[]{:S(2)}, u32[]{:S(2)}) collective-permute-start(bf16[256,3072]{1,0:T(8,128)(2,1)} %pad_maximum_fusion.4), channel_id=1, source_target_pairs={{4,0},{8,4},{12,8},{14,12},{10,14},{6,10},{2,6},{0,2},{5,1},{9,5},... | collective-permute-start | bytes 4718600 | tf_op jit(solution)/shard_map/ppermute | solution.py:58
  410.6 42.4 %collective-permute-start.48 = (bf16[256,3072]{1,0:T(8,128)(2,1)}, bf16[256,3072]{1,0:T(8,128)(2,1)}, u32[]{:S(2)}, u32[]{:S(2)}) collective-permute-start(bf16[256,3072]{1,0:T(8,128)(2,1)} %pad_maximum_fusion.3), channel_id=1, source_target_pairs={{0,4},{4,8},{8,12},{12,14},{14,10},{10,6},{6,2},{2,0},{1,5},{5,9},... | collective-permute-start | bytes 4718600 | tf_op jit(solution)/shard_map/ppermute | solution.py:58
  416.6 36.5 %collective-permute-start.44 = (bf16[256,2048]{1,0:T(8,128)(2,1)}, bf16[256,2048]{1,0:T(8,128)(2,1)}, u32[]{:S(2)}, u32[]{:S(2)}) collective-permute-start(bf16[256,2048]{1,0:T(8,128)(2,1)} %get-tuple-element.220), channel_id=1, source_target_pairs={{0,16},{16,0},{1,17},{17,1},{2,18},{18,2},{3,19},{19,3},{4,20},{20... | collective-permute-start | bytes 3145736 | tf_op jit(solution)/shard_map/ppermute | solution.py:168
  417.6 40.8 %collective-permute-start.43 = (bf16[256,2048]{1,0:T(8,128)(2,1)}, bf16[256,2048]{1,0:T(8,128)(2,1)S(1)}, u32[]{:S(2)}, u32[]{:S(2)}) collective-permute-start(bf16[256,2048]{1,0:T(8,128)(2,1)} %get-tuple-element.220), channel_id=1, source_target_pairs={{0,1},{1,0},{2,3},{3,2},{4,5},{5,4},{6,7},{7,6},{8,9},{9,8},{10,11... | collective-permute-start | bytes 3145736 | tf_op jit(solution)/shard_map/ppermute | solution.py:169
  451.4 50.5 %collective-permute-start.52 = (bf16[256,3072]{1,0:T(8,128)(2,1)}, bf16[256,3072]{1,0:T(8,128)(2,1)}, u32[]{:S(2)}, u32[]{:S(2)}) collective-permute-start(bf16[256,3072]{1,0:T(8,128)(2,1)} %fusion.1), channel_id=1, source_target_pairs={{4,0},{8,4},{12,8},{14,12},{10,14},{6,10},{2,6},{0,2},{5,1},{9,5},... | collective-permute-start | bytes 4718600 | tf_op jit(solution)/shard_map/ppermute | solution.py:58
  458.0 43.8 %collective-permute-start.49 = (bf16[256,3072]{1,0:T(8,128)(2,1)}, bf16[256,3072]{1,0:T(8,128)(2,1)}, u32[]{:S(2)}, u32[]{:S(2)}) collective-permute-start(bf16[256,3072]{1,0:T(8,128)(2,1)} %fusion), channel_id=1, source_target_pairs={{0,4},{4,8},{8,12},{12,14},{14,10},{10,6},{6,2},{2,0},{1,5},{5,9},... | collective-permute-start | bytes 4718600 | tf_op jit(solution)/shard_map/ppermute | solution.py:58
  506.1 262.2 %reduce-scatter.2.cloned.1.call-start = ((), (), s32[]{:S(2)}) async-start(), calls=%async_computation.4 | async-start | bytes 7077888 | tf_op jit(solution)/shard_map/reduce_scatter | solution.py:1176
  519.9 44.5 %collective-permute-start.53 = (bf16[1024,512]{1,0:T(8,128)(2,1)}, bf16[1024,512]{1,0:T(8,128)(2,1)}, u32[]{:S(2)}, u32[]{:S(2)}) collective-permute-start(bf16[1024,512]{1,0:T(8,128)(2,1)} %add_convert_fusion.2), channel_id=1, source_target_pairs={{0,16},{16,0},{1,17},{17,1},{2,18},{18,2},{3,19},{19,3},{4,20},{20... | collective-permute-start | bytes 3145736 | tf_op jit(solution)/shard_map/ppermute | solution.py:1177
  555.3 80.1 %collective-permute-start.63 = (bf16[256,3072]{1,0:T(8,128)(2,1)}, bf16[256,3072]{1,0:T(8,128)(2,1)}, u32[]{:S(2)}, u32[]{:S(2)}) collective-permute-start(bf16[256,3072]{1,0:T(8,128)(2,1)} %fusion.3), channel_id=1, source_target_pairs={{4,0},{8,4},{12,8},{14,12},{10,14},{6,10},{2,6},{0,2},{5,1},{9,5},... | collective-permute-start | bytes 4718600 | tf_op jit(solution)/shard_map/ppermute | solution.py:58
  562.6 72.8 %collective-permute-start.61 = (bf16[256,3072]{1,0:T(8,128)(2,1)}, bf16[256,3072]{1,0:T(8,128)(2,1)}, u32[]{:S(2)}, u32[]{:S(2)}) collective-permute-start(bf16[256,3072]{1,0:T(8,128)(2,1)} %fusion.2), channel_id=1, source_target_pairs={{0,4},{4,8},{8,12},{12,14},{14,10},{10,6},{6,2},{2,0},{1,5},{5,9},... | collective-permute-start | bytes 4718600 | tf_op jit(solution)/shard_map/ppermute | solution.py:58
  567.4 118.5 %collective-permute-start.71 = (bf16[640,256]{1,0:T(8,128)(2,1)}, bf16[640,256]{1,0:T(8,128)(2,1)}, u32[]{:S(2)}, u32[]{:S(2)}) collective-permute-start(bf16[640,256]{1,0:T(8,128)(2,1)} %pad_maximum_fusion.9), channel_id=1, source_target_pairs={{4,0},{8,4},{12,8},{14,12},{10,14},{6,10},{2,6},{0,2},{5,1},{9,5},... | collective-permute-start | bytes 983048 | tf_op jit(solution)/shard_map/ppermute | solution.py:58
  572.6 53.7 %collective-permute-start.59 = (bf16[128,1280]{1,0:T(8,128)(2,1)}, bf16[128,1280]{1,0:T(8,128)(2,1)S(1)}, u32[]{:S(2)}, u32[]{:S(2)}) collective-permute-start(bf16[128,1280]{1,0:T(8,128)(2,1)} %get-tuple-element.256), channel_id=1, source_target_pairs={{4,0},{8,4},{12,8},{14,12},{10,14},{6,10},{2,6},{0,2},{5,1},{9,5},... | collective-permute-start | bytes 983048 | tf_op jit(solution)/shard_map/ppermute | solution.py:58
  573.5 52.9 %collective-permute-start.58 = (bf16[128,1280]{1,0:T(8,128)(2,1)S(1)}, bf16[128,1280]{1,0:T(8,128)(2,1)S(1)}, u32[]{:S(2)}, u32[]{:S(2)}) collective-permute-start(bf16[128,1280]{1,0:T(8,128)(2,1)S(1)} %get-tuple-element.255), channel_id=1, source_target_pairs={{0,4},{4,8},{8,12},{12,14},{14,10},{10,6},{6,2},{2,0},{1,5},{5,9},... | collective-permute-start | bytes 983048 | tf_op jit(solution)/shard_map/ppermute | solution.py:58
  626.4 64.1 %collective-permute-start.68 = (bf16[640,256]{1,0:T(8,128)(2,1)}, bf16[640,256]{1,0:T(8,128)(2,1)}, u32[]{:S(2)}, u32[]{:S(2)}) collective-permute-start(bf16[640,256]{1,0:T(8,128)(2,1)} %pad_maximum_fusion.8), channel_id=1, source_target_pairs={{0,4},{4,8},{8,12},{12,14},{14,10},{10,6},{6,2},{2,0},{1,5},{5,9},... | collective-permute-start | bytes 983048 | tf_op jit(solution)/shard_map/ppermute | solution.py:58
  635.4 39.2 %collective-permute-start.64 = (bf16[256,1280]{1,0:T(8,128)(2,1)}, bf16[256,1280]{1,0:T(8,128)(2,1)}, u32[]{:S(2)}, u32[]{:S(2)}) collective-permute-start(bf16[256,1280]{1,0:T(8,128)(2,1)} %pad_maximum_fusion.6), channel_id=1, source_target_pairs={{4,0},{8,4},{12,8},{14,12},{10,14},{6,10},{2,6},{0,2},{5,1},{9,5},... | collective-permute-start | bytes 1966088 | tf_op jit(solution)/shard_map/ppermute | solution.py:58
  635.9 41.0 %collective-permute-start.62 = (bf16[256,1280]{1,0:T(8,128)(2,1)}, bf16[256,1280]{1,0:T(8,128)(2,1)}, u32[]{:S(2)}, u32[]{:S(2)}) collective-permute-start(bf16[256,1280]{1,0:T(8,128)(2,1)} %pad_maximum_fusion.5), channel_id=1, source_target_pairs={{0,4},{4,8},{8,12},{12,14},{14,10},{10,6},{6,2},{2,0},{1,5},{5,9},... | collective-permute-start | bytes 1966088 | tf_op jit(solution)/shard_map/ppermute | solution.py:58
  647.6 92.5 %collective-permute-start.60 = (bf16[512,2048]{1,0:T(8,128)(2,1)}, bf16[512,2048]{1,0:T(8,128)(2,1)}, u32[]{:S(2)}, u32[]{:S(2)}) collective-permute-start(bf16[512,2048]{1,0:T(8,128)(2,1)} %add_convert_fusion.1), channel_id=1, source_target_pairs={{0,16},{16,0},{1,17},{17,1},{2,18},{18,2},{3,19},{19,3},{4,20},{20... | collective-permute-start | bytes 6291464 | tf_op jit(solution)/shard_map/ppermute | solution.py:156
  690.5 26.2 %collective-permute-start.66 = (bf16[256,1280]{1,0:T(8,128)(2,1)}, bf16[256,1280]{1,0:T(8,128)(2,1)}, u32[]{:S(2)}, u32[]{:S(2)}) collective-permute-start(bf16[256,1280]{1,0:T(8,128)(2,1)} %fusion.4), channel_id=1, source_target_pairs={{0,4},{4,8},{8,12},{12,14},{14,10},{10,6},{6,2},{2,0},{1,5},{5,9},... | collective-permute-start | bytes 1966088 | tf_op jit(solution)/shard_map/ppermute | solution.py:58
  (167 other events, 2347.2 us)
Sparse Core Ops, SparseCore 0:
  75.1 218.0 all-gather.1
  520.0 156.5 reduce-scatter.1

commit v4 on v3

--- a/solution.py
+++ b/solution.py
@@ -171,11 +171,6 @@
 
     def parts(self):
         return [self.own, self.core, self.far, self.far_core]
-
-
-def tiny_group_sum(x):
-    x = x + lax.ppermute(x, "ch", SWAP)
-    return x + lax.ppermute(x, "br", SWAP)
 
 
 def entering(pair, reverse):
@@ -393,7 +388,7 @@
             edge_ref[8:16, own] = dz[rows - 8 :]
 
 
-def kernel_params(mib=48):
+def kernel_params(mib=54):
     return pltpu.CompilerParams(dimension_semantics=("arbitrary",), vmem_limit_bytes=mib * 1024 * 1024)
 
 
@@ -616,19 +611,26 @@
     return jnp.where(is_mine, mine_ref[:, own], other_ref[:, own]).astype(F32)
 
 
-def norm_one_whole_kernel(count, per, where, x_ref, mine_ref, other_ref, gain_ref, d_resid_ref, *refs):
-    out_ref = refs[-1]
+def norm_one_whole_kernel(count, per, where, x_ref, mine_ref, other_ref, gain_ref, d_resid_ref, out_ref, kept):
     width = x_ref.shape[1]
+    is_mine = (pl.program_id(0) // per) == where[where.shape[0] - 1]
+
+    @pl.when(is_mine)
+    def _():
+        kept[...] = mine_ref[...].astype(F32) * gain_ref[...]
+
+    @pl.when(jnp.logical_not(is_mine))
+    def _():
+        kept[...] = other_ref[...].astype(F32) * gain_ref[...]
+
     x = x_ref[...]
     rstd = lax.rsqrt(jnp.sum(x * x, axis=1, keepdims=True) * (1.0 / width) + NORM_EPS)
     along = 0.0
     for own, true in pieces_of(width, where, count):
-        d_normed = pick(where, mine_ref, other_ref, own, per) * gain_ref[:, own]
-        along = along + jnp.sum(d_normed * x_ref[:, true], axis=1, keepdims=True)
+        along = along + jnp.sum(kept[:, own] * x_ref[:, true], axis=1, keepdims=True)
     along = along * rstd * (1.0 / width)
     for own, true in pieces_of(width, where, count):
-        d_normed = pick(where, mine_ref, other_ref, own, per) * gain_ref[:, own]
-        out_ref[:, true] = d_resid_ref[:, own].astype(F32) + rstd * (d_normed - x_ref[:, true] * rstd * along)
+        out_ref[:, true] = d_resid_ref[:, own].astype(F32) + rstd * (kept[:, own] - x_ref[:, true] * rstd * along)
 
 
 def norm_call(kernel, count, where, x, gain, outputs=1, slots=False):
@@ -693,6 +695,7 @@
             grid=(tokens // rows,),
             in_specs=[time, mine, other, gain_spec] + [slot] * len(extra),
             out_specs=[time] * len(out_types),
+            scratch_shapes=[pltpu.VMEM((rows, width), F32)],
         ),
         out_shape=[jax.ShapeDtypeStruct((tokens, width), t) for t in out_types],
         compiler_params=kernel_params(),
@@ -1228,15 +1231,16 @@
     g_packed = jnp.concatenate([g_gates.reshape(count, gate_rows, fold), g_small], axis=1)
     total_rows = -(-g_packed.shape[1] // 32) * 32
     g_packed = jnp.pad(g_packed, ((0, 0), (0, total_rows - g_packed.shape[1]), (0, 0)))
-    g_packed_ring = Scatter(ring, lambda k, *t: g_packed[k], free=True)
-    for _ in range(4):
-        g_packed_ring.hop()
     in_hop.append(g_in_ring.last)
     g_in_ring.hop()
     in_hop.append(g_in_ring.last)
-    d_h_one.total(*in_hop[1])
+    g_down = g_down.astype(F32)
+    d_h_one.total(*in_hop[1], g_down)
     g_out.hop()
     g_in_ring.hop()
+    g_packed_ring = Scatter(ring, lambda k, *t: after(g_packed, *in_hop[2])[k], free=True)
+    for _ in range(4):
+        g_packed_ring.hop()
     (inputs_grad,) = sum_call(
         functools.partial(norm_one_whole_kernel), n_pieces, where, d_h_one, inputs, after(gain_one, *in_hop[2]),
         (d_attn,), (F32,)
@@ -1263,7 +1267,8 @@
             + jnp.sum(g_up_own * mlp_in[1].astype(F32), axis=1),
         ]
     )
-    gains = tiny_group_sum(gains)
+    gains = gains + after(lax.ppermute(gains, "ch", SWAP), inputs_grad)
+    gains = gains + lax.ppermute(gains, "br", SWAP)
     g_own = g_packed_ring.result()
     g_gate_w = g_own[:gate_rows].reshape(heads, part_in, 2, block).transpose(2, 0, 1, 3)[:, None, None]
     g_flat = g_own[gate_rows : gate_rows + g_rows].reshape(-1)

time: 789 us -> 783 us (level)
  local copies, waits for them, and re-layouts: 55.8 us -> 46.9 us
  waiting for transfers between devices: 246 us -> 238 us
    unnamed x222 -> x210, local copies, waits for them, and re-layouts: 35.1 us -> 20.7 us
    ppermute x64, waiting for transfers between devices: 200 us -> 190 us  [hop(): got = lax.ppermute(x, 'seq', self.pairs[way])]
  transfers between devices with their start and end apart: 91 -> 91, of which waited for: 32 -> 31; matrix products, arithmetic and copies ran while one was open for 20% -> 21% of each run, Pallas kernels for 26% -> 27%
where the time goes in v4:
time: 783 us; the launch traced here: 772 us
  Pallas kernels  239 us (31%)
  waiting for transfers between devices  238 us (30%)
  starting transfers between devices  99 us (13%)
  matrix products  84.4 us (11%)
  other arithmetic  48 us (6%)
  local copies, waits for them, and re-layouts  46.9 us (6%)
  between operations  15.9 us (2%)
    ppermute x64, waiting for transfers between devices, hop(): got = lax.ppermute(x, 'seq', self.pairs[way])  190 us
    pallas_call x10, Pallas kernels, weight_call(): pl.pallas_call(kernel, grid_spec=pltpu.PrefetchScalarGridSpec(num_scalar_...  148 us
    dot_general x25, matrix products, outer(): lax.dot_general(left, right, (((0,), (0,)), ((), ())), preferred_element_...  79.6 us
    ppermute x64, starting transfers between devices, hop(): got = lax.ppermute(x, 'seq', self.pairs[way])  71.5 us
    pallas_call x2, Pallas kernels, backward_local(): pl.pallas_call(backward_kernel, grid=(tokens // rows,), in_specs=[time(ch...  27.9 us
    ppermute x2, waiting for transfers between devices, __init__(): self.far = lax.ppermute(own, 'br', SWAP)  21.7 us
    unnamed x210, local copies, waits for them, and re-layouts  20.7 us
  transfers between devices with their start and end apart: 91, of which 31 were waited for; matrix products, arithmetic and copies ran while one was open for 21% of the time, Pallas kernels for 27%

profile of v4, /device:TPU:0, one launch (start us, length us, event | category | flops | bytes accessed | tf_op | source)
XLA Modules:
  0.0 771.7 jit_solution(12624656272036116462)
XLA Ops:
  21.2 6.7 collective-permute-done.5.refs_7_.refs_6_
  30.0 6.5 collective-permute-done.3.refs_10_
  45.8 6.6 collective-permute-done.11.refs_11_
  79.4 9.4 %shard_map.281 = (bf16[1024,2048]{1,0:T(8,128)(2,1)}, f32[8,2048]{1,0:T(8,128)}) custom-call(s32[26]{0:T(128)} %concatenate.73.where.scalar_ref, f32[1024,2048]{1,0:T(8,128)} %x_ref.6, bf16[320,640]{1,0:T(8,128)(2,1)} %copy-done.49, bf16[320,640]{1,0:T(8,128)(2,1)} %copy-done.53, bf16[320,640]{1,0:T(8,128)(2,1)} %copy-done.55, bf16[320,640]{1,0:T(8,128)(2,1)} %copy-done.51, ...), custom_call_target="tpu_custom_call" | custom-call | tf_op jit(solution)/shard_map/pallas_call | solution.py:497
  90.3 7.9 %shard_map.282 = bf16[16,1280]{1,0:T(8,128)(2,1)} custom-call(s32[26]{0:T(128)} %concatenate.73.where.scalar_ref, bf16[320,640]{1,0:T(8,128)(2,1)} %copy-done.49, bf16[320,640]{1,0:T(8,128)(2,1)} %copy-done.53, bf16[320,640]{1,0:T(8,128)(2,1)} %copy-done.55, bf16[320,640]{1,0:T(8,128)(2,1)} %copy-done.51, bf16[320,640]{1,0:T(8,128)(2,1)} %copy-done.50, ...), custom_call_target="tpu_custom_call" | custom-call | tf_op jit(solution)/shard_map/pallas_call | solution.py:748
  103.4 14.2 %shard_map.283.z_ref.refs_9_.refs_10_.z0_ref = bf16[1024,1280]{1,0:T(8,128)(2,1)} custom-call(s32[26]{0:T(128)} %concatenate.73.where.scalar_ref, bf16[320,640]{1,0:T(8,128)(2,1)} %copy-done.49, bf16[320,640]{1,0:T(8,128)(2,1)} %copy-done.53, bf16[320,640]{1,0:T(8,128)(2,1)} %copy-done.55, bf16[320,640]{1,0:T(8,128)(2,1)} %copy-done.51, ...), custom_call_target="tpu_custom_call" | custom-call | tf_op jit(solution)/shard_map/pallas_call | solution.py:748
  127.1 15.0 %shard_map.285 = (bf16[1024,640]{1,0:T(8,128)(2,1)}, f32[1024,1280]{1,0:T(8,128)}, f32[1024,640]{1,0:T(8,128)}, f32[1024,640]{1,0:T(8,128)}, f32[8,640]{1,0:T(8,128)}, /*index=5*/f32[8,640]{1,0:T(8,128)}) custom-call(bf16[1024,1280]{1,0:T(8,128)(2,1)} %shard_map.283.z_ref.refs_9_.refs_10_.z0_ref, f32[8,640]{1,0:T(8,128)} %convert_element_type.309.rim_ref, ...), custom_call_target="tpu_custom_call" | custom-call | tf_op jit(solution)/shard_map/pallas_call | solution.py:402
  152.7 8.5 %all-to-all-done = f32[8,2,640]{2,1,0:T(2,128)S(1)} async-done(((f32[8,2,640]{2,1,0:T(2,128)}), f32[8,2,640]{2,1,0:T(2,128)S(1)}, u32[]{:S(2)}, u32[]{:S(2)}) %all-to-all-start) | async-done | bytes 40992 | tf_op jit(solution)/shard_map/all_to_all | solution.py:179
  163.8 10.9 %collective-permute-done.26.refs_8_ = bf16[320,256]{1,0:T(8,128)(2,1)S(1)} collective-permute-done((bf16[320,256]{1,0:T(8,128)(2,1)S(1)}, bf16[320,256]{1,0:T(8,128)(2,1)S(1)}, u32[]{:S(2)}, u32[]{:S(2)}) %collective-permute-start.26) | collective-permute-done | bytes 163872 | tf_op jit(solution)/shard_map/ppermute | solution.py:58
  175.9 10.2 %shard_map.286 = (bf16[1024,640]{1,0:T(8,128)(2,1)}, bf16[256,2048]{1,0:T(8,128)(2,1)S(1)}, bf16[256,2048]{1,0:T(8,128)(2,1)S(1)}, bf16[256,2048]{1,0:T(8,128)(2,1)S(1)}, bf16[256,2048]{1,0:T(8,128)(2,1)}) custom-call(s32[26]{0:T(128)S(1)} %copy-done.36, bf16[640,256]{1,0:T(8,128)(2,1)S(1)} %bitcast.380, ...), custom_call_target="tpu_custom_call" | custom-call | tf_op jit(solution)/shard_map/pallas_call | solution.py:748
  195.5 9.7 %shard_map.287 = (bf16[1024,2048]{1,0:T(8,128)(2,1)}, bf16[1024,2048]{1,0:T(8,128)(2,1)}) custom-call(s32[26]{0:T(128)} %concatenate.73.where.scalar_ref, f32[1024,2048]{1,0:T(8,128)} %cot_ref.1), custom_call_target="tpu_custom_call" | custom-call | tf_op jit(solution)/shard_map/pallas_call | solution.py:643
  205.2 23.8 %collective-permute-done.31.refs_6_ = bf16[1536,256]{1,0:T(8,128)(2,1)S(1)} collective-permute-done((bf16[1536,256]{1,0:T(8,128)(2,1)S(1)}, bf16[1536,256]{1,0:T(8,128)(2,1)S(1)}, u32[]{:S(2)}, u32[]{:S(2)}) %collective-permute-start.31) | collective-permute-done | bytes 786464 | tf_op jit(solution)/shard_map/ppermute | solution.py:58
  229.0 22.4 %collective-permute-done.22.refs_1_ = bf16[1536,256]{1,0:T(8,128)(2,1)S(1)} collective-permute-done((bf16[1536,256]{1,0:T(8,128)(2,1)S(1)}, bf16[1536,256]{1,0:T(8,128)(2,1)S(1)}, u32[]{:S(2)}, u32[]{:S(2)}) %collective-permute-start.22) | collective-permute-done | bytes 786464 | tf_op jit(solution)/shard_map/ppermute | solution.py:58
  262.1 21.7 %collective-permute-done.36 = bf16[256,2048]{1,0:T(8,128)(2,1)S(1)} collective-permute-done((bf16[256,2048]{1,0:T(8,128)(2,1)}, bf16[256,2048]{1,0:T(8,128)(2,1)S(1)}, u32[]{:S(2)}, u32[]{:S(2)}) %collective-permute-start.36) | collective-permute-done | bytes 1048608 | tf_op jit(solution)/shard_map/ppermute | solution.py:168
  283.8 9.6 %collective-permute-done.33.refs_5_ = bf16[1536,256]{1,0:T(8,128)(2,1)S(1)} collective-permute-done((bf16[1536,256]{1,0:T(8,128)(2,1)S(1)}, bf16[1536,256]{1,0:T(8,128)(2,1)S(1)}, u32[]{:S(2)}, u32[]{:S(2)}) %collective-permute-start.33) | collective-permute-done | bytes 786464 | tf_op jit(solution)/shard_map/ppermute | solution.py:58
  295.9 17.5 %collective-permute-done.32.refs_3_ = bf16[1536,256]{1,0:T(8,128)(2,1)S(1)} collective-permute-done((bf16[1536,256]{1,0:T(8,128)(2,1)S(1)}, bf16[1536,256]{1,0:T(8,128)(2,1)S(1)}, u32[]{:S(2)}, u32[]{:S(2)}) %collective-permute-start.32) | collective-permute-done | bytes 786464 | tf_op jit(solution)/shard_map/ppermute | solution.py:58
  320.4 21.8 %shard_map.289 = (bf16[1024,1536]{1,0:T(8,128)(2,1)S(1)}, bf16[1024,1536]{1,0:T(8,128)(2,1)}, bf16[1024,1536]{1,0:T(8,128)(2,1)}) custom-call(s32[26]{0:T(128)S(1)} %copy-done.37, bf16[2,2048,1536]{2,1,0:T(8,128)(2,1)} %all-gather.2.cloned.1.call-done.refs_0_, bf16[1024,2048]{1,0:T(8,128)(2,1)} %pad_maximum_fusion.refs_1_), custom_call_target="tpu_custom_call" | custom-call | tf_op jit(solution)/shard_map/pallas_call | solution.py:748
  343.9 14.8 %shard_map.290.refs_1_ = bf16[1024,3072]{1,0:T(8,128)(2,1)} custom-call(s32[26]{0:T(128)S(1)} %copy-done.37, bf16[1536,256]{1,0:T(8,128)(2,1)S(1)} %copy-done.4, bf16[1536,256]{1,0:T(8,128)(2,1)S(1)} %copy-done.6, bf16[1536,256]{1,0:T(8,128)(2,1)S(1)} %copy-done.11, bf16[1536,256]{1,0:T(8,128)(2,1)S(1)} %collective-permute-done.32.refs_3_, ...), custom_call_target="tpu_custom_call" | custom-call | tf_op jit(solution)/shard_map/pallas_call | solution.py:748
  358.7 14.9 %shard_map.291 = (bf16[256,2048]{1,0:T(8,128)(2,1)S(1)}, bf16[256,2048]{1,0:T(8,128)(2,1)S(1)}) custom-call(s32[26]{0:T(128)S(1)} %copy-done.37, bf16[2,2048,1536]{2,1,0:T(8,128)(2,1)} %all-gather.2.cloned.1.call-done.refs_0_, bf16[1024,3072]{1,0:T(8,128)(2,1)} %shard_map.290.refs_1_), custom_call_target="tpu_custom_call" | custom-call | tf_op jit(solution)/shard_map/pallas_call | solution.py:748
  381.5 13.9 %shard_map.292 = (bf16[256,2048]{1,0:T(8,128)(2,1)S(1)}, bf16[256,2048]{1,0:T(8,128)(2,1)S(1)}) custom-call(s32[26]{0:T(128)S(1)} %copy-done.37, bf16[2,2048,1536]{2,1,0:T(8,128)(2,1)} %all-gather.2.cloned.1.call-done.refs_0_, bf16[1024,3072]{1,0:T(8,128)(2,1)} %shard_map.290.refs_1_), custom_call_target="tpu_custom_call" | custom-call | tf_op jit(solution)/shard_map/pallas_call | solution.py:748
  409.6 6.4 shard_map.293
  419.9 16.0 %shard_map.294 = bf16[1024,2048]{1,0:T(8,128)(2,1)} custom-call(s32[26]{0:T(128)S(1)} %copy-done.38, bf16[1536,256]{1,0:T(8,128)(2,1)S(1)} %copy-done.4, bf16[1536,256]{1,0:T(8,128)(2,1)S(1)} %copy-done.6, bf16[1536,256]{1,0:T(8,128)(2,1)S(1)} %copy-done.12, bf16[1536,256]{1,0:T(8,128)(2,1)S(1)} %collective-permute-done.32.refs_3_, ...), custom_call_target="tpu_custom_call" | custom-call | tf_op jit(solution)/shard_map/pallas_call | solution.py:748
  439.2 6.5 fusion.1
  456.7 19.1 %shard_map.295 = (f32[1024,640]{1,0:T(8,128)}, f32[1024,640]{1,0:T(8,128)}, bf16[1024,640]{1,0:T(8,128)(2,1)S(1)}, f32[8,640]{1,0:T(8,128)S(1)}) custom-call(s32[26]{0:T(128)S(1)} %copy-done.38, bf16[640,256]{1,0:T(8,128)(2,1)S(1)} %bitcast.381, bf16[640,256]{1,0:T(8,128)(2,1)S(1)} %copy-done.22, bf16[640,256]{1,0:T(8,128)(2,1)S(1)} %copy-done.26, ...), custom_call_target="tpu_custom_call" | custom-call | tf_op jit(solution)/shard_map/pallas_call | solution.py:748
  478.4 8.8 %convolution_convert_fusion = bf16[1536,2048]{1,0:T(8,128)(2,1)} fusion(bf16[1024,1536]{1,0:T(8,128)(2,1)S(1)} %copy-done.14, bf16[1024,2048]{1,0:T(8,128)(2,1)S(1)} %copy-done.85), kind=kOutput, calls=%fused_computation | convolution fusion | flops 6445596672 | bytes 13631488 | tf_op jit(solution)/shard_map/dot_general | solution.py:1113
  516.7 23.9 %shard_map.297 = (bf16[1024,640]{1,0:T(8,128)(2,1)}, f32[640,1280]{1,0:T(8,128)}, f32[16,640]{1,0:T(8,128)}, f32[16,640]{1,0:T(8,128)}) custom-call(f32[1024,640]{1,0:T(8,128)} %get-tuple-element.244.adj_ref, f32[1024,640]{1,0:T(8,128)} %get-tuple-element.245.tail_ref, f32[1,640]{1,0:T(1,128)} %broadcast_select_fusion.7.arrive_ref, ...), custom_call_target="tpu_custom_call" | custom-call | tf_op jit(solution)/shard_map/pallas_call | solution.py:433
  549.5 6.6 fusion.2
  575.3 15.3 %shard_map.298 = bf16[1024,2048]{1,0:T(8,128)(2,1)} custom-call(s32[26]{0:T(128)} %concatenate.73.where.scalar_ref, bf16[320,640]{1,0:T(8,128)(2,1)} %copy-done.49, bf16[320,640]{1,0:T(8,128)(2,1)} %copy-done.53, bf16[320,640]{1,0:T(8,128)(2,1)} %copy-done.55, bf16[320,640]{1,0:T(8,128)(2,1)} %copy-done.51, bf16[320,640]{1,0:T(8,128)(2,1)} %copy-done.50, ...), custom_call_target="tpu_custom_call" | custom-call | tf_op jit(solution)/shard_map/pallas_call | solution.py:748
  592.7 28.4 %collective-permute-done.59 = bf16[128,1280]{1,0:T(8,128)(2,1)S(1)} collective-permute-done((bf16[128,1280]{1,0:T(8,128)(2,1)}, bf16[128,1280]{1,0:T(8,128)(2,1)S(1)}, u32[]{:S(2)}, u32[]{:S(2)}) %collective-permute-start.59) | collective-permute-done | bytes 327712 | tf_op jit(solution)/shard_map/ppermute | solution.py:58
  647.8 21.4 %collective-permute-done.64 = bf16[256,1280]{1,0:T(8,128)(2,1)S(1)} collective-permute-done((bf16[256,1280]{1,0:T(8,128)(2,1)S(1)}, bf16[256,1280]{1,0:T(8,128)(2,1)S(1)}, u32[]{:S(2)}, u32[]{:S(2)}) %collective-permute-start.64) | collective-permute-done | bytes 655392 | tf_op jit(solution)/shard_map/ppermute | solution.py:58
  736.0 6.5 collective-permute-done.76
  746.5 13.2 %shard_map.299 = f32[1024,2048]{1,0:T(8,128)} custom-call(s32[26]{0:T(128)} %concatenate.73.where.scalar_ref, f32[1024,2048]{1,0:T(8,128)} %x_ref.6, bf16[512,2048]{1,0:T(8,128)(2,1)} %add_convert_fusion.mine_ref, bf16[512,2048]{1,0:T(8,128)(2,1)} %collective-permute-done.65.other_ref, f32[1,2048]{1,0:T(1,128)} %get-tuple-element.274.gain_ref, ...), custom_call_target="tpu_custom_call" | custom-call | tf_op jit(solution)/shard_map/pallas_call | solution.py:691
  (543 shorter events, 317.6 us)
Async XLA Ops:
  7.2 313.2 %all-gather.2.cloned.1.call-start = ((), (), s32[]{:S(2)}) async-start(), calls=%async_computation.3 | async-start | bytes 14155776 | tf_op jit(solution)/shard_map/all_gather | solution.py:962
  76.7 45.7 %collective-permute-start.18 = (bf16[640,256]{1,0:T(8,128)(2,1)S(1)}, bf16[640,256]{1,0:T(8,128)(2,1)S(1)}, u32[]{:S(2)}, u32[]{:S(2)}) collective-permute-start(bf16[640,256]{1,0:T(8,128)(2,1)S(1)} %bitcast.378), channel_id=1, source_target_pairs={{4,0},{8,4},{12,8},{14,12},{10,14},{6,10},{2,6},{0,2},{5,1},{9,5},... | collective-permute-start | bytes 983048 | tf_op jit(solution)/shard_map/ppermute | solution.py:58
  77.4 47.0 %collective-permute-start.17 = (bf16[640,256]{1,0:T(8,128)(2,1)S(1)}, bf16[640,256]{1,0:T(8,128)(2,1)S(1)}, u32[]{:S(2)}, u32[]{:S(2)}) collective-permute-start(bf16[640,256]{1,0:T(8,128)(2,1)S(1)} %bitcast.379), channel_id=1, source_target_pairs={{0,4},{4,8},{8,12},{12,14},{14,10},{10,6},{6,2},{2,0},{1,5},{5,9},... | collective-permute-start | bytes 983048 | tf_op jit(solution)/shard_map/ppermute | solution.py:58
  187.1 64.2 %collective-permute-start.29 = (bf16[256,2048]{1,0:T(8,128)(2,1)S(1)}, bf16[256,2048]{1,0:T(8,128)(2,1)S(1)}, u32[]{:S(2)}, u32[]{:S(2)}) collective-permute-start(bf16[256,2048]{1,0:T(8,128)(2,1)S(1)} %get-tuple-element.197.refs_11_), channel_id=1, source_target_pairs={{0,1},{1,0},{2,3},{3,2},{4,5},{5,4},{6,7},{7,6},{8,9},{9,8},{10,11... | collective-permute-start | bytes 3145736 | tf_op jit(solution)/shard_map/ppermute | solution.py:138
  191.2 60.2 %collective-permute-start.30 = (bf16[256,2048]{1,0:T(8,128)(2,1)S(1)}, bf16[256,2048]{1,0:T(8,128)(2,1)S(1)}, u32[]{:S(2)}, u32[]{:S(2)}) collective-permute-start(bf16[256,2048]{1,0:T(8,128)(2,1)S(1)} %add_convert_fusion.4), channel_id=1, source_target_pairs={{0,16},{16,0},{1,17},{17,1},{2,18},{18,2},{3,19},{19,3},{4,20},{20... | collective-permute-start | bytes 3145736 | tf_op jit(solution)/shard_map/ppermute | solution.py:134
  191.9 37.1 %collective-permute-start.31 = (bf16[1536,256]{1,0:T(8,128)(2,1)S(1)}, bf16[1536,256]{1,0:T(8,128)(2,1)S(1)}, u32[]{:S(2)}, u32[]{:S(2)}) collective-permute-start(bf16[1536,256]{1,0:T(8,128)(2,1)S(1)} %copy-done.4), channel_id=1, source_target_pairs={{0,4},{4,8},{8,12},{12,14},{14,10},{10,6},{6,2},{2,0},{1,5},{5,9},... | collective-permute-start | bytes 2359304 | tf_op jit(solution)/shard_map/ppermute | solution.py:58
  193.3 58.1 %collective-permute-start.22 = (bf16[1536,256]{1,0:T(8,128)(2,1)S(1)}, bf16[1536,256]{1,0:T(8,128)(2,1)S(1)}, u32[]{:S(2)}, u32[]{:S(2)}) collective-permute-start(bf16[1536,256]{1,0:T(8,128)(2,1)S(1)} %copy-done.4), channel_id=1, source_target_pairs={{4,0},{8,4},{12,8},{14,12},{10,14},{6,10},{2,6},{0,2},{5,1},{9,5},... | collective-permute-start | bytes 2359304 | tf_op jit(solution)/shard_map/ppermute | solution.py:58
  258.1 25.7 %collective-permute-start.36 = (bf16[256,2048]{1,0:T(8,128)(2,1)}, bf16[256,2048]{1,0:T(8,128)(2,1)S(1)}, u32[]{:S(2)}, u32[]{:S(2)}) collective-permute-start(bf16[256,2048]{1,0:T(8,128)(2,1)} %get-tuple-element.203), channel_id=1, source_target_pairs={{0,16},{16,0},{1,17},{17,1},{2,18},{18,2},{3,19},{19,3},{4,20},{20... | collective-permute-start | bytes 3145736 | tf_op jit(solution)/shard_map/ppermute | solution.py:168
  260.1 33.3 %collective-permute-start.33 = (bf16[1536,256]{1,0:T(8,128)(2,1)S(1)}, bf16[1536,256]{1,0:T(8,128)(2,1)S(1)}, u32[]{:S(2)}, u32[]{:S(2)}) collective-permute-start(bf16[1536,256]{1,0:T(8,128)(2,1)S(1)} %collective-permute-done.31.refs_6_), channel_id=1, source_target_pairs={{0,4},{4,8},{8,12},{12,14},{14,10},{10,6},{6,2},{2,0},{1,5},{5,9},... | collective-permute-start | bytes 2359304 | tf_op jit(solution)/shard_map/ppermute | solution.py:58
  260.4 32.9 %collective-permute-start.28 = (bf16[1536,256]{1,0:T(8,128)(2,1)S(1)}, bf16[1536,256]{1,0:T(8,128)(2,1)S(1)}, u32[]{:S(2)}, u32[]{:S(2)}) collective-permute-start(bf16[1536,256]{1,0:T(8,128)(2,1)S(1)} %collective-permute-done.22.refs_1_), channel_id=1, source_target_pairs={{4,0},{8,4},{12,8},{14,12},{10,14},{6,10},{2,6},{0,2},{5,1},{9,5},... | collective-permute-start | bytes 2359304 | tf_op jit(solution)/shard_map/ppermute | solution.py:58
  262.1 52.9 %collective-permute-start.35 = (bf16[256,2048]{1,0:T(8,128)(2,1)}, bf16[256,2048]{1,0:T(8,128)(2,1)S(1)}, u32[]{:S(2)}, u32[]{:S(2)}) collective-permute-start(bf16[256,2048]{1,0:T(8,128)(2,1)} %get-tuple-element.203), channel_id=1, source_target_pairs={{0,1},{1,0},{2,3},{3,2},{4,5},{5,4},{6,7},{7,6},{8,9},{9,8},{10,11... | collective-permute-start | bytes 3145736 | tf_op jit(solution)/shard_map/ppermute | solution.py:169
  283.8 31.2 %collective-permute-start.37 = (bf16[256,2048]{1,0:T(8,128)(2,1)S(1)}, bf16[256,2048]{1,0:T(8,128)(2,1)S(1)}, u32[]{:S(2)}, u32[]{:S(2)}) collective-permute-start(bf16[256,2048]{1,0:T(8,128)(2,1)S(1)} %collective-permute-done.36), channel_id=1, source_target_pairs={{0,1},{1,0},{2,3},{3,2},{4,5},{5,4},{6,7},{7,6},{8,9},{9,8},{10,11... | collective-permute-start | bytes 3145736 | tf_op jit(solution)/shard_map/ppermute | solution.py:170
  380.4 28.3 %collective-permute-start.42 = (bf16[256,2048]{1,0:T(8,128)(2,1)}, bf16[256,2048]{1,0:T(8,128)(2,1)}, u32[]{:S(2)}, u32[]{:S(2)}) collective-permute-start(bf16[256,2048]{1,0:T(8,128)(2,1)} %add_convert_fusion.3), channel_id=1, source_target_pairs={{0,16},{16,0},{1,17},{17,1},{2,18},{18,2},{3,19},{19,3},{4,20},{20... | collective-permute-start | bytes 3145736 | tf_op jit(solution)/shard_map/ppermute | solution.py:134
  401.8 37.3 %collective-permute-start.51 = (bf16[256,3072]{1,0:T(8,128)(2,1)}, bf16[256,3072]{1,0:T(8,128)(2,1)}, u32[]{:S(2)}, u32[]{:S(2)}) collective-permute-start(bf16[256,3072]{1,0:T(8,128)(2,1)} %pad_maximum_fusion.4), channel_id=1, source_target_pairs={{4,0},{8,4},{12,8},{14,12},{10,14},{6,10},{2,6},{0,2},{5,1},{9,5},... | collective-permute-start | bytes 4718600 | tf_op jit(solution)/shard_map/ppermute | solution.py:58
  407.9 39.3 %collective-permute-start.48 = (bf16[256,3072]{1,0:T(8,128)(2,1)}, bf16[256,3072]{1,0:T(8,128)(2,1)}, u32[]{:S(2)}, u32[]{:S(2)}) collective-permute-start(bf16[256,3072]{1,0:T(8,128)(2,1)} %pad_maximum_fusion.3), channel_id=1, source_target_pairs={{0,4},{4,8},{8,12},{12,14},{14,10},{10,6},{6,2},{2,0},{1,5},{5,9},... | collective-permute-start | bytes 4718600 | tf_op jit(solution)/shard_map/ppermute | solution.py:58
  416.1 31.1 %collective-permute-start.44 = (bf16[256,2048]{1,0:T(8,128)(2,1)}, bf16[256,2048]{1,0:T(8,128)(2,1)}, u32[]{:S(2)}, u32[]{:S(2)}) collective-permute-start(bf16[256,2048]{1,0:T(8,128)(2,1)} %get-tuple-element.222), channel_id=1, source_target_pairs={{0,16},{16,0},{1,17},{17,1},{2,18},{18,2},{3,19},{19,3},{4,20},{20... | collective-permute-start | bytes 3145736 | tf_op jit(solution)/shard_map/ppermute | solution.py:168
  417.6 35.0 %collective-permute-start.43 = (bf16[256,2048]{1,0:T(8,128)(2,1)}, bf16[256,2048]{1,0:T(8,128)(2,1)S(1)}, u32[]{:S(2)}, u32[]{:S(2)}) collective-permute-start(bf16[256,2048]{1,0:T(8,128)(2,1)} %get-tuple-element.222), channel_id=1, source_target_pairs={{0,1},{1,0},{2,3},{3,2},{4,5},{5,4},{6,7},{7,6},{8,9},{9,8},{10,11... | collective-permute-start | bytes 3145736 | tf_op jit(solution)/shard_map/ppermute | solution.py:169
  445.7 48.2 %collective-permute-start.52 = (bf16[256,3072]{1,0:T(8,128)(2,1)}, bf16[256,3072]{1,0:T(8,128)(2,1)S(1)}, u32[]{:S(2)}, u32[]{:S(2)}) collective-permute-start(bf16[256,3072]{1,0:T(8,128)(2,1)} %fusion.1), channel_id=1, source_target_pairs={{4,0},{8,4},{12,8},{14,12},{10,14},{6,10},{2,6},{0,2},{5,1},{9,5},... | collective-permute-start | bytes 4718600 | tf_op jit(solution)/shard_map/ppermute | solution.py:58
  452.0 41.8 %collective-permute-start.49 = (bf16[256,3072]{1,0:T(8,128)(2,1)}, bf16[256,3072]{1,0:T(8,128)(2,1)}, u32[]{:S(2)}, u32[]{:S(2)}) collective-permute-start(bf16[256,3072]{1,0:T(8,128)(2,1)} %fusion), channel_id=1, source_target_pairs={{0,4},{4,8},{8,12},{12,14},{14,10},{10,6},{6,2},{2,0},{1,5},{5,9},... | collective-permute-start | bytes 4718600 | tf_op jit(solution)/shard_map/ppermute | solution.py:58
  498.8 218.1 %reduce-scatter.2.cloned.1.call-start = ((), (), s32[]{:S(2)}) async-start(), calls=%async_computation.4 | async-start | bytes 7077888 | tf_op jit(solution)/shard_map/reduce_scatter | solution.py:1179
  513.6 44.7 %collective-permute-start.53 = (bf16[1024,512]{1,0:T(8,128)(2,1)}, bf16[1024,512]{1,0:T(8,128)(2,1)}, u32[]{:S(2)}, u32[]{:S(2)}) collective-permute-start(bf16[1024,512]{1,0:T(8,128)(2,1)} %add_convert_fusion.2), channel_id=1, source_target_pairs={{0,16},{16,0},{1,17},{17,1},{2,18},{18,2},{3,19},{19,3},{4,20},{20... | collective-permute-start | bytes 3145736 | tf_op jit(solution)/shard_map/ppermute | solution.py:1180
  548.2 79.1 %collective-permute-start.63 = (bf16[256,3072]{1,0:T(8,128)(2,1)}, bf16[256,3072]{1,0:T(8,128)(2,1)}, u32[]{:S(2)}, u32[]{:S(2)}) collective-permute-start(bf16[256,3072]{1,0:T(8,128)(2,1)} %fusion.3), channel_id=1, source_target_pairs={{4,0},{8,4},{12,8},{14,12},{10,14},{6,10},{2,6},{0,2},{5,1},{9,5},... | collective-permute-start | bytes 4718600 | tf_op jit(solution)/shard_map/ppermute | solution.py:58
  556.1 71.2 %collective-permute-start.61 = (bf16[256,3072]{1,0:T(8,128)(2,1)}, bf16[256,3072]{1,0:T(8,128)(2,1)}, u32[]{:S(2)}, u32[]{:S(2)}) collective-permute-start(bf16[256,3072]{1,0:T(8,128)(2,1)} %fusion.2), channel_id=1, source_target_pairs={{0,4},{4,8},{8,12},{12,14},{14,10},{10,6},{6,2},{2,0},{1,5},{5,9},... | collective-permute-start | bytes 4718600 | tf_op jit(solution)/shard_map/ppermute | solution.py:58
  561.1 79.9 %collective-permute-start.71 = (bf16[640,256]{1,0:T(8,128)(2,1)}, bf16[640,256]{1,0:T(8,128)(2,1)}, u32[]{:S(2)}, u32[]{:S(2)}) collective-permute-start(bf16[640,256]{1,0:T(8,128)(2,1)} %pad_maximum_fusion.9), channel_id=1, source_target_pairs={{4,0},{8,4},{12,8},{14,12},{10,14},{6,10},{2,6},{0,2},{5,1},{9,5},... | collective-permute-start | bytes 983048 | tf_op jit(solution)/shard_map/ppermute | solution.py:58
  566.7 54.4 %collective-permute-start.59 = (bf16[128,1280]{1,0:T(8,128)(2,1)}, bf16[128,1280]{1,0:T(8,128)(2,1)S(1)}, u32[]{:S(2)}, u32[]{:S(2)}) collective-permute-start(bf16[128,1280]{1,0:T(8,128)(2,1)} %get-tuple-element.258), channel_id=1, source_target_pairs={{4,0},{8,4},{12,8},{14,12},{10,14},{6,10},{2,6},{0,2},{5,1},{9,5},... | collective-permute-start | bytes 983048 | tf_op jit(solution)/shard_map/ppermute | solution.py:58
  567.4 53.7 %collective-permute-start.58 = (bf16[128,1280]{1,0:T(8,128)(2,1)S(1)}, bf16[128,1280]{1,0:T(8,128)(2,1)S(1)}, u32[]{:S(2)}, u32[]{:S(2)}) collective-permute-start(bf16[128,1280]{1,0:T(8,128)(2,1)S(1)} %get-tuple-element.257), channel_id=1, source_target_pairs={{0,4},{4,8},{8,12},{12,14},{14,10},{10,6},{6,2},{2,0},{1,5},{5,9},... | collective-permute-start | bytes 983048 | tf_op jit(solution)/shard_map/ppermute | solution.py:58
  627.3 41.9 %collective-permute-start.64 = (bf16[256,1280]{1,0:T(8,128)(2,1)S(1)}, bf16[256,1280]{1,0:T(8,128)(2,1)S(1)}, u32[]{:S(2)}, u32[]{:S(2)}) collective-permute-start(bf16[256,1280]{1,0:T(8,128)(2,1)S(1)} %pad_maximum_fusion.6), channel_id=1, source_target_pairs={{4,0},{8,4},{12,8},{14,12},{10,14},{6,10},{2,6},{0,2},{5,1},{9,5},... | collective-permute-start | bytes 1966088 | tf_op jit(solution)/shard_map/ppermute | solution.py:58
  627.9 44.0 %collective-permute-start.62 = (bf16[256,1280]{1,0:T(8,128)(2,1)S(1)}, bf16[256,1280]{1,0:T(8,128)(2,1)S(1)}, u32[]{:S(2)}, u32[]{:S(2)}) collective-permute-start(bf16[256,1280]{1,0:T(8,128)(2,1)S(1)} %pad_maximum_fusion.5), channel_id=1, source_target_pairs={{0,4},{4,8},{8,12},{12,14},{14,10},{10,6},{6,2},{2,0},{1,5},{5,9},... | collective-permute-start | bytes 1966088 | tf_op jit(solution)/shard_map/ppermute | solution.py:58
  639.5 79.7 %collective-permute-start.60 = (bf16[512,2048]{1,0:T(8,128)(2,1)}, bf16[512,2048]{1,0:T(8,128)(2,1)}, u32[]{:S(2)}, u32[]{:S(2)}) collective-permute-start(bf16[512,2048]{1,0:T(8,128)(2,1)} %add_convert_fusion.1), channel_id=1, source_target_pairs={{0,16},{16,0},{1,17},{17,1},{2,18},{18,2},{3,19},{19,3},{4,20},{20... | collective-permute-start | bytes 6291464 | tf_op jit(solution)/shard_map/ppermute | solution.py:156
  643.5 39.2 %collective-permute-start.72 = (bf16[640,256]{1,0:T(8,128)(2,1)}, bf16[640,256]{1,0:T(8,128)(2,1)}, u32[]{:S(2)}, u32[]{:S(2)}) collective-permute-start(bf16[640,256]{1,0:T(8,128)(2,1)} %fusion.20), channel_id=1, source_target_pairs={{4,0},{8,4},{12,8},{14,12},{10,14},{6,10},{2,6},{0,2},{5,1},{9,5},... | collective-permute-start | bytes 983048 | tf_op jit(solution)/shard_map/ppermute | solution.py:58
  646.4 38.9 %collective-permute-start.69 = (bf16[640,256]{1,0:T(8,128)(2,1)}, bf16[640,256]{1,0:T(8,128)(2,1)}, u32[]{:S(2)}, u32[]{:S(2)}) collective-permute-start(bf16[640,256]{1,0:T(8,128)(2,1)} %fusion.19), channel_id=1, source_target_pairs={{0,4},{4,8},{8,12},{12,14},{14,10},{10,6},{6,2},{2,0},{1,5},{5,9},... | collective-permute-start | bytes 983048 | tf_op jit(solution)/shard_map/ppermute | solution.py:58
  698.4 30.9 %collective-permute-start.73 = (bf16[256,1280]{1,0:T(8,128)(2,1)}, bf16[256,1280]{1,0:T(8,128)(2,1)}, u32[]{:S(2)}, u32[]{:S(2)}) collective-permute-start(bf16[256,1280]{1,0:T(8,128)(2,1)} %fusion.7), channel_id=1, source_target_pairs={{4,0},{8,4},{12,8},{14,12},{10,14},{6,10},{2,6},{0,2},{5,1},{9,5},... | collective-permute-start | bytes 1966088 | tf_op jit(solution)/shard_map/ppermute | solution.py:58
  (161 other events, 2710.3 us)
Sparse Core Ops, SparseCore 0:
  75.1 217.8 all-gather.1
  515.1 163.1 reduce-scatter.1
